TPU v7x, 256 devices: a whole 4x4x8 slice. The times are simulated.
256 devices in a mesh: ctx: 32 (over x, y, z_hi), tp: 8 (over z_lo, core).
Axes of the slice: x: 4, y: 4, z: 8 (z_hi: 2, z_lo: 4; z = z_hi * 4 + z_lo), core: 2. Of those that a mesh axis runs over, the one named last changes fastest.
Arguments:
- medium_input: bfloat16 [8192, 3, 4096], P('ctx', None, 'tp'), may hold values from -6 to 6
- long_input: bfloat16 [8192, 2, 4096], P('ctx', None, 'tp'), may hold values from -6 to 6
- medium_taps: float32 [3, 3, 4096], P(None, None, 'tp'), may hold values from -3.5 to 3.5
- long_taps: float32 [3, 2, 4096], P(None, None, 'tp'), may hold values from -3.5 to 3.5
- medium_filter: bfloat16 [128, 4096], P(None, 'tp'), may hold values from -0.75 to 0.75
- norm_gain: float32 [4096], P('tp'), may hold values from 0.1 to 1.9
- long_residue: float32 [4096, 16], P(('tp', 'ctx')), may hold values from -1.5 to 1.5
- long_log_decay: float32 [4096, 16], P(('tp', 'ctx')), as said below
- cotangent: bfloat16 [8192, 4096], P('ctx', 'tp'), may hold values from -6 to 6
Outputs:
- mixed: bfloat16 [8192, 4096], P('ctx', 'tp')
- grad_medium_input: bfloat16 [8192, 3, 4096], P('ctx', None, 'tp')
- grad_long_input: bfloat16 [8192, 2, 4096], P('ctx', None, 'tp')
- grad_medium_taps: float32 [3, 3, 4096], P(None, None, 'tp')
- grad_long_taps: float32 [3, 2, 4096], P(None, None, 'tp')
- grad_medium_filter: float32 [128, 4096], P(None, 'tp')
- grad_norm_gain: float32 [4096], P('tp')
- grad_long_residue: float32 [4096, 16], P(('tp', 'ctx'))
- grad_long_log_decay: float32 [4096, 16], P(('tp', 'ctx'))
Inputs may be any that keep to these rules, and one draw needn't show every extreme that they name: `long_log_decay`: natural logarithm of each mode's decay per base.
All inputs are finite; a program needn't handle non-finite values.
Results may differ from a plain program's by a relative error of at most 0.03.
Values may be sent and summed in bfloat16 or wider, within the bound.
No kernel may reach another device: no remote copies, remote signals or barrier semaphores. Data moves between devices by JAX's collectives and lax.ppermute only.
A program may use at most 128 MiB of HBM per device.

v0:
```python
import math

import jax
import jax.numpy as jnp
from jax import lax
from jax.sharding import PartitionSpec as P

D = 4096


precise = lax.Precision.HIGHEST


def passed_along(array, axis, by):
    count = lax.axis_size(axis)
    pairs = [(i, i + by) for i in range(count) if 0 <= i + by < count]
    return lax.ppermute(array, axis, pairs)


def rounded(values):
    return lax.optimization_barrier(values.astype(jnp.bfloat16)).astype(jnp.float32)


def angles(offset, count_rows, count_cols, period):
    product = (jnp.arange(count_rows, dtype=jnp.int32)[:, None] + offset) * jnp.arange(
        count_cols, dtype=jnp.int32
    )[None, :]
    phase_angle = (product % period).astype(jnp.float32) * (2.0 * math.pi / period)
    return (jnp.cos(phase_angle), jnp.sin(phase_angle))


def featurize(extended, taps):
    values = extended.astype(jnp.float32)
    return taps[0] * values[2:] + taps[1] * values[1:-1] + taps[2] * values[:-2]


def unfeaturize(grad_local, grad_after, extended, taps):
    joined = jnp.concatenate([grad_local, grad_after], 0)
    grad_raw = taps[0] * joined[:-2] + taps[1] * joined[1:-1] + taps[2] * joined[2:]
    values = extended.astype(jnp.float32)
    grad_taps = jnp.stack(
        [
            jnp.sum(grad_local * values[2:], 0),
            jnp.sum(grad_local * values[1:-1], 0),
            jnp.sum(grad_local * values[:-2], 0),
        ]
    )
    return (grad_raw, grad_taps)


def half_spectra(pieces, cos_table, sin_table):
    real_part = jnp.einsum("fp,bpc->bfc", cos_table, pieces, precision=precise)
    imag_part = -jnp.einsum("fp,bpc->bfc", sin_table, pieces, precision=precise)
    return (real_part, imag_part)


def block_rows(real_part, imag_part, cos_table, sin_table):
    return jnp.einsum("mf,bfc->bmc", cos_table, real_part, precision=precise) - jnp.einsum(
        "mf,bfc->bmc", sin_table, imag_part, precision=precise
    )


def fourier_tables(length):
    total = 2 * length
    outer = total // 128
    inner_half = length // 128
    section_cos, section_sin = angles(0, outer, inner_half, outer)
    twist_cos, twist_sin = angles(0, outer, 128, total)
    last_cos, last_sin = angles(0, 128, 128, 128)
    return (
        section_cos,
        section_sin,
        twist_cos[:, :, None],
        twist_sin[:, :, None],
        last_cos,
        last_sin,
    )


def forward_fourier(signal, tables):
    section_cos, section_sin, twist_cos, twist_sin, last_cos, last_sin = tables
    outer, inner_half = section_cos.shape
    channels = signal.shape[1]
    folded = signal.reshape(inner_half, 128 * channels)
    first_re = jnp.dot(section_cos, folded, precision=precise).reshape(outer, 128, channels)
    first_im = -jnp.dot(section_sin, folded, precision=precise).reshape(outer, 128, channels)
    turned_re = first_re * twist_cos + first_im * twist_sin
    turned_im = first_im * twist_cos - first_re * twist_sin
    spec_re = jnp.einsum("kbc,bj->kjc", turned_re, last_cos, precision=precise) + jnp.einsum(
        "kbc,bj->kjc", turned_im, last_sin, precision=precise
    )
    spec_im = jnp.einsum("kbc,bj->kjc", turned_im, last_cos, precision=precise) - jnp.einsum(
        "kbc,bj->kjc", turned_re, last_sin, precision=precise
    )
    return (spec_re, spec_im)


def inverse_fourier(spec_re, spec_im, tables):
    section_cos, section_sin, twist_cos, twist_sin, last_cos, last_sin = tables
    outer, inner_half = section_cos.shape
    channels = spec_re.shape[2]
    back_re = jnp.einsum("kjc,bj->kbc", spec_re, last_cos, precision=precise) - jnp.einsum(
        "kjc,bj->kbc", spec_im, last_sin, precision=precise
    )
    back_im = jnp.einsum("kjc,bj->kbc", spec_im, last_cos, precision=precise) + jnp.einsum(
        "kjc,bj->kbc", spec_re, last_sin, precision=precise
    )
    turned_re = (back_re * twist_cos - back_im * twist_sin).reshape(outer, 128 * channels)
    turned_im = (back_im * twist_cos + back_re * twist_sin).reshape(outer, 128 * channels)
    signal = jnp.dot(section_cos.T, turned_re, precision=precise) - jnp.dot(
        section_sin.T, turned_im, precision=precise
    )
    return (signal / float(outer * 128)).reshape(inner_half * 128, channels)


def long_kernel(residue, log_decay, length):
    rate = jnp.exp(log_decay)
    weight = residue * jnp.sqrt(2.0 * rate)
    position = jnp.arange(length, dtype=jnp.int32).astype(jnp.float32)[:, None]
    total = jnp.zeros((length, residue.shape[0]), jnp.float32)
    for index_mode in range(residue.shape[1]):
        total = total + weight[:, index_mode] * jnp.exp(-rate[:, index_mode] * position)
    return total


def long_kernel_back(residue, log_decay, grad_kernel):
    rate = jnp.exp(log_decay)
    root_rate = jnp.sqrt(2.0 * rate)
    position = jnp.arange(grad_kernel.shape[0], dtype=jnp.int32).astype(jnp.float32)[:, None]
    residue_list = []
    decay_list = []
    for index_mode in range(residue.shape[1]):
        decay_curve = jnp.exp(-rate[:, index_mode] * position)
        plain_sum = jnp.sum(grad_kernel * decay_curve, 0)
        slope_sum = jnp.sum(grad_kernel * decay_curve * (0.5 - rate[:, index_mode] * position), 0)
        residue_list.append(root_rate[:, index_mode] * plain_sum)
        decay_list.append(residue[:, index_mode] * root_rate[:, index_mode] * slope_sum)
    return (jnp.stack(residue_list, 1), jnp.stack(decay_list, 1))


def channel_forward(prod_chan, residue, log_decay):
    length = prod_chan.shape[0]
    tables = fourier_tables(length)
    kernel = long_kernel(residue, log_decay, length)
    prod_re, prod_im = forward_fourier(prod_chan.astype(jnp.float32), tables)
    kern_re, kern_im = forward_fourier(kernel, tables)
    conv_chan = inverse_fourier(
        prod_re * kern_re - prod_im * kern_im, prod_re * kern_im + prod_im * kern_re, tables
    )
    return (conv_chan.astype(jnp.bfloat16), (tables, prod_re, prod_im, kern_re, kern_im))


def channel_backward(grad_chan, saved, residue, log_decay):
    tables, prod_re, prod_im, kern_re, kern_im = saved
    grad_re, grad_im = forward_fourier(grad_chan.astype(jnp.float32), tables)
    back_chan = inverse_fourier(
        grad_re * kern_re + grad_im * kern_im, grad_im * kern_re - grad_re * kern_im, tables
    )
    grad_kernel = inverse_fourier(
        grad_re * prod_re + grad_im * prod_im, grad_im * prod_re - grad_re * prod_im, tables
    )
    grad_residue, grad_log = long_kernel_back(residue, log_decay, grad_kernel)
    return (back_chan.astype(jnp.bfloat16), grad_residue, grad_log)


def on_device(
    medium_input,
    long_input,
    medium_taps,
    long_taps,
    medium_filter,
    norm_gain,
    long_residue,
    long_log_decay,
    cotangent,
):
    tok_rows, chan_width = cotangent.shape
    filter_len = medium_filter.shape[0]
    block_count = tok_rows // filter_len
    packed = jnp.concatenate(
        [
            medium_input[tok_rows - filter_len - 1 :, 1:].reshape(-1, chan_width),
            medium_input[tok_rows - 2 :, :1].reshape(-1, chan_width),
            long_input[tok_rows - 2 :].reshape(-1, chan_width),
        ],
        0,
    )
    before = passed_along(packed, "ctx", 1)
    kv_rows = 2 * (filter_len + 1)
    prev_kv = before[:kv_rows].reshape(filter_len + 1, 2, chan_width)
    prev_q = before[kv_rows : kv_rows + 2].reshape(2, 1, chan_width)
    prev_long = before[kv_rows + 2 :].reshape(2, 2, chan_width)
    ext_kv = jnp.concatenate([prev_kv, medium_input[:, 1:]], 0)
    ext_medium = jnp.concatenate([jnp.concatenate([prev_q, prev_kv[-2:]], 1), medium_input], 0)
    ext_long = jnp.concatenate([prev_long, long_input], 0)
    feat_kv = rounded(featurize(ext_kv, medium_taps[:, 1:]))
    q_one = rounded(featurize(ext_medium[:, :1], medium_taps[:, :1]))[:, 0]
    feat_long = rounded(featurize(ext_long, long_taps))
    q_two = feat_long[:, 0]
    k_two = feat_long[:, 1]
    key_ext = feat_kv[:, 0]
    val_ext = feat_kv[:, 1]
    key_loc = key_ext[filter_len - 1 :]
    val_loc = val_ext[filter_len - 1 :]
    prod_one = rounded(key_ext * val_ext)
    padded = jnp.concatenate([jnp.zeros((1, chan_width), jnp.float32), prod_one], 0).reshape(
        block_count + 1, filter_len, chan_width
    )
    cos_full, sin_full = angles(0, 2 * filter_len, 2 * filter_len, 2 * filter_len)
    cos_lo, sin_lo = (cos_full[:, :filter_len], sin_full[:, :filter_len])
    cos_hi, sin_hi = (cos_full[:, filter_len:], sin_full[:, filter_len:])
    top_cos, top_sin = angles(filter_len, filter_len, 2 * filter_len, 2 * filter_len)
    low_cos, low_sin = angles(0, filter_len, 2 * filter_len, 2 * filter_len)
    top_cos, top_sin = (top_cos / (2.0 * filter_len), top_sin / (2.0 * filter_len))
    low_cos, low_sin = (low_cos / (2.0 * filter_len), low_sin / (2.0 * filter_len))
    lo_re, lo_im = half_spectra(padded[:-1], cos_lo, sin_lo)
    hi_re, hi_im = half_spectra(padded[1:], cos_hi, sin_hi)
    win_re = lo_re + hi_re
    win_im = lo_im + hi_im
    filter_f = medium_filter.astype(jnp.float32)
    ker_re = jnp.dot(cos_lo, filter_f, precision=precise)
    ker_im = -jnp.dot(sin_lo, filter_f, precision=precise)
    conv_one = block_rows(
        win_re * ker_re - win_im * ker_im, win_re * ker_im + win_im * ker_re, top_cos, top_sin
    ).reshape(tok_rows, chan_width)
    gated = q_one * conv_one
    square_sum = lax.psum(jnp.sum(gated * gated, 1, keepdims=True), "tp")
    scale = lax.rsqrt(square_sum / D + 1e-06)
    normed = rounded(gated * scale * norm_gain)
    prod_two = (k_two * normed).astype(jnp.bfloat16)
    grad_out = cotangent.astype(jnp.float32)
    grad_conv = (grad_out * q_two).astype(jnp.bfloat16)
    prod_chan = lax.all_to_all(prod_two, "ctx", split_axis=1, concat_axis=0, tiled=True)
    conv_chan, saved = channel_forward(prod_chan, long_residue, long_log_decay)
    long_conv = lax.all_to_all(conv_chan, "ctx", split_axis=0, concat_axis=1, tiled=True)
    grad_chan = lax.all_to_all(grad_conv, "ctx", split_axis=1, concat_axis=0, tiled=True)
    back_chan, grad_residue, grad_log = channel_backward(
        grad_chan, saved, long_residue, long_log_decay
    )
    grad_prod_two = lax.all_to_all(back_chan, "ctx", split_axis=0, concat_axis=1, tiled=True)
    conv_f = long_conv.astype(jnp.float32)
    mixed = (q_two * conv_f).astype(jnp.bfloat16)
    grad_q_two = grad_out * conv_f
    grad_prod_f = grad_prod_two.astype(jnp.float32)
    grad_k_two = grad_prod_f * normed
    grad_normed = grad_prod_f * k_two
    gain_local = jnp.sum(grad_normed * gated * scale, 0)
    weighted = grad_normed * norm_gain
    inner_sum = lax.psum(jnp.sum(weighted * gated, 1, keepdims=True), "tp")
    grad_gated = scale * (weighted - gated * scale * scale * (inner_sum / D))
    grad_conv_one = rounded(grad_gated * q_one)
    grad_q_one = grad_gated * conv_one
    head_rows = jnp.stack(
        [
            jnp.sum(filter_f * grad_conv_one[shift_rows : shift_rows + filter_len], 0)
            for shift_rows in range(2)
        ]
    )
    head_medium = jnp.stack([grad_q_one[:2], head_rows * val_loc[:2], head_rows * key_loc[:2]], 1)
    head_long = jnp.stack([grad_q_two[:2], grad_k_two[:2]], 1)
    packed_back = jnp.concatenate(
        [
            grad_conv_one[: filter_len - 1],
            head_medium.reshape(-1, chan_width),
            head_long.reshape(-1, chan_width),
        ],
        0,
    )
    after = passed_along(packed_back.astype(jnp.bfloat16), "ctx", -1).astype(packed_back.dtype)
    next_conv = after[: filter_len - 1]
    next_medium = after[filter_len - 1 : filter_len + 5].reshape(2, 3, chan_width)
    next_long = after[filter_len + 5 :].reshape(2, 2, chan_width)
    grad_pad = jnp.concatenate(
        [grad_conv_one, next_conv, jnp.zeros((1, chan_width), jnp.float32)], 0
    ).reshape(block_count + 1, filter_len, chan_width)
    glo_re, glo_im = half_spectra(grad_pad[:-1], cos_lo, sin_lo)
    ghi_re, ghi_im = half_spectra(grad_pad, cos_hi, sin_hi)
    gwin_re = glo_re + ghi_re[1:]
    gwin_im = glo_im + ghi_im[1:]
    grad_prod_one = block_rows(
        gwin_re * ker_re + gwin_im * ker_im, gwin_im * ker_re - gwin_re * ker_im, low_cos, low_sin
    ).reshape(tok_rows, chan_width)
    dpos_re = ghi_re[:-1]
    dpos_im = ghi_im[:-1]
    cross_re = jnp.sum(dpos_re * win_re + dpos_im * win_im, 0)
    cross_im = jnp.sum(dpos_im * win_re - dpos_re * win_im, 0)
    grad_filter = jnp.dot(low_cos, cross_re, precision=precise) - jnp.dot(
        low_sin, cross_im, precision=precise
    )
    grad_k_one = grad_prod_one * val_loc
    grad_v_one = grad_prod_one * key_loc
    grad_medium, taps_medium = unfeaturize(
        jnp.stack([grad_q_one, grad_k_one, grad_v_one], 1), next_medium, ext_medium, medium_taps
    )
    grad_long, taps_long = unfeaturize(
        jnp.stack([grad_q_two, grad_k_two], 1), next_long, ext_long, long_taps
    )
    taps_medium, taps_long, grad_filter, gain_total = (
        lax.psum(taps_medium.astype(jnp.bfloat16), "ctx").astype(jnp.float32),
        lax.psum(taps_long.astype(jnp.bfloat16), "ctx").astype(jnp.float32),
        lax.psum(grad_filter.astype(jnp.bfloat16), "ctx").astype(jnp.float32),
        lax.psum(gain_local.astype(jnp.bfloat16), "ctx").astype(jnp.float32),
    )
    return (
        mixed,
        grad_medium.astype(jnp.bfloat16),
        grad_long.astype(jnp.bfloat16),
        taps_medium,
        taps_long,
        grad_filter,
        gain_total,
        grad_residue,
        grad_log,
    )


def solution(mesh):
    return jax.shard_map(
        on_device,
        mesh=mesh,
        in_specs=(
            P("ctx", None, "tp"),
            P("ctx", None, "tp"),
            P(None, None, "tp"),
            P(None, None, "tp"),
            P(None, "tp"),
            P("tp"),
            P(("tp", "ctx"), None),
            P(("tp", "ctx"), None),
            P("ctx", "tp"),
        ),
        out_specs=(
            P("ctx", "tp"),
            P("ctx", None, "tp"),
            P("ctx", None, "tp"),
            P(None, None, "tp"),
            P(None, None, "tp"),
            P(None, "tp"),
            P("tp"),
            P(("tp", "ctx"), None),
            P(("tp", "ctx"), None),
        ),
        check_vma=False,
    )
```

profile of v0, /device:TPU:64, one launch (start us, length us, event | category | flops | bytes accessed | tf_op | source)
XLA Modules:
  0.0 714.9 jit_solution(17902630459113587547)
XLA Ops:
  10.7 8.0 %collective-permute-start = (bf16[264,512]{1,0:T(8,128)(2,1)}, bf16[264,512]{1,0:T(8,128)(2,1)}, u32[]{:S(2)}, u32[]{:S(2)}) collective-permute-start(bf16[264,512]{1,0:T(8,128)(2,1)} %pad_maximum_fusion.5), channel_id=1, source_target_pairs={{0,8},{8,16},{16,24},{24,32},{32,40},{40,48},{48,56},{56,64},{64,7... | collective-permute-start | bytes 811016 | tf_op jit(solution)/shard_map/ppermute | solution.py:17
  32.6 2.4 fusion.105
  35.1 2.6 convolution_add_fusion.4
  41.5 2.0 reshape.471
  52.6 2.6 fusion.471
  60.8 2.9 convolution_subtract_fusion.10
  64.7 10.2 %psum.42 = f32[256,1]{0,1:T(1,128)S(1)} all-reduce(f32[256,1]{0,1:T(1,128)S(1)} %bitcast.550), channel_id=1, replica_groups=mesh['ctx'=32,'tp'=8] {'tp'}, use_global_device_ids=true, to_apply=%region_1.2 | all-reduce | flops 256 | bytes 2048 | tf_op jit(solution)/shard_map/psum | solution.py:227
  81.2 7.5 %all-to-all-start = ((bf16[256,32,16]{0,2,1:T(8,128)(2,1)}), bf16[256,32,16]{0,2,1:T(8,128)(2,1)}, u32[]{:S(2)}, u32[]{:S(2)}) async-start(bf16[256,32,16]{0,2,1:T(8,128)(2,1)} %bitcast.531), calls=%async_computation | async-start | bytes 524288 | tf_op jit(solution)/shard_map/all_to_all | solution.py:233
  89.4 3.6 convolution_subtract_fusion.7
  94.8 8.0 %all-to-all-done = bf16[256,32,16]{0,2,1:T(8,128)(2,1)} async-done(((bf16[256,32,16]{0,2,1:T(8,128)(2,1)}), bf16[256,32,16]{0,2,1:T(8,128)(2,1)}, u32[]{:S(2)}, u32[]{:S(2)}) %all-to-all-start) | async-done | bytes 262176 | tf_op jit(solution)/shard_map/all_to_all | solution.py:233
  102.7 4.6 all-to-all-start.2
  109.2 4.2 reshape.473
  118.3 2.3 all-to-all-done.2
  120.7 2.6 copy.469
  123.2 5.7 reshape.476
  129.0 2.0 copy.470
  130.9 2.1 copy.471
  146.3 2.3 multiply_add_fusion.1
  148.6 1.9 fusion.30
  150.5 1.9 fusion.34
  152.5 1.9 fusion.15
  154.4 1.9 fusion.42
  156.4 1.9 fusion.46
  158.3 3.2 fusion.19
  161.5 1.9 fusion.20
  165.4 1.9 fusion.40
  167.3 1.9 fusion.17
  169.2 1.9 fusion.18
  171.2 4.3 multiply_add_fusion
  177.2 2.2 fusion.245
  179.9 2.4 fusion.3
  185.5 10.1 %all-to-all-start.3 = ((bf16[32,256,16]{1,2,0:T(8,128)(2,1)}), bf16[32,256,16]{1,2,0:T(8,128)(2,1)}, u32[]{:S(2)}, u32[]{:S(2)}) async-start(bf16[32,256,16]{1,2,0:T(8,128)(2,1)} %copy.487), calls=%async_computation.3 | async-start | bytes 524288 | tf_op jit(solution)/shard_map/all_to_all | solution.py:240
  197.4 2.2 fusion.247
  201.8 2.2 fusion.249
  205.8 3.2 fusion.2
  208.9 3.7 reshape.488
  212.7 2.8 copy.512
  217.4 2.2 multiply_reduce_fusion.11
  219.7 2.2 multiply_reduce_fusion.3
  226.1 12.6 %all-to-all-start.1 = ((bf16[32,256,16]{1,2,0:T(8,128)(2,1)}), bf16[32,256,16]{1,2,0:T(8,128)(2,1)}, u32[]{:S(2)}, u32[]{:S(2)}) async-start(bf16[32,256,16]{1,2,0:T(8,128)(2,1)} %copy.466), calls=%async_computation.1 | async-start | bytes 524288 | tf_op jit(solution)/shard_map/all_to_all | solution.py:235
  243.5 13.4 %psum.43 = f32[256,1]{0,1:T(1,128)S(1)} all-reduce(f32[256,1]{0,1:T(1,128)S(1)} %bitcast.549), channel_id=1, replica_groups=mesh['ctx'=32,'tp'=8] {'tp'}, use_global_device_ids=true, to_apply=%region_3.4 | all-reduce | flops 256 | bytes 2048 | tf_op jit(solution)/shard_map/psum | solution.py:249
  258.7 2.1 copy.467
  260.8 2.5 fusion.65
  269.3 2.0 copy.488
  271.4 2.1 fusion.71
  273.5 7.0 collective-permute-done.1
  301.4 222.1 %all-reduce.1 = (bf16[3,3,512]{2,1,0:T(4,128)(2,1)S(1)}, bf16[3,2,512]{2,1,0:T(2,128)(2,1)S(1)}, bf16[512]{0:T(512)(128)(2,1)S(1)}) all-reduce(bf16[3,3,512]{2,1,0:T(4,128)(2,1)S(1)} %pad_maximum_fusion.7, bf16[3,2,512]{2,1,0:T(2,128)(2,1)S(1)} %pad_maximum_fusion.9, ...), channel_id=1, replica_groups=mesh['ctx'=32,'tp'=8] {'ctx'}, use_global_device_ids=true, to_apply=%region_9.10 | all-reduce | flops 8192 | bytes 32768 | tf_op jit(solution)/shard_map/psum | solution.py:299
  525.2 180.8 %all-reduce.4.cloned.1.call-done = bf16[128,512]{1,0:T(8,128)(2,1)} async-done(((bf16[128,512]{1,0:T(8,128)(2,1)}), bf16[128,512]{1,0:T(8,128)(2,1)}) %all-reduce.4.cloned.1.call-update) | async-done | bytes 131088 | tf_op jit(solution)/shard_map/psum | solution.py:301
  (468 shorter events, 119.8 us)
Async XLA Ops:
  7.2 11.5 %copy-start.50 = (f32[3,3,512]{2,1,0:T(4,128)S(1)}, f32[3,3,512]{2,1,0:T(4,128)}, u32[]{:S(2)}) copy-start(f32[3,3,512]{2,1,0:T(4,128)} %param.11) | copy-start | bytes 55300
  10.7 30.8 %collective-permute-start = (bf16[264,512]{1,0:T(8,128)(2,1)}, bf16[264,512]{1,0:T(8,128)(2,1)}, u32[]{:S(2)}, u32[]{:S(2)}) collective-permute-start(bf16[264,512]{1,0:T(8,128)(2,1)} %pad_maximum_fusion.5), channel_id=1, source_target_pairs={{0,8},{8,16},{16,24},{24,32},{32,40},{40,48},{48,56},{56,64},{64,7... | collective-permute-start | bytes 811016 | tf_op jit(solution)/shard_map/ppermute | solution.py:17
  23.7 2.9 copy-start.73
  35.1 3.0 copy-start.31
  39.9 20.9 %copy-start.10 = (f32[256,512]{0,1:T(8,128)}, f32[256,512]{0,1:T(8,128)S(1)}, u32[]{:S(2)}) copy-start(f32[256,512]{0,1:T(8,128)S(1)} %copy.419) | copy-start | bytes 1572868
  41.4 17.4 %copy-start.12 = (f32[256,512]{0,1:T(8,128)}, f32[256,512]{0,1:T(8,128)S(1)}, u32[]{:S(2)}) copy-start(f32[256,512]{0,1:T(8,128)S(1)} %fusion.148) | copy-start | bytes 1572868
  46.5 2.9 copy-start.32
  56.4 7.4 %copy-start.16 = (bf16[256,1,512]{2,0,1:T(8,128)(2,1)}, bf16[256,1,512]{2,0,1:T(8,128)(2,1)S(1)}, u32[]{:S(2)}) copy-start(bf16[256,1,512]{2,0,1:T(8,128)(2,1)S(1)} %fusion.75) | copy-start | bytes 786436
  57.8 3.0 copy-start.4
  76.6 2.8 copy-start.8
  81.2 21.5 %all-to-all-start = ((bf16[256,32,16]{0,2,1:T(8,128)(2,1)}), bf16[256,32,16]{0,2,1:T(8,128)(2,1)}, u32[]{:S(2)}, u32[]{:S(2)}) async-start(bf16[256,32,16]{0,2,1:T(8,128)(2,1)} %bitcast.531), calls=%async_computation | async-start | bytes 524288 | tf_op jit(solution)/shard_map/all_to_all | solution.py:233
  102.7 17.9 %all-to-all-start.2 = ((bf16[256,32,16]{0,2,1:T(8,128)(2,1)}), bf16[256,32,16]{0,2,1:T(8,128)(2,1)}, u32[]{:S(2)}, u32[]{:S(2)}) async-start(bf16[256,32,16]{0,2,1:T(8,128)(2,1)} %bitcast.90), calls=%async_computation.2 | async-start | bytes 524288 | tf_op jit(solution)/shard_map/all_to_all | solution.py:236
  185.5 40.6 %all-to-all-start.3 = ((bf16[32,256,16]{1,2,0:T(8,128)(2,1)}), bf16[32,256,16]{1,2,0:T(8,128)(2,1)}, u32[]{:S(2)}, u32[]{:S(2)}) async-start(bf16[32,256,16]{1,2,0:T(8,128)(2,1)} %copy.487), calls=%async_computation.3 | async-start | bytes 524288 | tf_op jit(solution)/shard_map/all_to_all | solution.py:240
  195.6 4.0 copy-start.30
  212.7 3.0 copy-start.43
  215.7 3.9 copy-start.58
  215.7 3.9 copy-start.60
  215.7 3.9 copy-start.62
  215.7 3.9 copy-start.64
  215.7 3.9 copy-start.66
  215.7 3.9 copy-start.68
  215.7 3.9 copy-start.70
  215.7 3.9 copy-start.72
  215.8 3.9 copy-start.92
  215.8 3.9 copy-start.93
  215.8 3.9 copy-start.94
  215.8 3.9 copy-start.95
  215.8 3.9 copy-start.96
  215.8 3.9 copy-start.97
  215.8 3.9 copy-start.98
  224.4 14.3 %copy-start.107 = (f32[16]{0:T(128)S(1)}, f32[16]{0:T(128)}, u32[]{:S(2)}) copy-start(f32[16]{0:T(128)} %get-tuple-element.118) | copy-start | bytes 196
  224.4 14.3 %copy-start.108 = (f32[16]{0:T(128)S(1)}, f32[16]{0:T(128)}, u32[]{:S(2)}) copy-start(f32[16]{0:T(128)} %get-tuple-element.120) | copy-start | bytes 196
  224.4 14.3 %copy-start.109 = (f32[16]{0:T(128)S(1)}, f32[16]{0:T(128)}, u32[]{:S(2)}) copy-start(f32[16]{0:T(128)} %get-tuple-element.122) | copy-start | bytes 196
  224.4 14.3 %copy-start.110 = (f32[16]{0:T(128)S(1)}, f32[16]{0:T(128)}, u32[]{:S(2)}) copy-start(f32[16]{0:T(128)} %get-tuple-element.124) | copy-start | bytes 196
  224.4 15.1 %copy-start.89 = (f32[16,1]{0,1:T(1,128)S(1)}, f32[16,1]{0,1:T(1,128)}, u32[]{:S(2)}) copy-start(f32[16,1]{0,1:T(1,128)} %get-tuple-element.184) | copy-start | bytes 196
  224.4 15.1 %copy-start.90 = (f32[16,1]{0,1:T(1,128)S(1)}, f32[16,1]{0,1:T(1,128)}, u32[]{:S(2)}) copy-start(f32[16,1]{0,1:T(1,128)} %get-tuple-element.185) | copy-start | bytes 196
  224.4 15.0 %copy-start.91 = (f32[16,1]{0,1:T(1,128)S(1)}, f32[16,1]{0,1:T(1,128)}, u32[]{:S(2)}) copy-start(f32[16,1]{0,1:T(1,128)} %get-tuple-element.186) | copy-start | bytes 196
  225.9 17.4 %copy-start.3 = (f32[2,512,128]{1,2,0:T(8,128)S(1)}, f32[2,512,128]{1,2,0:T(8,128)}, u32[]{:S(2)}) copy-start(f32[2,512,128]{1,2,0:T(8,128)} %copy-done.1) | copy-start | bytes 1572868
  225.9 17.4 %copy-start.9 = (f32[256,2,512]{2,0,1:T(8,128)S(1)}, f32[256,2,512]{2,0,1:T(8,128)}, u32[]{:S(2)}) copy-start(f32[256,2,512]{2,0,1:T(8,128)} %copy-done.8) | copy-start | bytes 3145732
  225.9 17.4 %copy-start.18 = (bf16[256,1,512]{2,0,1:T(8,128)(2,1)S(1)}, bf16[256,1,512]{2,0,1:T(8,128)(2,1)}, u32[]{:S(2)}) copy-start(bf16[256,1,512]{2,0,1:T(8,128)(2,1)} %copy-done.16) | copy-start | bytes 786436
  226.1 30.8 %all-to-all-start.1 = ((bf16[32,256,16]{1,2,0:T(8,128)(2,1)}), bf16[32,256,16]{1,2,0:T(8,128)(2,1)}, u32[]{:S(2)}, u32[]{:S(2)}) async-start(bf16[32,256,16]{1,2,0:T(8,128)(2,1)} %copy.466), calls=%async_computation.1 | async-start | bytes 524288 | tf_op jit(solution)/shard_map/all_to_all | solution.py:235
  238.6 467.4 %all-reduce.4.cloned.1.call-start = ((), (), s32[]{:S(2)}) async-start(), calls=%async_computation.4 | async-start | bytes 262144 | tf_op jit(solution)/shard_map/psum | solution.py:301
  243.3 17.5 %copy-start.23 = (f32[256,512]{1,0:T(8,128)}, f32[256,512]{1,0:T(8,128)S(1)}, u32[]{:S(2)}) copy-start(f32[256,512]{1,0:T(8,128)S(1)} %copy.489) | copy-start | bytes 1572868
  260.8 3.7 copy-start.47
  267.8 12.7 %collective-permute-start.1 = (bf16[137,512]{1,0:T(8,128)(2,1)}, bf16[137,512]{1,0:T(8,128)(2,1)S(1)}, u32[]{:S(2)}, u32[]{:S(2)}) collective-permute-start(bf16[137,512]{1,0:T(8,128)(2,1)} %pad_maximum_fusion.6), channel_id=1, source_target_pairs={{8,0},{16,8},{24,16},{32,24},{40,32},{48,40},{56,48},{64,56},{72,6... | collective-permute-start | bytes 420872 | tf_op jit(solution)/shard_map/ppermute | solution.py:17
  271.4 9.2 %copy-start.25 = (f32[256,512]{1,0:T(8,128)S(1)}, f32[256,512]{1,0:T(8,128)}, u32[]{:S(2)}) copy-start(f32[256,512]{1,0:T(8,128)} %convert_element_type.449) | copy-start | bytes 1572868
  273.5 7.2 %copy-start.38 = (f32[256,256]{1,0:T(8,128)S(1)}, f32[256,256]{1,0:T(8,128)}, u32[]{:S(2)}) copy-start(f32[256,256]{1,0:T(8,128)} %fusion.138) | copy-start | bytes 786436
  293.6 3.0 copy-start.24
  (83 other events, 139.3 us)
Sparse Core Ops, SparseCore 0:
  296.8 409.2 all-reduce.3
where the time goes:
time: 727 us; the launch traced here: 715 us
  blocking collectives  246 us (34%)
  waiting for transfers between devices  198 us (27%)
  matrix products  92.9 us (13%)
  local copies, waits for them, and re-layouts  76.1 us (10%)
  starting transfers between devices  44.3 us (6%)
  other arithmetic  41 us (6%)
  between operations  16.9 us (2%)
    psum x1, blocking collectives, on_device(): lax.psum(taps_medium.astype(jnp.bfloat16), 'ctx').astype(jnp.float32)  222 us
    psum x1, waiting for transfers between devices, on_device(): lax.psum(grad_filter.astype(jnp.bfloat16), 'ctx').astype(jnp.float32)  181 us
  transfers between devices with their start and end apart: 7, of which 4 were waited for; matrix products, arithmetic and copies ran while one was open for 11% of the time, Pallas kernels for 0%

commit v1 on v0

v1 whole, which is shorter than its diff:
```python
import functools
import math

import jax
import jax.numpy as jnp
import ml_dtypes
import numpy as np
from jax import lax
from jax.experimental import pallas as pl
from jax.experimental.pallas import tpu as pltpu
from jax.sharding import PartitionSpec as P

D = 4096
MODES = 16
TAPS = 128
ROWS = 256
LANES = 128
CHUNKS = 8
STEPS = ROWS // CHUNKS
HALO = 144
SHARE = 5
LIMIT = 60
F32 = jnp.float32
BF16 = jnp.bfloat16
precise = lax.Precision.HIGHEST


def fourier_matrices():
    size = 2 * TAPS
    place = np.arange(size)
    mode = np.arange(TAPS)
    turn = 2.0 * math.pi / size
    cos_part = np.cos(turn * ((mode[:, None] * place[None, :]) % size))
    sin_part = -np.sin(turn * ((mode[:, None] * place[None, :]) % size))
    sin_part[0] = 1.0 - 2.0 * (place % 2)
    forward = np.concatenate([cos_part, sin_part], 0)
    weight = np.full((size,), 2.0 / size)
    weight[0] = weight[TAPS] = 1.0 / size
    backward = (forward * weight[:, None]).T

    def halves(table):
        high = table.astype(ml_dtypes.bfloat16)
        low = (table - high.astype(np.float64)).astype(ml_dtypes.bfloat16)
        return np.concatenate([high, low], 0)

    return halves(forward), halves(backward[:TAPS]), halves(backward[TAPS:])


def f32_of(value):
    return value.astype(F32)


def rounded(value):
    return value.astype(BF16).astype(F32)


def spectrum(table, signal):
    both = jnp.dot(table, signal, preferred_element_type=F32)
    return both[: 2 * TAPS] + both[2 * TAPS :]


def from_spectrum(table, values):
    high = values.astype(BF16)
    low = (values - high.astype(F32)).astype(BF16)
    both = jnp.dot(table, high, preferred_element_type=F32)
    rest = jnp.dot(table[:TAPS], low, preferred_element_type=F32)
    return both[:TAPS] + both[TAPS:] + rest


def split_spectrum(values):
    real, imag = values[:TAPS], values[TAPS:]
    first = lax.broadcasted_iota(jnp.int32, real.shape, 0) == 0
    return real, jnp.where(first, imag, real), jnp.where(first, 0.0, imag)


def spread(value, row):
    return jnp.broadcast_to(value[row : row + 1, :], (CHUNKS, LANES))


def chunk_index():
    return lax.broadcasted_iota(jnp.int32, (CHUNKS, LANES), 0)


def at_step(ref, step):
    return ref[pl.ds(step, CHUNKS, stride=STEPS), :]


def chunk_states(source, rate, backward):
    decay = jnp.exp(-rate)
    decays = [spread(decay, r) for r in range(MODES)]

    def body(n, states):
        value = at_step(source, STEPS - 1 - n if backward else n)
        return tuple(decays[r] * states[r] + value for r in range(MODES))

    first = at_step(source, 0)
    return lax.fori_loop(0, STEPS, body, (first - first,) * MODES, unroll=4)


def chunk_entries(ends, rate, backward):
    place = chunk_index()
    entries = []
    for r in range(MODES):
        total = ends[r]
        rate_r = spread(rate, r)
        for by in (1, 2, 4):
            factor = jnp.exp(rate_r * float(-STEPS * by))
            moved = pltpu.roll(total, CHUNKS - by if backward else by, 0)
            inside = place < CHUNKS - by if backward else place >= by
            total = total + jnp.where(inside, factor * moved, 0.0)
        moved = pltpu.roll(total, CHUNKS - 1 if backward else 1, 0)
        entries.append(jnp.where(place < CHUNKS - 1 if backward else place >= 1, moved, 0.0))
    return entries


def chunk_weights(rate, r, backward):
    place = chunk_index()
    after = (place if backward else CHUNKS - 1 - place).astype(F32) * float(STEPS)
    return jnp.exp(-spread(rate, r) * after), after


def local_answer(source, target, rate, weight, entries, backward):
    decay = jnp.exp(-rate)
    decays = [spread(decay, r) for r in range(MODES)]
    weights = [spread(weight, r) for r in range(MODES)]

    def body(n, states):
        step = STEPS - 1 - n if backward else n
        value = at_step(source, step)
        states = tuple(decays[r] * states[r] + value for r in range(MODES))
        terms = [weights[r] * states[r] for r in range(MODES)]
        while len(terms) > 1:
            terms = [terms[k] + terms[k + 1] for k in range(0, len(terms), 2)]
        target[pl.ds(step, CHUNKS, stride=STEPS), :] = terms[0]
        return states

    lax.fori_loop(0, STEPS, body, tuple(entries), unroll=2)


def add_entry(local, target, rate, weight, entry, backward):
    decay = jnp.exp(-rate)
    decays = [spread(decay, r) for r in range(MODES)]
    start = weight * entry
    place = chunk_index()
    ahead = (CHUNKS - 1 - place if backward else place).astype(F32) * float(STEPS)
    parts = [spread(start, r) * jnp.exp(-spread(rate, r) * ahead) for r in range(MODES)]

    def body(n, parts):
        step = STEPS - 1 - n if backward else n
        parts = tuple(decays[r] * parts[r] for r in range(MODES))
        terms = list(parts)
        while len(terms) > 1:
            terms = [terms[k] + terms[k + 1] for k in range(0, len(terms), 2)]
        target[pl.ds(step, CHUNKS, stride=STEPS), :] = at_step(local, step) + terms[0]
        return parts

    lax.fori_loop(0, STEPS, body, tuple(parts), unroll=4)


def entry_state(gathered, rate, count, backward):
    far = jnp.exp(rate * float(-ROWS))

    def body(n, state):
        device = gathered.shape[0] - 1 - n if backward else n
        return far * state + gathered[device, 0:MODES, :].astype(F32)

    return lax.fori_loop(0, count, body, jnp.zeros((MODES, LANES), F32))


def extend(ext, before, body):
    ext[6:8, :] = before
    ext[8 : 8 + ROWS, :] = body


def three(ext, taps):
    return (
        taps[0:1] * ext[8 : 8 + ROWS, :]
        + taps[1:2] * ext[7 : 7 + ROWS, :]
        + taps[2:3] * ext[6 : 6 + ROWS, :]
    )


def store_tap_sums(target, row, grad, ext):
    for shift in range(3):
        target[row + shift : row + shift + 1, :] = jnp.sum(
            grad * ext[8 - shift : 8 - shift + ROWS, :], 0, keepdims=True
        )


def tail_kernel(med, lng, taps, out, ext, rows):
    def feature(j):
        extend(ext, jnp.zeros((2, LANES), F32), f32_of(med[j]))
        return rounded(three(ext, taps[j]))

    key = feature(1)
    val = feature(2)
    out[0:TAPS, :] = (key[TAPS:] * val[TAPS:]).astype(BF16)
    rows[...] = jnp.zeros(rows.shape, F32)
    for j in range(3):
        ext[8 : 8 + ROWS, :] = f32_of(med[j])
        rows[2 * j : 2 * j + 2, :] = ext[6 + ROWS : 8 + ROWS, :]
    for j in range(2):
        ext[8 : 8 + ROWS, :] = f32_of(lng[j])
        rows[6 + 2 * j : 8 + 2 * j, :] = ext[6 + ROWS : 8 + ROWS, :]
    out[TAPS:HALO, :] = rows[...].astype(BF16)


def long_kernel(packed, before, lng, taps, cot, rate_out, weight_out, q_out, k_out, g_out, z_out, ext, halo, grad, rows):
    both = jnp.transpose(packed[...].reshape(LANES, LANES))
    rate = jnp.exp(both[:MODES])
    rate_out[...] = rate
    weight_out[...] = both[MODES : 2 * MODES] * jnp.sqrt(2.0 * rate)
    halo[...] = f32_of(before[...])
    feats = []
    for j in range(2):
        extend(ext, halo[TAPS + 6 + 2 * j : TAPS + 8 + 2 * j, :], f32_of(lng[j]))
        feats.append(three(ext, taps[j]).astype(BF16))
    q_out[...] = feats[0]
    k_out[...] = feats[1]
    sent = (f32_of(cot[...]) * f32_of(feats[0])).astype(BF16)
    g_out[...] = sent
    grad[...] = f32_of(sent)
    states = chunk_states(grad, rate, True)
    for r in range(MODES):
        factor, _ = chunk_weights(rate, r, True)
        rows[r : r + 1, :] = jnp.sum(factor * states[r], 0, keepdims=True)
    z_out[...] = jnp.broadcast_to(rows[...].astype(BF16)[None], z_out.shape)


def medium_kernel(med, before, taps, filt, forward, top, gconv, rate, weight,
                  prod_out, q_out, k_out, v_out, conv_out, gated_out, sq_out, y_out, ext, halo, grad):
    halo[...] = f32_of(before[...])
    feats = []
    for j in range(3):
        extend(ext, halo[TAPS + 2 * j : TAPS + 2 * j + 2, :], f32_of(med[j]))
        feats.append(three(ext, taps[j]).astype(BF16))
    q_out[...] = feats[0]
    k_out[...] = feats[1]
    v_out[...] = feats[2]
    prod_out[0:TAPS, :] = before[0:TAPS, :]
    prod_out[TAPS:, :] = (f32_of(feats[1]) * f32_of(feats[2])).astype(BF16)
    windows = jnp.concatenate([prod_out[0 : 2 * TAPS, :], prod_out[TAPS:, :]], 1)
    win = spectrum(forward[...], windows)
    ker = spectrum(forward[:, 0:TAPS], filt[...])
    ker_re, ker_alt, ker_im = split_spectrum(ker)
    ker_re, ker_alt, ker_im = (jnp.concatenate([k, k], 1) for k in (ker_re, ker_alt, ker_im))
    re, im = win[:TAPS], win[TAPS:]
    spec = jnp.concatenate([re * ker_re - im * ker_im, im * ker_alt + re * ker_im], 0)
    answer = from_spectrum(top[...], spec)
    conv = jnp.concatenate([answer[:, :LANES], answer[:, LANES:]], 0)
    conv_out[...] = conv
    gated = f32_of(feats[0]) * conv
    gated_out[...] = gated
    part = lax.dot_general(
        jnp.ones((8, LANES), F32), gated * gated, (((1,), (1,)), ((), ())),
        precision=precise, preferred_element_type=F32,
    )

    @pl.when(pl.program_id(0) == 0)
    def _():
        sq_out[...] = jnp.zeros(sq_out.shape, F32)

    sq_out[...] += part
    grad[...] = f32_of(gconv[...])
    ends = chunk_states(grad, rate[...], True)
    entries = chunk_entries(ends, rate[...], True)
    local_answer(grad, y_out, rate[...], weight[...], entries, True)


def inner_kernel(me, zg, rate, weight, y_loc, k_two, gated, gain, gp_out, zin_out, in_out, full):
    entry = entry_state(zg, rate[...], zg.shape[0] - 1 - me[0], True)
    zin_out[...] = entry
    add_entry(y_loc, full, rate[...], weight[...], entry, True)
    sent = full[...].astype(BF16)
    gp_out[...] = sent
    product = f32_of(sent) * f32_of(k_two[...]) * gain[...] * gated[...]
    part = lax.dot_general(
        jnp.ones((8, LANES), F32), product, (((1,), (1,)), ((), ())),
        precision=precise, preferred_element_type=F32,
    )

    @pl.when(pl.program_id(0) == 0)
    def _():
        in_out[...] = jnp.zeros(in_out.shape, F32)

    in_out[...] += part


def norm_kernel(sums, gated, conv, q_one, k_one, v_one, k_two, gp, gain, filt, cot,
                x_out, gco_out, gq1_out, gk2_out, gain_out, e_out, work, tail):
    ones = jnp.ones((8, LANES), F32)

    def column(values):
        return lax.dot_general(
            values, ones, (((0,), (0,)), ((), ())), precision=precise, preferred_element_type=F32
        )

    square = column(sums[:, 0:ROWS]) / float(D) + 1e-06
    inner = column(sums[:, ROWS:]) / float(D)
    scale = lax.rsqrt(square)
    gate = gated[...]
    key_two = f32_of(k_two[...])
    normed = rounded(gate * scale * gain[...])
    prod_two = (key_two * normed).astype(BF16)
    x_out[...] = prod_two
    grad_two = f32_of(gp[...])
    grad_k_two = grad_two * normed
    gk2_out[...] = grad_k_two
    grad_normed = grad_two * key_two
    gain_out[...] = jnp.broadcast_to(jnp.sum(grad_normed * gate * scale, 0, keepdims=True), gain_out.shape)
    grad_gated = scale * (grad_normed * gain[...] - gate * scale * scale * inner)
    grad_q_one = grad_gated * conv[...]
    gq1_out[...] = grad_q_one
    gco = (grad_gated * f32_of(q_one[...])).astype(BF16)
    gco_out[...] = gco
    e_out[0:TAPS, :] = gco[0:TAPS]
    tail[...] = jnp.zeros(tail.shape, F32)
    tail[0:2, :] = grad_q_one[0:2]
    work[...] = f32_of(gco)
    taps = f32_of(filt[...])
    for shift in range(2):
        head = jnp.sum(taps * work[shift : shift + TAPS, :], 0, keepdims=True)
        tail[2 + shift : 3 + shift, :] = head * f32_of(v_one[0:16, :])[shift : shift + 1]
        tail[4 + shift : 5 + shift, :] = head * f32_of(k_one[0:16, :])[shift : shift + 1]
    tail[6:8, :] = grad_k_two[0:2]
    tail[8:10, :] = f32_of(prod_two)[0:2]
    tail[10:12, :] = f32_of(cot[0:16, :])[0:2]
    e_out[TAPS:HALO, :] = tail[...].astype(BF16)


def filter_kernel(x, gco, gq1, gk2, gain, prod, med, lng, before, rate, forward, low, slot_out, ext, halo, f_out, work, slot):
    halo[...] = f32_of(before[...])
    work[...] = f32_of(x[...])
    states = chunk_states(work, rate[...], False)
    for r in range(MODES):
        factor, _ = chunk_weights(rate[...], r, False)
        slot[r : r + 1, :] = jnp.sum(factor * states[r], 0, keepdims=True)
    f_out[TAPS:, :] = jnp.zeros((f_out.shape[0] - TAPS, LANES), F32)
    f_out[TAPS : TAPS + 1, :] = gain[0:1, :]
    extend(ext, halo[TAPS : TAPS + 2, :], f32_of(med[0]))
    store_tap_sums(f_out, TAPS + 1, gq1[...], ext)
    extend(ext, halo[TAPS + 8 : TAPS + 10, :], f32_of(lng[1]))
    store_tap_sums(f_out, TAPS + 4, gk2[...], ext)
    windows = jnp.concatenate([prod[0 : 2 * TAPS, :], prod[TAPS:, :]], 1)
    win = spectrum(forward[...], windows)
    pieces = jnp.concatenate([gco[0:TAPS, :], gco[TAPS:, :]], 1)
    grd = spectrum(forward[:, TAPS:], pieces)
    win_re, win_alt, win_im = split_spectrum(win)
    re, im = grd[:TAPS], grd[TAPS:]
    spec = jnp.concatenate([re * win_re + im * win_im, im * win_alt - re * win_im], 0)
    f_out[0:TAPS, :] = from_spectrum(low[...], spec[:, :LANES] + spec[:, LANES:])
    for device in range(slot_out.shape[0]):
        slot[MODES:, :] = f_out[SHARE * device : SHARE * device + 8, :]
        slot_out[device] = slot[...].astype(BF16)


def behind_kernel(g, rate, ends_out, gs):
    gs[...] = f32_of(g[...])
    decay = jnp.exp(-rate[...])
    first = at_step(gs, 0)
    zero = first - first
    half = MODES // 2
    for base in range(0, MODES, half):
        decays = [spread(decay, base + r) for r in range(half)]

        def behind(n, carry):
            z, q = carry
            grad = at_step(gs, STEPS - 1 - n)
            q = tuple(decays[r] * (q[r] + z[r]) for r in range(half))
            z = tuple(decays[r] * z[r] + grad for r in range(half))
            return z, q

        z, q = lax.fori_loop(0, STEPS, behind, ((zero,) * half,) * 2, unroll=4)
        for r in range(half):
            ends_out[base + r] = z[r]
            ends_out[MODES + base + r] = q[r]


def modes_kernel(x, g, rate, weight, ends, y_out, sums_out, xs, gs):
    xs[...] = f32_of(x[...])
    gs[...] = f32_of(g[...])
    rates = rate[...]
    decay = jnp.exp(-rates)
    first = at_step(xs, 0)
    zero = first - first
    half = MODES // 2
    s_end, q_end, plain, slope = [], [], [], []
    for base in range(0, MODES, half):
        decays = [spread(decay, base + r) for r in range(half)]

        def ahead(n, carry):
            s, q, p, l = carry
            value, grad = at_step(xs, n), at_step(gs, n)
            q = tuple(decays[r] * (q[r] + s[r]) for r in range(half))
            s = tuple(decays[r] * s[r] + value for r in range(half))
            p = tuple(p[r] + grad * s[r] for r in range(half))
            l = tuple(l[r] + grad * q[r] for r in range(half))
            return s, q, p, l

        s, q, p, l = lax.fori_loop(0, STEPS, ahead, ((zero,) * half,) * 4, unroll=4)
        s_end += s
        q_end += q
        plain += p
        slope += l
    z_end = [ends[r] for r in range(MODES)]
    zq_end = [ends[MODES + r] for r in range(MODES)]
    entries = chunk_entries(s_end, rates, False)
    exits = chunk_entries(z_end, rates, True)
    for r in range(MODES):
        a = spread(decay, r)
        a_step = jnp.exp(spread(rates, r) * float(-STEPS - 1))
        one = plain[r] + entries[r] * a * z_end[r]
        two = (
            slope[r]
            + float(STEPS) * a_step * entries[r] * exits[r]
            + a * (entries[r] * zq_end[r] + exits[r] * (q_end[r] + s_end[r]))
        )
        back, back_steps = chunk_weights(rates, r, True)
        front, front_steps = chunk_weights(rates, r, False)
        rows = (
            one,
            two,
            back * z_end[r],
            back * (zq_end[r] + back_steps * z_end[r]),
            front * (q_end[r] + s_end[r] + front_steps * s_end[r]),
        )
        for kind, value in enumerate(rows):
            place = kind * MODES + r
            sums_out[place : place + 1, :] = jnp.sum(value, 0, keepdims=True)
    local_answer(xs, y_out, rates, weight[...], entries, False)


def answer_kernel(me, sg, rate, weight, y_loc, q_two, cot, sums, zin, after, gco, filt, k_one, v_one, med, lng, before,
                  forward, low, mixed_out, gq2_out, gk1_out, gv1_out, res_out, taps_out, next_out, ext, halo, full, tail):
    rates = rate[...]
    entry = entry_state(sg, rates, me[0], False)
    add_entry(y_loc, full, rates, weight[...], entry, False)
    conv = rounded(full[...])
    grad_out = f32_of(cot[...])
    mixed_out[...] = (f32_of(q_two[...]) * conv).astype(BF16)
    grad_q_two = grad_out * conv
    gq2_out[...] = grad_q_two
    tail[...] = f32_of(after[TAPS:HALO, :])
    decay = jnp.exp(-rates)
    exit_state = jnp.exp(rates * float(-ROWS)) * entry + f32_of(sg[me[0], 0:MODES, :])
    next_out[...] = jnp.zeros(next_out.shape, F32)
    state = exit_state
    for step in range(2):
        state = decay * state + tail[8 + step : 9 + step, :]
        value = rounded(jnp.sum(weight[...] * state, 0, keepdims=True))
        next_out[step : step + 1, :] = value * tail[10 + step : 11 + step, :]
    plain = sums[0:MODES, :] + entry * decay * sums[2 * MODES : 3 * MODES, :]
    slope = (
        sums[MODES : 2 * MODES, :]
        + float(ROWS) * jnp.exp(rates * float(-ROWS - 1)) * entry * zin[...]
        + decay * (entry * sums[3 * MODES : 4 * MODES, :] + zin[...] * sums[4 * MODES :, :])
    )
    res_out[0:MODES, :] = jnp.sqrt(2.0 * rates) * plain
    res_out[MODES:, :] = weight[...] * (0.5 * plain - rates * slope)
    pieces = jnp.concatenate(
        [gco[...], jnp.concatenate([gco[TAPS:, :], after[0:TAPS, :]], 0)], 1
    )
    win = spectrum(forward[...], pieces)
    ker = spectrum(forward[:, 0:TAPS], filt[...])
    ker_re, ker_alt, ker_im = (jnp.concatenate([k, k], 1) for k in split_spectrum(ker))
    re, im = win[:TAPS], win[TAPS:]
    spec = jnp.concatenate([re * ker_re + im * ker_im, im * ker_alt - re * ker_im], 0)
    answer = from_spectrum(low[...], spec)
    grad_prod = jnp.concatenate([answer[:, :LANES], answer[:, LANES:]], 0)
    grad_k = grad_prod * f32_of(v_one[...])
    grad_v = grad_prod * f32_of(k_one[...])
    gk1_out[...] = grad_k
    gv1_out[...] = grad_v
    halo[...] = f32_of(before[...])
    taps_out[...] = jnp.zeros(taps_out.shape, F32)
    extend(ext, halo[TAPS + 2 : TAPS + 4, :], f32_of(med[1]))
    store_tap_sums(taps_out, 0, grad_k, ext)
    extend(ext, halo[TAPS + 4 : TAPS + 6, :], f32_of(med[2]))
    store_tap_sums(taps_out, 3, grad_v, ext)
    extend(ext, halo[TAPS + 6 : TAPS + 8, :], f32_of(lng[0]))
    store_tap_sums(taps_out, 6, grad_q_two, ext)


def input_kernel(gq1, gk1, gv1, gq2, gk2, after, nxt, mtaps, ltaps, med_out, lng_out, ext, tail):
    tail[...] = f32_of(after[TAPS:HALO, :])

    def back(grad, following, taps):
        ext[0:ROWS, :] = grad[...]
        ext[ROWS : ROWS + 2, :] = following
        return (
            taps[0:1] * ext[0:ROWS, :] + taps[1:2] * ext[1 : ROWS + 1, :] + taps[2:3] * ext[2 : ROWS + 2, :]
        ).astype(BF16)

    med_out[0] = back(gq1, tail[0:2, :], mtaps[0])
    med_out[1] = back(gk1, tail[2:4, :], mtaps[1])
    med_out[2] = back(gv1, tail[4:6, :], mtaps[2])
    lng_out[0] = back(gq2, nxt[0:2, :], ltaps[0])
    lng_out[1] = back(gk2, tail[6:8, :], ltaps[1])


def finish_kernel(last, mtap_out, ltap_out, filt_out, gain_out, res_out, log_out, f_all):
    added = jnp.zeros((last.shape[1], LANES), F32)
    for device in range(last.shape[0]):
        piece = f32_of(last[device])
        f_all[SHARE * device : SHARE * device + 8, :] = piece[0:8]
        added = added + piece
    filt_out[...] = f_all[0:TAPS, :]
    gain_out[...] = f_all[TAPS : TAPS + 1, :]
    for shift in range(3):
        mtap_out[shift, 0:1, :] = f_all[TAPS + 1 + shift : TAPS + 2 + shift, :]
        ltap_out[shift, 1:2, :] = f_all[TAPS + 4 + shift : TAPS + 5 + shift, :]
        mtap_out[shift, 1:2, :] = added[SHARE + shift : SHARE + 1 + shift]
        mtap_out[shift, 2:3, :] = added[SHARE + 3 + shift : SHARE + 4 + shift]
        ltap_out[shift, 0:1, :] = added[SHARE + 6 + shift : SHARE + 7 + shift]
    block = pl.program_id(0)
    lane = lax.broadcasted_iota(jnp.int32, (MODES, LANES), 1)
    row = lax.broadcasted_iota(jnp.int32, (MODES, LANES), 0)
    picked = jnp.where(lane % MODES == row, added[SHARE + 9 : SHARE + 10], 0.0)
    goal = (row == lane // MODES + 8 * (block % 2)).astype(F32)
    part = lax.dot_general(
        picked, goal, (((1,), (1,)), ((), ())), precision=precise, preferred_element_type=F32
    )

    @pl.when(block == 0)
    def _():
        res_out[...] = part

    @pl.when(block == 1)
    def _():
        res_out[...] += part

    @pl.when(block == 2)
    def _():
        log_out[...] = part

    @pl.when(block == 3)
    def _():
        log_out[...] += part


def block_of(shape, kind):
    if kind in ("lane", "kept"):
        lead = shape[:-1]
        return pl.BlockSpec(lead + (LANES,), lambda l: (0,) * len(lead) + (l,))
    if kind == "whole":
        return pl.BlockSpec(shape, lambda l: (0,) * len(shape))
    if kind == "source":
        return pl.BlockSpec((8,) + shape[1:], lambda l: (l,) + (0,) * (len(shape) - 1))
    return pl.BlockSpec(memory_space=pltpu.SMEM)


def run(kernel, name, width, inputs, outputs, scratch, flops=1000000):
    arrays = [array for array, _ in inputs]
    moved = sum(a.size * a.dtype.itemsize for a in arrays)
    return pl.pallas_call(
        kernel,
        grid=(width // LANES,),
        in_specs=[block_of(a.shape, kind) for a, kind in inputs],
        out_specs=[block_of(shape, kind) for shape, _, kind in outputs],
        out_shape=[
            pltpu.VMEM(shape, dtype) if kind == "kept" else jax.ShapeDtypeStruct(shape, dtype)
            for shape, dtype, kind in outputs
        ],
        scratch_shapes=[pltpu.VMEM(shape, F32) for shape in scratch],
        compiler_params=pltpu.CompilerParams(vmem_limit_bytes=LIMIT * 1024 * 1024),
        cost_estimate=pl.CostEstimate(flops=flops, bytes_accessed=moved, transcendentals=0),
        name=name,
    )(*arrays)


def passed_along(array, axis, by):
    count = lax.axis_size(axis)
    pairs = [(i, i + by) for i in range(count) if 0 <= i + by < count]
    return lax.ppermute(array, axis, pairs)


def swap(array, axis):
    return lax.all_to_all(array, axis, split_axis=0, concat_axis=0, tiled=True)


def on_device(medium_input, long_input, medium_taps, long_taps, medium_filter, norm_gain, long_residue, long_log_decay, cotangent):
    width = cotangent.shape[1]
    count = lax.axis_size("ctx")
    me = lax.axis_index("ctx").astype(jnp.int32).reshape(1)
    forward, low, top = (jnp.asarray(table) for table in fourier_matrices())
    med = jnp.transpose(medium_input, (1, 0, 2))
    lng = jnp.transpose(long_input, (1, 0, 2))
    mtaps = jnp.transpose(medium_taps, (1, 0, 2))
    ltaps = jnp.transpose(long_taps, (1, 0, 2))
    gain = norm_gain.reshape(1, width)
    filt = medium_filter
    ext = (ROWS + 8, LANES)
    halo = (HALO, LANES)
    full = (ROWS, LANES)
    rows = (MODES, LANES)
    plane = (ROWS, width)
    modes = (MODES, width)

    mine = jnp.pad(jnp.concatenate([long_log_decay, long_residue], 1), ((0, 0), (0, LANES - 2 * MODES)))
    packed = swap(jnp.broadcast_to(mine[None], (count,) + mine.shape), "ctx")

    (tail,) = run(
        tail_kernel, "tail", width,
        [(med, "lane"), (lng, "lane"), (mtaps, "lane")],
        [((HALO, width), BF16, "lane")], [ext, rows],
    )
    before = passed_along(tail, "ctx", 1)

    rate, weight, q_two, k_two, gconv, z_all = run(
        long_kernel, "long", width,
        [(packed, "source"), (before, "lane"), (lng, "lane"), (ltaps, "lane"), (cotangent, "lane")],
        [(modes, F32, "lane"), (modes, F32, "lane"), (plane, BF16, "lane"), (plane, BF16, "lane"), (plane, BF16, "lane"), ((count,) + modes, BF16, "lane")],
        [ext, halo, full, rows],
    )
    zg = swap(z_all, "ctx")

    prod, q_one, k_one, v_one, conv, gated, square, y_back = run(
        medium_kernel, "medium", width,
        [(med, "lane"), (before, "lane"), (mtaps, "lane"), (filt, "lane"), (forward, "whole"), (top, "whole"), (gconv, "lane"), (rate, "lane"), (weight, "lane")],
        [((ROWS + TAPS, width), BF16, "lane"), (plane, BF16, "lane"), (plane, BF16, "lane"), (plane, BF16, "lane"), (plane, F32, "lane"), (plane, F32, "lane"), ((8, ROWS), F32, "whole"), (plane, F32, "lane")],
        [ext, halo, full],
    )
    grad_prod, zin, inner = run(
        inner_kernel, "inner", width,
        [(me, "scalar"), (zg, "lane"), (rate, "lane"), (weight, "lane"), (y_back, "lane"), (k_two, "lane"), (gated, "lane"), (gain, "lane")],
        [(plane, BF16, "lane"), (modes, F32, "lane"), ((8, ROWS), F32, "whole")],
        [full],
    )
    sums = swap(jnp.concatenate([square, inner], 1), "tp")

    x, gco, gq1, gk2, gain_row, edge = run(
        norm_kernel, "norm", width,
        [(sums, "whole"), (gated, "lane"), (conv, "lane"), (q_one, "lane"), (k_one, "lane"), (v_one, "lane"), (k_two, "lane"), (grad_prod, "lane"), (gain, "lane"), (filt, "lane"), (cotangent, "lane")],
        [(plane, BF16, "lane"), (plane, BF16, "lane"), (plane, F32, "lane"), (plane, F32, "lane"), ((8, width), F32, "lane"), ((HALO, width), BF16, "lane")],
        [full, rows],
    )
    after = passed_along(edge, "ctx", -1)
    (sent,) = run(
        filter_kernel, "filter", width,
        [(x, "lane"), (gco, "lane"), (gq1, "lane"), (gk2, "lane"), (gain_row, "lane"), (prod, "lane"), (med, "lane"), (lng, "lane"), (before, "lane"), (rate, "lane"), (forward, "whole"), (low, "whole")],
        [((count, MODES + 8, width), BF16, "lane")],
        [ext, halo, (SHARE * count + 8, LANES), full, (MODES + 8, LANES)],
    )
    got = swap(sent, "ctx")

    (ends,) = run(
        behind_kernel, "behind", width, [(gconv, "lane"), (rate, "lane")],
        [((2 * MODES, CHUNKS, width), F32, "lane")], [full],
    )
    y_front, mode_sums = run(
        modes_kernel, "modes", width,
        [(x, "lane"), (gconv, "lane"), (rate, "lane"), (weight, "lane"), (ends, "lane")],
        [(plane, F32, "lane"), ((5 * MODES, width), F32, "lane")],
        [full, full],
    )
    mixed, gq2, gk1, gv1, res, taps, nxt = run(
        answer_kernel, "answer", width,
        [(me, "scalar"), (got, "lane"), (rate, "lane"), (weight, "lane"), (y_front, "lane"), (q_two, "lane"), (cotangent, "lane"), (mode_sums, "lane"), (zin, "lane"), (after, "lane"), (gco, "lane"), (filt, "lane"), (k_one, "lane"), (v_one, "lane"), (med, "lane"), (lng, "lane"), (before, "lane"), (forward, "whole"), (low, "whole")],
        [(plane, BF16, "lane"), (plane, F32, "lane"), (plane, F32, "lane"), (plane, F32, "lane"), ((2 * MODES, width), F32, "lane"), ((MODES, width), F32, "lane"), ((8, width), F32, "lane")],
        [ext, halo, full, rows],
    )
    reduced = jnp.sum(got[:, MODES : MODES + SHARE].astype(F32), 0).astype(BF16)
    every = jnp.concatenate([reduced, taps[:9].astype(BF16)], 0)
    own = res.astype(BF16).reshape(2 * MODES, count, MODES).transpose(1, 0, 2).reshape(count, 1, width)
    last = swap(jnp.concatenate([jnp.broadcast_to(every[None], (count,) + every.shape), own], 1), "ctx")

    grad_med, grad_lng = run(
        input_kernel, "inputs", width,
        [(gq1, "lane"), (gk1, "lane"), (gv1, "lane"), (gq2, "lane"), (gk2, "lane"), (after, "lane"), (nxt, "lane"), (mtaps, "lane"), (ltaps, "lane")],
        [((3, ROWS, width), BF16, "lane"), ((2, ROWS, width), BF16, "lane")],
        [ext, rows],
    )
    taps_medium, taps_long, grad_filter, gain_total, grad_residue, grad_log = run(
        finish_kernel, "finish", width, [(last, "lane")],
        [((3, 3, width), F32, "lane"), ((3, 2, width), F32, "lane"), ((TAPS, width), F32, "lane"), ((1, width), F32, "lane"), ((MODES, MODES), F32, "whole"), ((MODES, MODES), F32, "whole")],
        [(SHARE * count + 8, LANES)],
    )
    return (
        mixed,
        jnp.transpose(grad_med, (1, 0, 2)),
        jnp.transpose(grad_lng, (1, 0, 2)),
        taps_medium,
        taps_long,
        grad_filter,
        gain_total.reshape(width),
        grad_residue,
        grad_log,
    )


def solution(mesh):
    return jax.shard_map(
        on_device,
        mesh=mesh,
        in_specs=(
            P("ctx", None, "tp"),
            P("ctx", None, "tp"),
            P(None, None, "tp"),
            P(None, None, "tp"),
            P(None, "tp"),
            P("tp"),
            P(("tp", "ctx"), None),
            P(("tp", "ctx"), None),
            P("ctx", "tp"),
        ),
        out_specs=(
            P("ctx", "tp"),
            P("ctx", None, "tp"),
            P("ctx", None, "tp"),
            P(None, None, "tp"),
            P(None, None, "tp"),
            P(None, "tp"),
            P("tp"),
            P(("tp", "ctx"), None),
            P(("tp", "ctx"), None),
        ),
        check_vma=False,
    )
```

time: 727 us -> 172 us (0.24); the launches traced: 715 us -> 170 us
  blocking collectives: 246 us -> 7.27 us
  waiting for transfers between devices: 198 us -> 43.8 us
  matrix products: 92.9 us -> 0 us
  local copies, waits for them, and re-layouts: 76.1 us -> 10.3 us
  Pallas kernels: 0 us -> 59.5 us
  other arithmetic: 41 us -> 4.37 us
  between operations: 16.9 us -> 0.8 us
    psum x3 -> x0, blocking collectives: 246 us -> none  [the longest x1 222 us: on_device(): lax.psum(taps_medium.astype(jnp.bfloat16), 'ctx').astype(jnp.float32)]
    psum x1 -> x0, waiting for transfers between devices: 181 us -> none  [on_device(): lax.psum(grad_filter.astype(jnp.bfloat16), 'ctx').astype(jnp.float32)]
    dot_general x52 -> x0, matrix products: 92.9 us -> none  [the longest x3 8.17 us: inverse_fourier(): jnp.einsum('kjc,bj->kbc', spec_im, last_sin, precision=precise)]
    pallas_call x0 -> x11, Pallas kernels: none -> 59.5 us  [run(): pl.pallas_call(kernel, grid=(width // LANES,), in_specs=[block_of(a.shape...]
    reshape x18 -> x1, local copies, waits for them, and re-layouts: 21.1 us -> 0.14 us  [on_device(): res.astype(BF16).reshape(2 * MODES, count, MODES).transpose(1, 0, 2)]
    convert_element_type x23 -> x1, other arithmetic: 19.1 us -> 0.84 us  [on_device(): res.astype(BF16).reshape(2 * MODES, count, MODES).transpose(1, 0, 2)]
    convert_element_type x9 -> x1, local copies, waits for them, and re-layouts: 15.2 us -> 0.12 us  [on_device(): res.astype(BF16).reshape(2 * MODES, count, MODES).transpose(1, 0, 2)]
    ppermute x2, waiting for transfers between devices: 7.03 us -> 20.7 us  [passed_along(): return lax.ppermute(array, axis, pairs)]
  transfers between devices with their start and end apart: 7 -> 6, of which waited for: 4 -> 5; matrix products, arithmetic and copies ran while one was open for 11% -> 3% of each run, Pallas kernels for 0% -> 17%
where the time goes in v1:
time: 172 us; the launch traced here: 170 us
  Pallas kernels  59.5 us (35%)
  waiting for transfers between devices  43.8 us (25%)
  starting transfers between devices  43.5 us (25%)
  local copies, waits for them, and re-layouts  10.3 us (6%)
  blocking collectives  7.27 us (4%)
  other arithmetic  4.37 us (3%)
    pallas_call x11, Pallas kernels, run(): pl.pallas_call(kernel, grid=(width // LANES,), in_specs=[block_of(a.shape...  59.5 us
    all_to_all x4, starting transfers between devices, swap(): return lax.all_to_all(array, axis, split_axis=0, concat_axis=0, tiled=True)  34.6 us
    all_to_all x4, waiting for transfers between devices, swap(): return lax.all_to_all(array, axis, split_axis=0, concat_axis=0, tiled=True)  23.1 us
    ppermute x2, waiting for transfers between devices, passed_along(): return lax.ppermute(array, axis, pairs)  20.7 us
    ppermute x2, starting transfers between devices, passed_along(): return lax.ppermute(array, axis, pairs)  8.89 us
    unnamed x27, local copies, waits for them, and re-layouts  8.29 us
    all_to_all x1, blocking collectives, swap(): return lax.all_to_all(array, axis, split_axis=0, concat_axis=0, tiled=True)  7.27 us
  transfers between devices with their start and end apart: 6, of which 5 were waited for; matrix products, arithmetic and copies ran while one was open for 3% of the time, Pallas kernels for 17%

profile of v1, /device:TPU:64, one launch (start us, length us, event | category | flops | bytes accessed | tf_op | source)
XLA Modules:
  0.0 169.6 jit_solution(17194690831683633367)
XLA Ops:
  0.6 0.0 copy-start.6
  0.7 0.8 select_maximum_fusion
  1.5 0.7 broadcast_in_dim.4
  2.2 12.1 %all-to-all-start = ((f32[32,16,128]{2,1,0:T(8,128)}), f32[32,16,128]{2,1,0:T(8,128)S(1)}, u32[]{:S(2)}, u32[]{:S(2)}) async-start(f32[32,16,128]{2,1,0:T(8,128)} %broadcast_in_dim.4), calls=%async_computation | async-start | bytes 524288 | tf_op jit(solution)/shard_map/all_to_all | solution.py:578
  14.4 0.0 copy-start.7
  14.4 0.8 copy.46
  15.2 0.0 copy-done.7
  15.2 0.6 copy.47
  15.9 3.4 %tail.1 = bf16[144,512]{1,0:T(8,128)(2,1)} custom-call(bf16[3,256,512]{2,1,0:T(8,128)(2,1)} %bitcast.28, bf16[2,256,512]{2,1,0:T(8,128)(2,1)} %bitcast.24, f32[3,3,512]{2,1,0:T(4,128)} %bitcast.35), custom_call_target="tpu_custom_call" | custom-call | flops 1000000 | bytes 1329152 | tf_op jit(solution)/shard_map/tail/pallas_call | solution.py:555
  19.3 7.6 %collective-permute-start = (bf16[144,512]{1,0:T(8,128)(2,1)}, bf16[144,512]{1,0:T(8,128)(2,1)S(1)}, u32[]{:S(2)}, u32[]{:S(2)}) collective-permute-start(bf16[144,512]{1,0:T(8,128)(2,1)} %tail.1), channel_id=1, source_target_pairs={{0,8},{8,16},{16,24},{24,32},{32,40},{40,48},{48,56},{56,64},{64,7... | collective-permute-start | bytes 442376 | tf_op jit(solution)/shard_map/ppermute | solution.py:574
  26.9 0.6 copy.49
  27.5 5.3 %collective-permute-done.before = bf16[144,512]{1,0:T(8,128)(2,1)S(1)} collective-permute-done((bf16[144,512]{1,0:T(8,128)(2,1)}, bf16[144,512]{1,0:T(8,128)(2,1)S(1)}, u32[]{:S(2)}, u32[]{:S(2)}) %collective-permute-start) | collective-permute-done | bytes 147488 | tf_op jit(solution)/shard_map/ppermute | solution.py:574
  32.8 0.0 all-to-all-done.packed
  32.8 0.7 copy-done.1
  33.5 0.1 copy-done.4
  33.6 4.2 %long.1 = (f32[16,512]{1,0:T(8,128)}, f32[16,512]{1,0:T(8,128)}, bf16[256,512]{1,0:T(8,128)(2,1)}, bf16[256,512]{1,0:T(8,128)(2,1)}, bf16[256,512]{1,0:T(8,128)(2,1)}, /*index=5*/bf16[32,16,512]{2,1,0:T(8,128)(2,1)}) custom-call(f32[32,16,128]{2,1,0:T(8,128)} %copy-done.4, bf16[144,512]{1,0:T(8,128)(2,1)} %copy-done.1, bf16[2,256,512]{2,1,0:T(8,128)(2,1)} %bitcast.25, ...), custom_call_target="tpu_custom_call" | custom-call | flops 1000000 | bytes 1208320 | tf_op jit(solution)/shard_map/long/pallas_call | solution.py:555
  37.8 12.9 %all-to-all-start.1 = ((bf16[32,16,512]{2,1,0:T(8,128)(2,1)}), bf16[32,16,512]{2,1,0:T(8,128)(2,1)S(1)}, u32[]{:S(2)}, u32[]{:S(2)}) async-start(bf16[32,16,512]{2,1,0:T(8,128)(2,1)} %get-tuple-element.53), calls=%async_computation.1 | async-start | bytes 1048576 | tf_op jit(solution)/shard_map/all_to_all | solution.py:578
  50.7 9.4 %medium.1 = (bf16[384,512]{1,0:T(8,128)(2,1)}, bf16[256,512]{1,0:T(8,128)(2,1)}, bf16[256,512]{1,0:T(8,128)(2,1)}, bf16[256,512]{1,0:T(8,128)(2,1)}, f32[256,512...) custom-call(bf16[3,256,512]{2,1,0:T(8,128)(2,1)} %bitcast.29, ...), custom_call_target="tpu_custom_call" | custom-call | flops 1000000 | bytes 1804288 | tf_op jit(solution)/shard_map/medium/pallas_call | solution.py:555
  60.1 10.0 %all-to-all-done.1.zg = bf16[32,16,512]{2,1,0:T(8,128)(2,1)S(1)} async-done(((bf16[32,16,512]{2,1,0:T(8,128)(2,1)}), bf16[32,16,512]{2,1,0:T(8,128)(2,1)S(1)}, u32[]{:S(2)}, u32[]{:S(2)}) %all-to-all-start.1) | async-done | bytes 524320 | tf_op jit(solution)/shard_map/all_to_all | solution.py:578
  70.1 0.8 copy-done.2
  70.9 4.8 %inner.1 = (bf16[256,512]{1,0:T(8,128)(2,1)}, f32[16,512]{1,0:T(8,128)}, f32[8,256]{1,0:T(8,128)}) custom-call(s32[1]{0:T(128)} %bitcast.me, bf16[32,16,512]{2,1,0:T(8,128)(2,1)} %copy-done.2, f32[16,512]{1,0:T(8,128)} %get-tuple-element.50.rate, f32[16,512]{1,0:T(8,128)} %get-tuple-element.51.weight, f32[256,512]{1,0:T(8,128)} %get-tuple-element.54.y_loc, ...), custom_call_target="tpu_custom_call" | custom-call | flops 1000000 | bytes 1902596 | tf_op jit(solution)/shard_map/inner/pallas_call | solution.py:555
  75.7 0.7 maximum_bitcast_fusion
  76.4 7.3 %all_to_all.31 = f32[8,1,512]{2,1,0:T(1,128)S(1)} all-to-all(f32[8,1,512]{2,1,0:T(1,128)S(1)} %copy.36), channel_id=1, replica_groups=mesh['ctx'=32,'tp'=8] {'tp'}, dimensions={0} | all-to-all | bytes 32768 | tf_op jit(solution)/shard_map/all_to_all | solution.py:578
  83.7 0.6 copy.48
  84.3 5.0 %norm.1 = (bf16[256,512]{1,0:T(8,128)(2,1)}, bf16[256,512]{1,0:T(8,128)(2,1)}, f32[256,512]{1,0:T(8,128)}, f32[256,512]{1,0:T(8,128)}, f32[8,512]{1,0:T(8,128)}, /*index=5*/bf16[144,512]{1,0:T(8,128)(2,1)}) custom-call(f32[8,512]{1,0:T(8,128)} %bitcast.40, f32[256,512]{1,0:T(8,128)} %get-tuple-element.56.gated, f32[256,512]{1,0:T(8,128)} %get-tuple-element.58.conv, ...), custom_call_target="tpu_custom_call" | custom-call | flops 1000000 | bytes 2770944 | tf_op jit(solution)/shard_map/norm/pallas_call | solution.py:555
  89.3 5.9 %filter.1 = bf16[32,24,512]{2,1,0:T(8,128)(2,1)} custom-call(bf16[256,512]{1,0:T(8,128)(2,1)} %get-tuple-element.63.x, bf16[256,512]{1,0:T(8,128)(2,1)} %get-tuple-element.64.gco, f32[256,512]{1,0:T(8,128)} %get-tuple-element.65.gq1, f32[256,512]{1,0:T(8,128)} %get-tuple-element.66.gk2, f32[8,512]{1,0:T(8,128)} %get-tuple-element.67.gain, ...), custom_call_target="tpu_custom_call" | custom-call | flops 1000000 | bytes 3866624 | tf_op jit(solution)/shard_map/filter/pallas_call | solution.py:555
  95.2 4.1 %all-to-all-start.3 = ((bf16[32,24,512]{2,1,0:T(8,128)(2,1)}), bf16[32,24,512]{2,1,0:T(8,128)(2,1)S(1)}, u32[]{:S(2)}, u32[]{:S(2)}) async-start(bf16[32,24,512]{2,1,0:T(8,128)(2,1)} %filter.1), calls=%async_computation.3 | async-start | bytes 1572864 | tf_op jit(solution)/shard_map/all_to_all | solution.py:578
  99.3 1.3 collective-permute-start.1
  100.6 4.0 %behind.1.ends = f32[32,8,512]{2,1,0:T(8,128)} custom-call(bf16[256,512]{1,0:T(8,128)(2,1)} %get-tuple-element.49.gconv.g, f32[16,512]{1,0:T(8,128)} %get-tuple-element.50.rate), custom_call_target="tpu_custom_call" | custom-call | flops 1000000 | bytes 294912 | tf_op jit(solution)/shard_map/behind/pallas_call | solution.py:555
  104.6 8.5 %modes.1 = (f32[256,512]{1,0:T(8,128)}, f32[80,512]{1,0:T(8,128)}) custom-call(bf16[256,512]{1,0:T(8,128)(2,1)} %get-tuple-element.63.x, bf16[256,512]{1,0:T(8,128)(2,1)} %get-tuple-element.49.gconv.g, f32[16,512]{1,0:T(8,128)} %get-tuple-element.50.rate, f32[16,512]{1,0:T(8,128)} %get-tuple-element.51.weight, f32[32,8,512]{2,1,0:T(8,128)} %behind.1.ends), custom_call_target="tpu_custom_call" | custom-call | flops 1000000 | bytes 1114112 | tf_op jit(solution)/shard_map/modes/pallas_call | solution.py:555
  113.1 15.4 %collective-permute-done.1.after = bf16[144,512]{1,0:T(8,128)(2,1)S(1)} collective-permute-done((bf16[144,512]{1,0:T(8,128)(2,1)S(1)}, bf16[144,512]{1,0:T(8,128)(2,1)S(1)}, u32[]{:S(2)}, u32[]{:S(2)}) %collective-permute-start.1) | collective-permute-done | bytes 147488 | tf_op jit(solution)/shard_map/ppermute | solution.py:574
  128.5 2.8 %all-to-all-done.3.sg = bf16[32,24,512]{2,1,0:T(8,128)(2,1)S(1)} async-done(((bf16[32,24,512]{2,1,0:T(8,128)(2,1)}), bf16[32,24,512]{2,1,0:T(8,128)(2,1)S(1)}, u32[]{:S(2)}, u32[]{:S(2)}) %all-to-all-start.3) | async-done | bytes 786464 | tf_op jit(solution)/shard_map/all_to_all | solution.py:578
  131.2 0.9 copy-done
  132.1 6.5 %answer.1 = (bf16[256,512]{1,0:T(8,128)(2,1)}, f32[256,512]{1,0:T(8,128)}, f32[256,512]{1,0:T(8,128)}, f32[256,512]{1,0:T(8,128)}, f32[32,512]{1,0:T(8,128)}, /*index=5*/f32[16,512]{1,0:T(8,128)}, f32[8,512]{1,0:T(8,128)}) custom-call(s32[1]{0:T(128)} %bitcast.me, bf16[32,24,512]{2,1,0:T(8,128)(2,1)} %copy-done, f32[16,512]{1,0:T(8,128)} %get-tuple-element.50.rate, ...), custom_call_target="tpu_custom_call" | custom-call | flops 1000000 | bytes 5013508 | tf_op jit(solution)/shard_map/answer/pallas_call | solution.py:555
  138.6 0.8 slice.13
  139.4 0.8 convert_element_type.4
  140.3 0.1 copy.37
  140.4 0.2 copy.38
  140.6 0.1 copy.39
  140.7 1.0 slice_reduce_fusion
  141.8 0.1 broadcast_in_dim.5
  141.8 0.9 pad_maximum_fusion
  142.8 5.5 %all-to-all-start.4 = ((bf16[32,15,512]{2,1,0:T(8,128)(2,1)}), bf16[32,15,512]{2,1,0:T(8,128)(2,1)S(1)}, u32[]{:S(2)}, u32[]{:S(2)}) async-start(bf16[32,15,512]{2,1,0:T(8,128)(2,1)} %pad_maximum_fusion), calls=%async_computation.4 | async-start | bytes 1048576 | tf_op jit(solution)/shard_map/all_to_all | solution.py:578
  148.3 4.2 %inputs.1 = (bf16[3,256,512]{2,1,0:T(8,128)(2,1)}, bf16[2,256,512]{2,1,0:T(8,128)(2,1)}) custom-call(f32[256,512]{1,0:T(8,128)} %get-tuple-element.65.gq1, f32[256,512]{1,0:T(8,128)} %get-tuple-element.75.gk1, f32[256,512]{1,0:T(8,128)} %get-tuple-element.76.gv1, f32[256,512]{1,0:T(8,128)} %get-tuple-element.77.gq2, f32[256,512]{1,0:T(8,128)} %get-tuple-element.66.gk2, ...), custom_call_target="tpu_custom_call" | custom-call | flops 1000000 | bytes 2816000 | tf_op jit(solution)/shard_map/inputs/pallas_call | solution.py:555
  152.6 2.4 %copy.40 = bf16[256,2,512]{2,1,0:T(2,128)(2,1)} copy(bf16[256,2,512]{2,0,1:T(8,128)(2,1)} %bitcast.33) | data formatting | bytes 1048576
  154.9 10.4 %all-to-all-done.4.last = bf16[32,15,512]{2,1,0:T(8,128)(2,1)S(1)} async-done(((bf16[32,15,512]{2,1,0:T(8,128)(2,1)}), bf16[32,15,512]{2,1,0:T(8,128)(2,1)S(1)}, u32[]{:S(2)}, u32[]{:S(2)}) %all-to-all-start.4) | async-done | bytes 491552 | tf_op jit(solution)/shard_map/all_to_all | solution.py:578
  165.3 0.8 copy-done.3
  166.1 3.5 %finish.1 = (f32[3,3,512]{2,1,0:T(4,128)}, f32[3,2,512]{2,1,0:T(2,128)}, f32[128,512]{1,0:T(8,128)}, f32[1,512]{1,0:T(1,128)}, f32[16,16]{1,0:T(8,128)}, /*index=5*/f32[16,16]{1,0:T(8,128)}) custom-call(bf16[32,15,512]{2,1,0:T(8,128)(2,1)} %copy-done.3), custom_call_target="tpu_custom_call" | custom-call | flops 1000000 | bytes 491520 | tf_op jit(solution)/shard_map/finish/pallas_call | solution.py:555
  (16 shorter events, 0.1 us)
Async XLA Ops:
  0.6 13.7 %copy-start.6 = (bf16[256,2,512]{2,1,0:T(2,128)(2,1)S(1)}, bf16[256,2,512]{2,1,0:T(2,128)(2,1)}, u32[]{:S(2)}) copy-start(bf16[256,2,512]{2,1,0:T(2,128)(2,1)} %param.13) | copy-start | bytes 1572868
  2.2 30.6 %all-to-all-start = ((f32[32,16,128]{2,1,0:T(8,128)}), f32[32,16,128]{2,1,0:T(8,128)S(1)}, u32[]{:S(2)}, u32[]{:S(2)}) async-start(f32[32,16,128]{2,1,0:T(8,128)} %broadcast_in_dim.4), calls=%async_computation | async-start | bytes 524288 | tf_op jit(solution)/shard_map/all_to_all | solution.py:578
  14.4 0.9 copy-start.7
  15.9 11.0 %copy-start.8 = (f32[3,2,512]{2,1,0:T(2,128)S(1)}, f32[3,2,512]{2,1,0:T(2,128)}, u32[]{:S(2)}) copy-start(f32[3,2,512]{2,1,0:T(2,128)} %param.15) | copy-start | bytes 36868
  19.3 13.5 %collective-permute-start = (bf16[144,512]{1,0:T(8,128)(2,1)}, bf16[144,512]{1,0:T(8,128)(2,1)S(1)}, u32[]{:S(2)}, u32[]{:S(2)}) collective-permute-start(bf16[144,512]{1,0:T(8,128)(2,1)} %tail.1), channel_id=1, source_target_pairs={{0,8},{8,16},{16,24},{24,32},{32,40},{40,48},{48,56},{56,64},{64,7... | collective-permute-start | bytes 442376 | tf_op jit(solution)/shard_map/ppermute | solution.py:574
  32.8 0.7 copy-start.1
  32.8 0.7 copy-start.4
  37.8 32.3 %all-to-all-start.1 = ((bf16[32,16,512]{2,1,0:T(8,128)(2,1)}), bf16[32,16,512]{2,1,0:T(8,128)(2,1)S(1)}, u32[]{:S(2)}, u32[]{:S(2)}) async-start(bf16[32,16,512]{2,1,0:T(8,128)(2,1)} %get-tuple-element.53), calls=%async_computation.1 | async-start | bytes 1048576 | tf_op jit(solution)/shard_map/all_to_all | solution.py:578
  70.1 0.8 copy-start.2
  70.9 4.8 %copy-start.9 = (f32[8,256]{1,0:T(8,128)S(1)}, f32[8,256]{1,0:T(8,128)}, u32[]{:S(2)}) copy-start(f32[8,256]{1,0:T(8,128)} %get-tuple-element.52) | copy-start | bytes 24580
  95.2 4.1 %copy-start.10 = (bf16[144,512]{1,0:T(8,128)(2,1)S(1)}, bf16[144,512]{1,0:T(8,128)(2,1)}, u32[]{:S(2)}) copy-start(bf16[144,512]{1,0:T(8,128)(2,1)} %get-tuple-element.73) | copy-start | bytes 442372
  95.2 36.0 %all-to-all-start.3 = ((bf16[32,24,512]{2,1,0:T(8,128)(2,1)}), bf16[32,24,512]{2,1,0:T(8,128)(2,1)S(1)}, u32[]{:S(2)}, u32[]{:S(2)}) async-start(bf16[32,24,512]{2,1,0:T(8,128)(2,1)} %filter.1), calls=%async_computation.3 | async-start | bytes 1572864 | tf_op jit(solution)/shard_map/all_to_all | solution.py:578
  99.3 29.2 %collective-permute-start.1 = (bf16[144,512]{1,0:T(8,128)(2,1)S(1)}, bf16[144,512]{1,0:T(8,128)(2,1)S(1)}, u32[]{:S(2)}, u32[]{:S(2)}) collective-permute-start(bf16[144,512]{1,0:T(8,128)(2,1)S(1)} %copy-done.10), channel_id=1, source_target_pairs={{8,0},{16,8},{24,16},{32,24},{40,32},{48,40},{56,48},{64,56},{72,6... | collective-permute-start | bytes 442376 | tf_op jit(solution)/shard_map/ppermute | solution.py:574
  128.5 2.8 %copy-start.5 = (bf16[144,512]{1,0:T(8,128)(2,1)}, bf16[144,512]{1,0:T(8,128)(2,1)S(1)}, u32[]{:S(2)}) copy-start(bf16[144,512]{1,0:T(8,128)(2,1)S(1)} %collective-permute-done.1.after) | copy-start | bytes 442372
  131.2 0.9 copy-start
  142.8 22.6 %all-to-all-start.4 = ((bf16[32,15,512]{2,1,0:T(8,128)(2,1)}), bf16[32,15,512]{2,1,0:T(8,128)(2,1)S(1)}, u32[]{:S(2)}, u32[]{:S(2)}) async-start(bf16[32,15,512]{2,1,0:T(8,128)(2,1)} %pad_maximum_fusion), calls=%async_computation.4 | async-start | bytes 1048576 | tf_op jit(solution)/shard_map/all_to_all | solution.py:578
  165.3 0.8 copy-start.3

commit v2 on v1

v2 whole, which is shorter than its diff:
```python
import functools
import math

import jax
import jax.numpy as jnp
import ml_dtypes
import numpy as np
from jax import lax
from jax.experimental import pallas as pl
from jax.experimental.pallas import tpu as pltpu
from jax.sharding import PartitionSpec as P

D = 4096
MODES = 16
TAPS = 128
ROWS = 256
LANES = 128
CHUNKS = 8
STEPS = ROWS // CHUNKS
HALO = 144
WIDE = ROWS + TAPS
Q_END = TAPS
LONG_END = TAPS + 6
SHARE = 5
PAIRS = 16
HALF = SHARE * PAIRS
F32 = jnp.float32
BF16 = jnp.bfloat16
precise = lax.Precision.HIGHEST


def fourier_matrices():
    size = 2 * TAPS
    place = np.arange(size)
    mode = np.arange(TAPS)
    turn = 2.0 * math.pi / size
    cos_part = np.cos(turn * ((mode[:, None] * place[None, :]) % size))
    sin_part = -np.sin(turn * ((mode[:, None] * place[None, :]) % size))
    sin_part[0] = 1.0 - 2.0 * (place % 2)
    forward = np.concatenate([cos_part, sin_part], 0)
    weight = np.full((size,), 2.0 / size)
    weight[0] = weight[TAPS] = 1.0 / size
    backward = (forward * weight[:, None]).T

    return tuple(
        table.astype(ml_dtypes.bfloat16) for table in (forward, backward[:TAPS], backward[TAPS:])
    )


def f32_of(value):
    return value.astype(F32)


def rounded(value):
    return value.astype(BF16).astype(F32)


def spectrum(table, signal):
    return jnp.dot(table, signal, preferred_element_type=F32)


def from_spectrum(table, values):
    return jnp.dot(table, values.astype(BF16), preferred_element_type=F32)


def split_spectrum(values):
    real, imag = values[:TAPS], values[TAPS:]
    first = lax.broadcasted_iota(jnp.int32, real.shape, 0) == 0
    return real, jnp.where(first, imag, real), jnp.where(first, 0.0, imag)


def spread(value, row):
    return jnp.broadcast_to(value[row : row + 1, :], (CHUNKS, LANES))


def chunk_index():
    return lax.broadcasted_iota(jnp.int32, (CHUNKS, LANES), 0)


def at_step(ref, step):
    return ref[pl.ds(step, CHUNKS, stride=STEPS), :]


def chunk_states(source, rate, backward):
    decay = jnp.exp(-rate)
    decays = [spread(decay, r) for r in range(MODES)]

    def body(n, states):
        value = at_step(source, STEPS - 1 - n if backward else n)
        return tuple(decays[r] * states[r] + value for r in range(MODES))

    first = at_step(source, 0)
    return lax.fori_loop(0, STEPS, body, (first - first,) * MODES, unroll=4)


def powers(rate):
    return [jnp.exp(rate * float(-STEPS * by)) for by in (1, 2, 4)]


def chunk_entries(ends, power, backward):
    place = chunk_index()
    inside = [place < CHUNKS - by if backward else place >= by for by in (1, 2, 4)]
    entries = []
    for r in range(MODES):
        total = ends[r]
        for level, by in enumerate((1, 2, 4)):
            moved = pltpu.roll(total, CHUNKS - by if backward else by, 0)
            total = total + jnp.where(inside[level], spread(power[level], r) * moved, 0.0)
        moved = pltpu.roll(total, CHUNKS - 1 if backward else 1, 0)
        entries.append(jnp.where(inside[0], moved, 0.0))
    return entries


def chunk_weights(power, backward):
    after = chunk_index() if backward else CHUNKS - 1 - chunk_index()
    bits = [(after & by) != 0 for by in (1, 2, 4)]

    def weight(r):
        parts = [jnp.where(bit, spread(level, r), 1.0) for bit, level in zip(bits, power)]
        return parts[0] * parts[1] * parts[2]

    return weight, after.astype(F32) * float(STEPS)


def local_answer(source, target, rate, weight, entries, backward):
    decay = jnp.exp(-rate)
    decays = [spread(decay, r) for r in range(MODES)]
    weights = [spread(weight, r) for r in range(MODES)]

    def body(n, states):
        step = STEPS - 1 - n if backward else n
        value = at_step(source, step)
        states = tuple(decays[r] * states[r] + value for r in range(MODES))
        terms = [weights[r] * states[r] for r in range(MODES)]
        while len(terms) > 1:
            terms = [terms[k] + terms[k + 1] for k in range(0, len(terms), 2)]
        target[pl.ds(step, CHUNKS, stride=STEPS), :] = terms[0]
        return states

    lax.fori_loop(0, STEPS, body, tuple(entries), unroll=2)


def add_entry(local, target, rate, weight, entry, backward, inside=None):
    decay = jnp.exp(-rate)
    decays = [spread(decay, r) for r in range(MODES)]
    start = weight * entry
    factor, _ = chunk_weights(powers(rate), not backward)
    parts = [spread(start, r) * factor(r) for r in range(MODES)]
    if inside is not None:
        parts = [parts[r] + spread(weight, r) * inside[r] for r in range(MODES)]

    def body(n, parts):
        step = STEPS - 1 - n if backward else n
        parts = tuple(decays[r] * parts[r] for r in range(MODES))
        terms = list(parts)
        while len(terms) > 1:
            terms = [terms[k] + terms[k + 1] for k in range(0, len(terms), 2)]
        target[pl.ds(step, CHUNKS, stride=STEPS), :] = at_step(local, step) + terms[0]
        return parts

    lax.fori_loop(0, STEPS, body, tuple(parts), unroll=4)


def pair_state(early, late, rate, backward):
    near = jnp.exp(rate * float(-ROWS))
    return early + near * late if backward else near * early + late


def entry_state(gathered, other, rate, me, backward):
    far = jnp.exp(rate * float(-2 * ROWS))
    near = jnp.exp(rate * float(-ROWS))
    pair, second = me // 2, me % 2
    pairs = gathered.shape[0]

    def body(n, state):
        index = pairs - 1 - n if backward else n
        return far * state + gathered[index, 0:MODES, :].astype(F32)

    count = pairs - 1 - pair if backward else pair
    state = lax.fori_loop(0, count, body, jnp.zeros((MODES, LANES), F32))
    outer = second if backward else 1 - second
    return jnp.where(outer == 1, state, near * state + other)


def extend(ext, before, body):
    ext[6:8, :] = before
    ext[8 : 8 + ROWS, :] = body


def three(ext, taps):
    return (
        taps[0:1] * ext[8 : 8 + ROWS, :]
        + taps[1:2] * ext[7 : 7 + ROWS, :]
        + taps[2:3] * ext[6 : 6 + ROWS, :]
    )


def store_tap_sums(target, row, grad, ext):
    for shift in range(3):
        target[row + shift : row + shift + 1, :] = jnp.sum(
            grad * ext[8 - shift : 8 - shift + ROWS, :], 0, keepdims=True
        )


def tail_kernel(med, ends, taps, out, ext, rows):
    feats = []
    for j in (1, 2):
        extend(ext, jnp.zeros((2, LANES), F32), f32_of(med[j]))
        feats.append(rounded(three(ext, taps[j])))
    out[0:TAPS, :] = (feats[0][TAPS:] * feats[1][TAPS:]).astype(BF16)
    rows[...] = jnp.zeros(rows.shape, F32)
    for j in range(3):
        ext[8 : 8 + ROWS, :] = f32_of(med[j])
        rows[2 * j : 2 * j + 2, :] = ext[6 + ROWS : 8 + ROWS, :]
    rows[6:10, :] = ends[...]
    out[TAPS:HALO, :] = rows[...].astype(BF16)


def long_kernel(packed, before, lng, taps, cot, rate_out, weight_out, q_out, k_out, g_out, z_out, ends_out, ext, halo, grad, rows):
    both = jnp.transpose(packed[...].reshape(LANES, LANES))
    rate = jnp.exp(both[:MODES])
    rate_out[...] = rate
    weight_out[...] = both[MODES : 2 * MODES] * jnp.sqrt(2.0 * rate)
    halo[...] = f32_of(before[...])
    feats = []
    for j in range(2):
        extend(ext, halo[LONG_END + 2 * j : LONG_END + 2 * j + 2, :], f32_of(lng[j]))
        feats.append(three(ext, taps[j]).astype(BF16))
    q_out[...] = feats[0]
    k_out[...] = feats[1]
    sent = (f32_of(cot[...]) * f32_of(feats[0])).astype(BF16)
    g_out[...] = sent
    grad[...] = f32_of(sent)
    states = chunk_states(grad, rate, True)
    factor, _ = chunk_weights(powers(rate), True)
    for r in range(MODES):
        ends_out[r] = states[r]
        rows[r : r + 1, :] = jnp.sum(factor(r) * states[r], 0, keepdims=True)
    z_out[...] = rows[...].astype(BF16)


def join_kernel(me, own, other, rate, slot_out):
    first = me[0] % 2 == 0
    mine, theirs = f32_of(own[...]), f32_of(other[...])
    early, late = jnp.where(first, mine, theirs), jnp.where(first, theirs, mine)
    joined = pair_state(early, late, rate[...], True).astype(BF16)
    slot_out[...] = jnp.broadcast_to(joined[None], slot_out.shape)


def medium_kernel(med, before, taps, filt, forward, top,
                  prod_out, q_out, k_out, v_out, conv_out, gated_out, sq_out, ext, halo):
    halo[...] = f32_of(before[...])
    feats = []
    for j in range(3):
        extend(ext, halo[TAPS + 2 * j : TAPS + 2 * j + 2, :], f32_of(med[j]))
        feats.append(three(ext, taps[j]).astype(BF16))
    query, key, value = feats
    q_out[...] = query
    k_out[...] = key
    v_out[...] = value
    prod_out[0:TAPS, :] = before[0:TAPS, :]
    prod_out[TAPS:, :] = (f32_of(key) * f32_of(value)).astype(BF16)
    windows = jnp.concatenate([prod_out[0 : 2 * TAPS, :], prod_out[TAPS:, :]], 1)
    win = spectrum(forward[...], windows)
    ker = spectrum(forward[:, 0:TAPS], filt[...])
    ker_re, ker_alt, ker_im = split_spectrum(ker)
    ker_re, ker_alt, ker_im = (jnp.concatenate([k, k], 1) for k in (ker_re, ker_alt, ker_im))
    re, im = win[:TAPS], win[TAPS:]
    spec = jnp.concatenate([re * ker_re - im * ker_im, im * ker_alt + re * ker_im], 0)
    answer = from_spectrum(top[...], spec)
    conv = jnp.concatenate([answer[:, :LANES], answer[:, LANES:]], 0)
    conv_out[...] = conv
    gated = f32_of(query) * conv
    gated_out[...] = gated
    part = lax.dot_general(
        jnp.ones((8, LANES), F32), gated * gated, (((1,), (1,)), ((), ())),
        precision=precise, preferred_element_type=F32,
    )

    @pl.when(pl.program_id(0) == 0)
    def _():
        sq_out[...] = jnp.zeros(sq_out.shape, F32)

    sq_out[...] += part


def back_kernel(gconv, rate, weight, ends, y_out, grad):
    grad[...] = f32_of(gconv[...])
    entries = chunk_entries([ends[r] for r in range(MODES)], powers(rate[...]), True)
    local_answer(grad, y_out, rate[...], weight[...], entries, True)


def inner_kernel(me, zg, z_other, rate, weight, y_loc, k_two, gated, gain, square, gp_out, zin_out, in_out, full, total):
    entry = entry_state(zg, f32_of(z_other[...]), rate[...], me[0], True)
    zin_out[...] = entry
    add_entry(y_loc, full, rate[...], weight[...], entry, True)
    sent = full[...].astype(BF16)
    gp_out[...] = sent
    product = f32_of(sent) * f32_of(k_two[...]) * gain[...] * gated[...]
    part = lax.dot_general(
        jnp.ones((8, LANES), F32), product, (((1,), (1,)), ((), ())),
        precision=precise, preferred_element_type=F32,
    )

    @pl.when(pl.program_id(0) == 0)
    def _():
        total[...] = part

    @pl.when(pl.program_id(0) > 0)
    def _():
        total[...] += part

    @pl.when(pl.program_id(0) == pl.num_programs(0) - 1)
    def _():
        for device in range(in_out.shape[0]):
            in_out[device, 0:1, 0:ROWS] = square[0:1, :]
            in_out[device, 0:1, ROWS:] = total[0:1, :]


def norm_kernel(me, sums, gated, conv, q_one, k_one, v_one, k_two, gp, gain, filt, cot, prod, med, lng, before, rate, forward, low,
                x_out, gco_out, gq1_out, gk2_out, e_out, pair_out, keep_out, work, tail, ext, halo, f_out):
    ones = jnp.ones((8, LANES), F32)

    def column(values):
        return lax.dot_general(
            values, ones, (((0,), (0,)), ((), ())), precision=precise, preferred_element_type=F32
        )

    square = column(sums[:, 0, 0:ROWS]) / float(D) + 1e-06
    inner = column(sums[:, 0, ROWS:]) / float(D)
    scale = lax.rsqrt(square)
    gate = gated[...]
    key_two = f32_of(k_two[...])
    normed = rounded(gate * scale * gain[...])
    prod_two = (key_two * normed).astype(BF16)
    x_out[...] = prod_two
    grad_two = f32_of(gp[...])
    grad_k_two = grad_two * normed
    gk2_out[...] = grad_k_two
    grad_normed = grad_two * key_two
    f_out[TAPS:, :] = jnp.zeros((f_out.shape[0] - TAPS, LANES), F32)
    f_out[TAPS : TAPS + 1, :] = jnp.sum(grad_normed * gate * scale, 0, keepdims=True)
    grad_gated = scale * (grad_normed * gain[...] - gate * scale * scale * inner)
    grad_q_one = grad_gated * conv[...]
    gq1_out[...] = grad_q_one
    gco = (grad_gated * f32_of(q_one[...])).astype(BF16)
    gco_out[...] = gco
    e_out[0:TAPS, :] = gco[0:TAPS]
    tail[...] = jnp.zeros(tail.shape, F32)
    tail[0:2, :] = grad_q_one[0:2]
    work[...] = f32_of(gco)
    taps = f32_of(filt[...])
    for shift in range(2):
        head = jnp.sum(taps * work[shift : shift + TAPS, :], 0, keepdims=True)
        tail[2 + shift : 3 + shift, :] = head * f32_of(v_one[0:16, :])[shift : shift + 1]
        tail[4 + shift : 5 + shift, :] = head * f32_of(k_one[0:16, :])[shift : shift + 1]
    tail[6:8, :] = grad_k_two[0:2]
    tail[8:10, :] = f32_of(prod_two)[0:2]
    tail[10:12, :] = f32_of(cot[0:16, :])[0:2]
    e_out[TAPS:HALO, :] = tail[...].astype(BF16)
    halo[...] = f32_of(before[...])
    extend(ext, halo[Q_END : Q_END + 2, :], f32_of(med[0]))
    store_tap_sums(f_out, TAPS + 1, grad_q_one, ext)
    extend(ext, halo[LONG_END + 2 : LONG_END + 4, :], f32_of(lng[1]))
    store_tap_sums(f_out, TAPS + 4, grad_k_two, ext)
    win = spectrum(forward[...], jnp.concatenate([prod[0 : 2 * TAPS, :], prod[TAPS:, :]], 1))
    grd = spectrum(forward[:, TAPS:], jnp.concatenate([gco[0:TAPS], gco[TAPS:]], 1))
    win_re, win_alt, win_im = split_spectrum(win)
    re, im = grd[:TAPS], grd[TAPS:]
    spec = jnp.concatenate([re * win_re + im * win_im, im * win_alt - re * win_im], 0)
    f_out[0:TAPS, :] = from_spectrum(low[...], spec[:, :LANES] + spec[:, LANES:])
    work[...] = f32_of(prod_two)
    states = chunk_states(work, rate[...], False)
    factor, _ = chunk_weights(powers(rate[...]), False)
    for r in range(MODES):
        tail[r : r + 1, :] = jnp.sum(factor(r) * states[r], 0, keepdims=True)
    second = me[0] % 2
    pair_out[0:MODES, :] = tail[...].astype(BF16)
    pair_out[MODES:, :] = f_out[pl.ds(pl.multiple_of(HALF * (1 - second), 16), HALF), :].astype(BF16)
    keep_out[...] = f_out[pl.ds(pl.multiple_of(HALF * second, 16), HALF), :]


def share_kernel(me, pair, got, keep, rate, slot_out, add, slot):
    first = me[0] % 2 == 0
    mine, theirs = f32_of(pair[0:MODES, :]), f32_of(got[0:MODES, :])
    early, late = jnp.where(first, mine, theirs), jnp.where(first, theirs, mine)
    slot[0:MODES, :] = pair_state(early, late, rate[...], False)
    add[HALF:, :] = jnp.zeros((8, add.shape[1]), F32)
    add[0:HALF, :] = keep[...] + f32_of(got[MODES:, :])
    for device in range(slot_out.shape[0]):
        slot[MODES:, :] = add[SHARE * device : SHARE * device + 8, :]
        slot_out[device] = slot[...].astype(BF16)


def behind_kernel(g, rate, ends_out, gs):
    gs[...] = f32_of(g[...])
    decay = jnp.exp(-rate[...])
    first = at_step(gs, 0)
    zero = first - first
    half = MODES // 2
    for base in range(0, MODES, half):
        decays = [spread(decay, base + r) for r in range(half)]

        def behind(n, carry):
            z, q = carry
            grad = at_step(gs, STEPS - 1 - n)
            q = tuple(decays[r] * (q[r] + z[r]) for r in range(half))
            z = tuple(decays[r] * z[r] + grad for r in range(half))
            return z, q

        z, q = lax.fori_loop(0, STEPS, behind, ((zero,) * half,) * 2, unroll=4)
        for r in range(half):
            ends_out[base + r] = z[r]
            ends_out[MODES + base + r] = q[r]


def modes_kernel(x, g, rate, weight, ends, y_out, sums_out, entry_out, xs, gs):
    xs[...] = f32_of(x[...])
    gs[...] = f32_of(g[...])
    rates = rate[...]
    decay = jnp.exp(-rates)
    first = at_step(xs, 0)
    zero = first - first
    half = MODES // 2
    power = powers(rates)
    s_end, q_end, plain, slope = [], [], [], []
    z_end = [ends[r] for r in range(MODES)]
    zq_end = [ends[MODES + r] for r in range(MODES)]
    for base in range(0, MODES, half):
        decays = [spread(decay, base + r) for r in range(half)]
        weights = [spread(weight, base + r) for r in range(half)]

        def ahead(n, carry):
            s, q, p, l = carry
            value, grad = at_step(xs, n), at_step(gs, n)
            q = tuple(decays[r] * (q[r] + s[r]) for r in range(half))
            s = tuple(decays[r] * s[r] + value for r in range(half))
            p = tuple(p[r] + grad * s[r] for r in range(half))
            l = tuple(l[r] + grad * q[r] for r in range(half))
            terms = [weights[r] * s[r] for r in range(half)]
            while len(terms) > 1:
                terms = [terms[k] + terms[k + 1] for k in range(0, len(terms), 2)]
            answer = terms[0] if base == 0 else at_step(y_out, n) + terms[0]
            y_out[pl.ds(n, CHUNKS, stride=STEPS), :] = answer
            return s, q, p, l

        s, q, p, l = lax.fori_loop(0, STEPS, ahead, ((zero,) * half,) * 4, unroll=4)
        s_end += s
        q_end += q
        plain += p
        slope += l
    entries = chunk_entries(s_end, power, False)
    exits = chunk_entries(z_end, power, True)
    back, back_steps = chunk_weights(power, True)
    front, front_steps = chunk_weights(power, False)
    for r in range(MODES):
        a = spread(decay, r)
        a_step = a * spread(power[0], r)
        one = plain[r] + entries[r] * a * z_end[r]
        two = (
            slope[r]
            + float(STEPS) * a_step * entries[r] * exits[r]
            + a * (entries[r] * zq_end[r] + exits[r] * (q_end[r] + s_end[r]))
        )
        back_r, front_r = back(r), front(r)
        rows = (
            one,
            two,
            back_r * z_end[r],
            back_r * (zq_end[r] + back_steps * z_end[r]),
            front_r * (q_end[r] + s_end[r] + front_steps * s_end[r]),
        )
        for kind, value in enumerate(rows):
            place = kind * MODES + r
            sums_out[place : place + 1, :] = jnp.sum(value, 0, keepdims=True)
    for r in range(MODES):
        entry_out[r] = entries[r]


def kernel_spectrum(forward, filt, copies):
    parts = split_spectrum(spectrum(forward[:, 0:TAPS], filt[...]))
    return [jnp.concatenate([part] * copies, 1) if copies > 1 else part for part in parts]


def local_taps(gco, filt, k_one, v_one, med, before, forward, low, grad_out, taps_out, ext, halo):
    second = gco[TAPS:, :]
    pieces = jnp.concatenate(
        [gco[...], jnp.concatenate([second, jnp.zeros(second.shape, BF16)], 0)], 1
    )
    win = spectrum(forward[...], pieces)
    ker_re, ker_alt, ker_im = kernel_spectrum(forward, filt, 2)
    re, im = win[:TAPS], win[TAPS:]
    spec = jnp.concatenate([re * ker_re + im * ker_im, im * ker_alt - re * ker_im], 0)
    answer = from_spectrum(low[...], spec)
    grad_prod = jnp.concatenate([answer[:, :LANES], answer[:, LANES:]], 0)
    grad_out[...] = grad_prod
    halo[...] = f32_of(before[...])
    taps_out[...] = jnp.zeros(taps_out.shape, F32)
    for place, other in enumerate((v_one, k_one)):
        extend(ext, halo[TAPS + 2 + 2 * place : TAPS + 4 + 2 * place, :], f32_of(med[place + 1]))
        store_tap_sums(taps_out, 3 * place, grad_prod * f32_of(other[...]), ext)


def answer_kernel(me, sg, pair, other, rate, weight, y_loc, inside, q_two, cot, sums, zin, lng, before, tap_rows, after, filt, k_one, v_one, med, forward, low,
                  mixed_out, gq2_out, res_out, row_out, exit_out, late_out, ext, halo, full, rows):
    rates = rate[...]
    entry = entry_state(sg, f32_of(other[0:MODES, :]), rates, me[0], False)
    add_entry(y_loc, full, rates, weight[...], entry, False, inside)
    conv = rounded(full[...])
    grad_out = f32_of(cot[...])
    mixed_out[...] = (f32_of(q_two[...]) * conv).astype(BF16)
    grad_q_two = grad_out * conv
    gq2_out[...] = grad_q_two
    decay = jnp.exp(-rates)
    exit_out[...] = jnp.exp(rates * float(-ROWS)) * entry + f32_of(pair[0:MODES, :])
    plain = sums[0:MODES, :] + entry * decay * sums[2 * MODES : 3 * MODES, :]
    slope = (
        sums[MODES : 2 * MODES, :]
        + float(ROWS) * jnp.exp(rates * float(-ROWS - 1)) * entry * zin[...]
        + decay * (entry * sums[3 * MODES : 4 * MODES, :] + zin[...] * sums[4 * MODES :, :])
    )
    res_out[0:MODES, :] = (jnp.sqrt(2.0 * rates) * plain).astype(BF16)
    res_out[MODES:, :] = (weight[...] * (0.5 * plain - rates * slope)).astype(BF16)
    added = f32_of(sg[0])
    for device in range(1, sg.shape[0]):
        added = added + f32_of(sg[device])
    rows[0:8, :] = added[MODES : MODES + 8]
    rows[SHARE : SHARE + 6, :] = tap_rows[0:6, :]
    win = spectrum(forward[:, TAPS:], after[0:TAPS, :])
    ker_re, ker_alt, ker_im = kernel_spectrum(forward, filt, 1)
    re, im = win[:TAPS], win[TAPS:]
    spec = jnp.concatenate([re * ker_re + im * ker_im, im * ker_alt - re * ker_im], 0)
    late = from_spectrum(low[...], spec)
    late_out[...] = late
    for place, other in enumerate((v_one, k_one)):
        ext[0:ROWS, :] = f32_of(med[place + 1])
        grad = late * f32_of(other[TAPS:, :])
        for shift in range(3):
            row = SHARE + 3 * place + shift
            rows[row : row + 1, :] += jnp.sum(grad * ext[TAPS - shift : ROWS - shift, :], 0, keepdims=True)
    halo[...] = f32_of(before[TAPS:HALO, :])
    extend(ext, halo[6:8, :], f32_of(lng[0]))
    store_tap_sums(rows, SHARE + 6, grad_q_two, ext)
    row_out[...] = rows[...].astype(BF16)


def input_kernel(gq1, gpo, late, gq2, gk2, k_one, v_one, after, leave, rate, weight, mtaps, ltaps,
                 med_out, lng_out, ext, tail, nxt):
    tail[...] = f32_of(after[TAPS:HALO, :])
    grad_prod = jnp.concatenate([gpo[0:TAPS, :], gpo[TAPS:, :] + late[...]], 0)
    state = leave[...]
    decay = jnp.exp(-rate[...])
    for step in range(2):
        state = decay * state + tail[8 + step : 9 + step, :]
        value = rounded(jnp.sum(weight[...] * state, 0, keepdims=True))
        nxt[step : step + 1, :] = value * tail[10 + step : 11 + step, :]

    def back(grad, following, taps):
        ext[0:ROWS, :] = grad
        ext[ROWS : ROWS + 2, :] = following
        return (
            taps[0:1] * ext[0:ROWS, :] + taps[1:2] * ext[1 : ROWS + 1, :] + taps[2:3] * ext[2 : ROWS + 2, :]
        ).astype(BF16)

    med_out[0] = back(gq1[...], tail[0:2, :], mtaps[0])
    med_out[1] = back(grad_prod * f32_of(v_one[...]), tail[2:4, :], mtaps[1])
    med_out[2] = back(grad_prod * f32_of(k_one[...]), tail[4:6, :], mtaps[2])
    lng_out[0] = back(gq2[...], nxt[0:2, :], ltaps[0])
    lng_out[1] = back(gk2[...], tail[6:8, :], ltaps[1])


def finish_kernel(last, mtap_out, ltap_out, filt_out, gain_out, res_out, log_out, f_all):
    added = jnp.zeros((last.shape[1], LANES), F32)
    for place in range(last.shape[0]):
        second, pair = place // PAIRS, place % PAIRS
        piece = f32_of(last[2 * pair + second])
        f_all[SHARE * place : SHARE * place + 8, :] = piece[0:8]
        added = added + piece
    filt_out[...] = f_all[0:TAPS, :]
    gain_out[...] = f_all[TAPS : TAPS + 1, :]
    for shift in range(3):
        mtap_out[shift, 0:1, :] = f_all[TAPS + 1 + shift : TAPS + 2 + shift, :]
        ltap_out[shift, 1:2, :] = f_all[TAPS + 4 + shift : TAPS + 5 + shift, :]
        mtap_out[shift, 1:2, :] = added[SHARE + shift : SHARE + 1 + shift]
        mtap_out[shift, 2:3, :] = added[SHARE + 3 + shift : SHARE + 4 + shift]
        ltap_out[shift, 0:1, :] = added[SHARE + 6 + shift : SHARE + 7 + shift]
    block = pl.program_id(0)
    lane = lax.broadcasted_iota(jnp.int32, (MODES, LANES), 1)
    row = lax.broadcasted_iota(jnp.int32, (MODES, LANES), 0)
    picked = jnp.where(lane % MODES == row, added[SHARE + 9 : SHARE + 10], 0.0)
    goal = (row == lane // MODES + 8 * (block % 2)).astype(F32)
    part = lax.dot_general(
        picked, goal, (((1,), (1,)), ((), ())), precision=precise, preferred_element_type=F32
    )

    @pl.when(block == 0)
    def _():
        res_out[...] = part

    @pl.when(block == 1)
    def _():
        res_out[...] += part

    @pl.when(block == 2)
    def _():
        log_out[...] = part

    @pl.when(block == 3)
    def _():
        log_out[...] += part


def block_of(shape, kind, lanes):
    if kind == "lane":
        lead = shape[:-1]
        return pl.BlockSpec(lead + (lanes,), lambda l: (0,) * len(lead) + (l,))
    if kind == "whole":
        return pl.BlockSpec(shape, lambda l: (0,) * len(shape))
    if kind == "source":
        return pl.BlockSpec((8,) + shape[1:], lambda l: (l,) + (0,) * (len(shape) - 1))
    return pl.BlockSpec(memory_space=pltpu.SMEM)


def run(kernel, name, width, inputs, outputs, scratch, limit=63, flops=1000000, lanes=LANES):
    arrays = [array for array, _ in inputs]
    moved = sum(a.size * a.dtype.itemsize for a in arrays)
    return pl.pallas_call(
        kernel,
        grid=(width // lanes,),
        in_specs=[block_of(a.shape, kind, lanes) for a, kind in inputs],
        out_specs=[block_of(shape, kind, lanes) for shape, _, kind in outputs],
        out_shape=[
            jax.ShapeDtypeStruct(shape, dtype) for shape, dtype, _ in outputs
        ],
        scratch_shapes=[pltpu.VMEM(shape, F32) for shape in scratch],
        compiler_params=pltpu.CompilerParams(vmem_limit_bytes=limit * 1024 * 1024),
        cost_estimate=pl.CostEstimate(flops=flops, bytes_accessed=moved, transcendentals=0),
        name=name,
    )(*arrays)


def passed_along(array, axis, by):
    count = lax.axis_size(axis)
    pairs = [(i, i + by) for i in range(count) if 0 <= i + by < count]
    return lax.ppermute(array, axis, pairs)


def exchanged(array):
    return lax.ppermute(array, "ctx", [(i, i ^ 1) for i in range(lax.axis_size("ctx"))])


def in_plane(array):
    groups = [[2 * p + z for p in range(PAIRS)] for z in range(2)]
    return lax.all_to_all(array, "ctx", split_axis=0, concat_axis=0, tiled=True, axis_index_groups=groups)


def swap(array, axis):
    return lax.all_to_all(array, axis, split_axis=0, concat_axis=0, tiled=True)


def on_device(medium_input, long_input, medium_taps, long_taps, medium_filter, norm_gain, long_residue, long_log_decay, cotangent):
    width = cotangent.shape[1]
    count = lax.axis_size("ctx")
    me = lax.axis_index("ctx").astype(jnp.int32).reshape(1)
    forward, low, top = (jnp.asarray(table) for table in fourier_matrices())
    med = jnp.transpose(medium_input, (1, 0, 2))
    lng = jnp.transpose(long_input, (1, 0, 2))
    mtaps = jnp.transpose(medium_taps, (1, 0, 2))
    ltaps = jnp.transpose(long_taps, (1, 0, 2))
    gain = norm_gain.reshape(1, width)
    filt = medium_filter
    ext = (ROWS + 8, LANES)
    halo = (HALO, LANES)
    wide = (WIDE, width)
    full = (ROWS, LANES)
    rows = (MODES, LANES)
    plane = (ROWS, width)
    modes = (MODES, width)

    mine = jnp.pad(jnp.concatenate([long_log_decay, long_residue], 1), ((0, 0), (0, LANES - 2 * MODES)))
    packed = swap(jnp.broadcast_to(mine[None], (count,) + mine.shape), "ctx")

    ends = jnp.transpose(long_input[ROWS - 2 :].astype(F32), (1, 0, 2)).reshape(4, width)
    (tail,) = run(
        tail_kernel, "tail", width, [(med, "lane"), (ends, "lane"), (mtaps, "lane")],
        [((HALO, width), BF16, "lane")], [ext, rows], limit=16,
    )
    before = passed_along(tail, "ctx", 1)

    rate, weight, q_two, k_two, gconv, z_all, z_ends = run(
        long_kernel, "long", width,
        [(packed, "source"), (before, "lane"), (lng, "lane"), (ltaps, "lane"), (cotangent, "lane")],
        [(modes, F32, "lane"), (modes, F32, "lane"), (plane, BF16, "lane"), (plane, BF16, "lane"), (plane, BF16, "lane"), (modes, BF16, "lane"), ((MODES, CHUNKS, width), F32, "lane")],
        [ext, halo, full, rows],
    )
    z_other = exchanged(z_all)
    prod, q_one, k_one, v_one, conv, gated, square = run(
        medium_kernel, "medium", width,
        [(med, "lane"), (before, "lane"), (mtaps, "lane"), (filt, "lane"), (forward, "whole"), (top, "whole")],
        [(wide, BF16, "lane"), (plane, BF16, "lane"), (plane, BF16, "lane"), (plane, BF16, "lane"), (plane, F32, "lane"), (plane, F32, "lane"), ((8, ROWS), F32, "whole")],
        [ext, halo],
    )
    z_other, square = lax.optimization_barrier((z_other, square))
    (z_pairs,) = run(
        join_kernel, "join", width, [(me, "scalar"), (z_all, "lane"), (z_other, "lane"), (rate, "lane")],
        [((PAIRS,) + modes, BF16, "lane")], [], lanes=width,
    )
    zg = in_plane(z_pairs)
    (y_back,) = run(
        back_kernel, "back", width,
        [(gconv, "lane"), (rate, "lane"), (weight, "lane"), (z_ends, "lane")],
        [(plane, F32, "lane")], [full],
    )
    grad_prod, zin, inner = run(
        inner_kernel, "inner", width,
        [(me, "scalar"), (zg, "lane"), (z_other, "lane"), (rate, "lane"), (weight, "lane"), (y_back, "lane"), (k_two, "lane"), (gated, "lane"), (gain, "lane"), (square, "whole")],
        [(plane, BF16, "lane"), (modes, F32, "lane"), ((8, 1, 2 * ROWS), F32, "whole")],
        [full, (8, ROWS)],
    )
    sums = swap(inner, "tp")
    later, _ = lax.optimization_barrier((gconv, inner))
    (ends_back,) = run(
        behind_kernel, "behind", width, [(later, "lane"), (rate, "lane")],
        [((2 * MODES, CHUNKS, width), F32, "lane")], [full],
    )
    sums, ends_back = lax.optimization_barrier((sums, ends_back))

    x, gco, gq1, gk2, edge, pair, keep = run(
        norm_kernel, "norm", width,
        [(me, "scalar"), (sums, "whole"), (gated, "lane"), (conv, "lane"), (q_one, "lane"), (k_one, "lane"), (v_one, "lane"), (k_two, "lane"), (grad_prod, "lane"), (gain, "lane"), (filt, "lane"), (cotangent, "lane"), (prod, "lane"), (med, "lane"), (lng, "lane"), (before, "lane"), (rate, "lane"), (forward, "whole"), (low, "whole")],
        [(plane, BF16, "lane"), (plane, BF16, "lane"), (plane, F32, "lane"), (plane, F32, "lane"), ((HALO, width), BF16, "lane"), ((MODES + HALF, width), BF16, "lane"), ((HALF, width), F32, "lane")],
        [full, rows, ext, halo, (2 * HALF, LANES)],
    )
    after = passed_along(edge, "ctx", -1)
    other = exchanged(pair)
    gpo, tap_rows = run(
        local_taps, "taps", width,
        [(gco, "lane"), (filt, "lane"), (k_one, "lane"), (v_one, "lane"), (med, "lane"), (before, "lane"), (forward, "whole"), (low, "whole")],
        [(plane, F32, "lane"), ((8, width), F32, "lane")], [ext, halo],
    )
    other, after, tap_rows = lax.optimization_barrier((other, after, tap_rows))
    (sent,) = run(
        share_kernel, "share", width,
        [(me, "scalar"), (pair, "lane"), (other, "lane"), (keep, "lane"), (rate, "lane")],
        [((PAIRS, MODES + 8, width), BF16, "lane")], [(HALF + 8, width), (MODES + 8, width)], lanes=width,
    )
    got = in_plane(sent)

    y_front, mode_sums, inside = run(
        modes_kernel, "modes", width,
        [(x, "lane"), (gconv, "lane"), (rate, "lane"), (weight, "lane"), (ends_back, "lane")],
        [(plane, F32, "lane"), ((5 * MODES, width), F32, "lane"), ((MODES, CHUNKS, width), F32, "lane")], [full, full],
    )
    mixed, gq2, res, every, leave, late = run(
        answer_kernel, "answer", width,
        [(me, "scalar"), (got, "lane"), (pair, "lane"), (other, "lane"), (rate, "lane"), (weight, "lane"), (y_front, "lane"), (inside, "lane"), (q_two, "lane"), (cotangent, "lane"), (mode_sums, "lane"), (zin, "lane"), (lng, "lane"), (before, "lane"), (tap_rows, "lane"), (after, "lane"), (filt, "lane"), (k_one, "lane"), (v_one, "lane"), (med, "lane"), (forward, "whole"), (low, "whole")],
        [(plane, BF16, "lane"), (plane, F32, "lane"), ((2 * MODES, width), BF16, "lane"), ((MODES, width), BF16, "lane"), (modes, F32, "lane"), ((TAPS, width), F32, "lane")],
        [ext, rows, full, rows],
    )
    every = jnp.broadcast_to(every[None, : SHARE + 9], (count, SHARE + 9, width))
    own = res.reshape(2 * MODES, count, MODES).transpose(1, 0, 2).reshape(count, 1, width)
    last = swap(jnp.concatenate([every, own], 1), "ctx")

    grad_med, grad_lng = run(
        input_kernel, "inputs", width,
        [(gq1, "lane"), (gpo, "lane"), (late, "lane"), (gq2, "lane"), (gk2, "lane"), (k_one, "lane"), (v_one, "lane"), (after, "lane"), (leave, "lane"), (rate, "lane"), (weight, "lane"), (mtaps, "lane"), (ltaps, "lane")],
        [((3, ROWS, width), BF16, "lane"), ((2, ROWS, width), BF16, "lane")],
        [ext, rows, (8, LANES)],
    )
    taps_medium, taps_long, grad_filter, gain_total, grad_residue, grad_log = run(
        finish_kernel, "finish", width, [(last, "lane")],
        [((3, 3, width), F32, "lane"), ((3, 2, width), F32, "lane"), ((TAPS, width), F32, "lane"), ((1, width), F32, "lane"), ((MODES, MODES), F32, "whole"), ((MODES, MODES), F32, "whole")],
        [(SHARE * count + 8, LANES)], limit=16,
    )
    return (
        mixed,
        jnp.transpose(grad_med, (1, 0, 2)),
        jnp.transpose(grad_lng, (1, 0, 2)),
        taps_medium,
        taps_long,
        grad_filter,
        gain_total.reshape(width),
        grad_residue,
        grad_log,
    )


def solution(mesh):
    return jax.shard_map(
        on_device,
        mesh=mesh,
        in_specs=(
            P("ctx", None, "tp"),
            P("ctx", None, "tp"),
            P(None, None, "tp"),
            P(None, None, "tp"),
            P(None, "tp"),
            P("tp"),
            P(("tp", "ctx"), None),
            P(("tp", "ctx"), None),
            P("ctx", "tp"),
        ),
        out_specs=(
            P("ctx", "tp"),
            P("ctx", None, "tp"),
            P("ctx", None, "tp"),
            P(None, None, "tp"),
            P(None, None, "tp"),
            P(None, "tp"),
            P("tp"),
            P(("tp", "ctx"), None),
            P(("tp", "ctx"), None),
        ),
        check_vma=False,
    )
```

time: 172 us -> 160 us (0.930)
  waiting for transfers between devices: 43.8 us -> 35.3 us
  starting transfers between devices: 43.5 us -> 51 us
  blocking collectives: 7.27 us -> 0 us
  other arithmetic: 4.37 us -> 2.51 us
    ppermute x2, waiting for transfers between devices: 20.7 us -> 4.14 us  [passed_along(): return lax.ppermute(array, axis, pairs)]
    all_to_all x4 -> x3, starting transfers between devices: 34.6 us -> 25.4 us  [swap(): return lax.all_to_all(array, axis, split_axis=0, concat_axis=0, tiled=True)]
    all_to_all x0 -> x2, starting transfers between devices: none -> 8.93 us  [in_plane(): lax.all_to_all(array, 'ctx', split_axis=0, concat_axis=0, tiled=True, axi...]
    ppermute x0 -> x2, waiting for transfers between devices: none -> 8.26 us  [exchanged(): lax.ppermute(array, 'ctx', [(i, i ^ 1) for i in range(lax.axis_size('ctx'...]
    ppermute x0 -> x2, starting transfers between devices: none -> 7.65 us  [exchanged(): lax.ppermute(array, 'ctx', [(i, i ^ 1) for i in range(lax.axis_size('ctx'...]
    all_to_all x1 -> x0, blocking collectives: 7.27 us -> none  [swap(): return lax.all_to_all(array, axis, split_axis=0, concat_axis=0, tiled=True)]
    all_to_all x4 -> x3, waiting for transfers between devices: 23.1 us -> 17 us  [swap(): return lax.all_to_all(array, axis, split_axis=0, concat_axis=0, tiled=True)]
    all_to_all x0 -> x2, waiting for transfers between devices: none -> 5.87 us  [in_plane(): lax.all_to_all(array, 'ctx', split_axis=0, concat_axis=0, tiled=True, axi...]
  transfers between devices with their start and end apart: 6 -> 9, of which waited for: 5 -> 7; matrix products, arithmetic and copies ran while one was open for 3% -> 3% of each run, Pallas kernels for 17% -> 20%
where the time goes in v2:
time: 160 us; the launch traced here: 158 us
  Pallas kernels  58 us (36%)
  starting transfers between devices  51 us (32%)
  waiting for transfers between devices  35.3 us (22%)
  local copies, waits for them, and re-layouts  10.5 us (7%)
  other arithmetic  2.51 us (2%)
    pallas_call x14, Pallas kernels, run(): pl.pallas_call(kernel, grid=(width // lanes,), in_specs=[block_of(a.shape...  58 us
    all_to_all x3, starting transfers between devices, swap(): return lax.all_to_all(array, axis, split_axis=0, concat_axis=0, tiled=True)  25.4 us
    all_to_all x3, waiting for transfers between devices, swap(): return lax.all_to_all(array, axis, split_axis=0, concat_axis=0, tiled=True)  17 us
    ppermute x2, starting transfers between devices, passed_along(): return lax.ppermute(array, axis, pairs)  9.02 us
    all_to_all x2, starting transfers between devices, in_plane(): lax.all_to_all(array, 'ctx', split_axis=0, concat_axis=0, tiled=True, axi...  8.93 us
    unnamed x32, local copies, waits for them, and re-layouts  8.49 us
    ppermute x2, waiting for transfers between devices, exchanged(): lax.ppermute(array, 'ctx', [(i, i ^ 1) for i in range(lax.axis_size('ctx'...  8.26 us
    ppermute x2, starting transfers between devices, exchanged(): lax.ppermute(array, 'ctx', [(i, i ^ 1) for i in range(lax.axis_size('ctx'...  7.65 us
  transfers between devices with their start and end apart: 9, of which 7 were waited for; matrix products, arithmetic and copies ran while one was open for 3% of the time, Pallas kernels for 20%

profile of v2, /device:TPU:64, one launch (start us, length us, event | category | flops | bytes accessed | tf_op | source)
XLA Modules:
  0.0 158.1 jit_solution(501081342821112525)
XLA Ops:
  0.7 0.9 select_maximum_fusion
  1.5 0.7 broadcast_in_dim.4
  2.2 12.1 %all-to-all-start = ((f32[32,16,128]{2,1,0:T(8,128)}), f32[32,16,128]{2,1,0:T(8,128)S(1)}, u32[]{:S(2)}, u32[]{:S(2)}) async-start(f32[32,16,128]{2,1,0:T(8,128)} %broadcast_in_dim.4), calls=%async_computation | async-start | bytes 524288 | tf_op jit(solution)/shard_map/all_to_all | solution.py:658
  14.4 0.7 convert_bitcast_fusion
  15.2 0.5 tail.1
  15.7 0.1 copy-done.1
  15.8 7.7 %collective-permute-start = (bf16[144,512]{1,0:T(8,128)(2,1)S(1)}, bf16[144,512]{1,0:T(8,128)(2,1)S(1)}, u32[]{:S(2)}, u32[]{:S(2)}) collective-permute-start(bf16[144,512]{1,0:T(8,128)(2,1)S(1)} %tail.1), channel_id=1, source_target_pairs={{0,8},{8,16},{16,24},{24,32},{32,40},{40,48},{48,56},{56,64},{64,7... | collective-permute-start | bytes 442376 | tf_op jit(solution)/shard_map/ppermute | solution.py:645
  23.5 0.8 copy.38
  24.4 0.6 copy.40
  25.0 4.1 %collective-permute-done.before = bf16[144,512]{1,0:T(8,128)(2,1)S(1)} collective-permute-done((bf16[144,512]{1,0:T(8,128)(2,1)S(1)}, bf16[144,512]{1,0:T(8,128)(2,1)S(1)}, u32[]{:S(2)}, u32[]{:S(2)}) %collective-permute-start) | collective-permute-done | bytes 147488 | tf_op jit(solution)/shard_map/ppermute | solution.py:645
  29.1 5.5 %all-to-all-done.packed = f32[32,16,128]{2,1,0:T(8,128)S(1)} async-done(((f32[32,16,128]{2,1,0:T(8,128)}), f32[32,16,128]{2,1,0:T(8,128)S(1)}, u32[]{:S(2)}, u32[]{:S(2)}) %all-to-all-start) | async-done | bytes 262176 | tf_op jit(solution)/shard_map/all_to_all | solution.py:658
  34.6 0.7 copy-done.4
  35.3 4.2 %long.1 = (f32[16,512]{1,0:T(8,128)}, f32[16,512]{1,0:T(8,128)}, bf16[256,512]{1,0:T(8,128)(2,1)}, bf16[256,512]{1,0:T(8,128)(2,1)}, bf16[256,512]{1,0:T(8,128)(...) custom-call(f32[32,16,128]{2,1,0:T(8,128)} %copy-done.4, bf16[144,512]{1,0:T(8,128)(2,1)} %copy-done.2, ...), custom_call_target="tpu_custom_call" | custom-call | flops 1000000 | bytes 1208320 | tf_op jit(solution)/shard_map/long/pallas_call | solution.py:627
  39.5 1.0 collective-permute-start.1
  40.5 5.6 %medium.1 = (bf16[384,512]{1,0:T(8,128)(2,1)}, bf16[256,512]{1,0:T(8,128)(2,1)}, bf16[256,512]{1,0:T(8,128)(2,1)}, bf16[256,512]{1,0:T(8,128)(2,1)}, f32[256,512...) custom-call(bf16[3,256,512]{2,1,0:T(8,128)(2,1)} %bitcast.22, bf16[144,512]{1,0:T(8,128)(2,1)} %copy-done.2, ...), custom_call_target="tpu_custom_call" | custom-call | flops 1000000 | bytes 1280000 | tf_op jit(solution)/shard_map/medium/pallas_call | solution.py:627
  46.1 1.4 collective-permute-done.1.other.z_other
  47.4 0.6 copy-done.9
  48.0 1.5 join.1
  49.6 5.4 %all-to-all-start.1 = ((bf16[16,16,512]{2,1,0:T(8,128)(2,1)}), bf16[16,16,512]{2,1,0:T(8,128)(2,1)S(1)}, u32[]{:S(2)}, u32[]{:S(2)}) async-start(bf16[16,16,512]{2,1,0:T(8,128)(2,1)} %join.1), calls=%async_computation.1 | async-start | bytes 524288 | tf_op jit(solution)/shard_map/all_to_all | solution.py:654
  54.9 4.3 %back.1.y_loc = f32[256,512]{1,0:T(8,128)} custom-call(bf16[256,512]{1,0:T(8,128)(2,1)} %get-tuple-element.71.gconv.g, f32[16,512]{1,0:T(8,128)} %get-tuple-element.63.rate, f32[16,512]{1,0:T(8,128)} %get-tuple-element.64.weight, f32[16,8,512]{2,1,0:T(8,128)} %get-tuple-element.66.ends), custom_call_target="tpu_custom_call" | custom-call | flops 1000000 | bytes 589824 | tf_op jit(solution)/shard_map/back/pallas_call | solution.py:627
  59.3 4.1 %all-to-all-done.1.zg = bf16[16,16,512]{2,1,0:T(8,128)(2,1)S(1)} async-done(((bf16[16,16,512]{2,1,0:T(8,128)(2,1)}), bf16[16,16,512]{2,1,0:T(8,128)(2,1)S(1)}, u32[]{:S(2)}, u32[]{:S(2)}) %all-to-all-start.1) | async-done | bytes 262176 | tf_op jit(solution)/shard_map/all_to_all | solution.py:654
  63.4 0.7 copy-done.5
  64.1 4.7 %inner.1 = (bf16[256,512]{1,0:T(8,128)(2,1)}, f32[16,512]{1,0:T(8,128)}, f32[8,1,512]{2,1,0:T(1,128)}) custom-call(s32[1]{0:T(128)} %bitcast.me, bf16[16,16,512]{2,1,0:T(8,128)(2,1)} %copy-done.5, bf16[16,512]{1,0:T(8,128)(2,1)} %copy-done.9, f32[16,512]{1,0:T(8,128)} %get-tuple-element.63.rate, f32[16,512]{1,0:T(8,128)} %get-tuple-element.64.weight, ...), custom_call_target="tpu_custom_call" | custom-call | flops 1000000 | bytes 1665028 | tf_op jit(solution)/shard_map/inner/pallas_call | solution.py:627
  68.8 5.1 %all-to-all-start.2 = ((f32[8,1,512]{2,1,0:T(1,128)}), f32[8,1,512]{2,1,0:T(1,128)S(1)}, u32[]{:S(2)}, u32[]{:S(2)}) async-start(f32[8,1,512]{2,1,0:T(1,128)} %get-tuple-element.70), calls=%async_computation.2 | async-start | bytes 32768 | tf_op jit(solution)/shard_map/all_to_all | solution.py:658
  73.9 4.0 %behind.1.ends = f32[32,8,512]{2,1,0:T(8,128)} custom-call(bf16[256,512]{1,0:T(8,128)(2,1)} %get-tuple-element.71.gconv.g, f32[16,512]{1,0:T(8,128)} %get-tuple-element.63.rate), custom_call_target="tpu_custom_call" | custom-call | flops 1000000 | bytes 294912 | tf_op jit(solution)/shard_map/behind/pallas_call | solution.py:627
  77.9 0.6 copy-done.10
  78.5 7.4 %norm.1 = (bf16[256,512]{1,0:T(8,128)(2,1)}, bf16[256,512]{1,0:T(8,128)(2,1)}, f32[256,512]{1,0:T(8,128)}, f32[256,512]{1,0:T(8,128)}, bf16[144,512]{1,0:T(8,128...) custom-call(s32[1]{0:T(128)} %bitcast.me, f32[8,1,512]{2,1,0:T(1,128)} %copy-done.10, ...), custom_call_target="tpu_custom_call" | custom-call | flops 1000000 | bytes 4851716 | tf_op jit(solution)/shard_map/norm/pallas_call | solution.py:627
  85.9 1.3 collective-permute-start.3
  87.2 6.6 %collective-permute-start.2 = (bf16[96,512]{1,0:T(8,128)(2,1)}, bf16[96,512]{1,0:T(8,128)(2,1)S(1)}, u32[]{:S(2)}, u32[]{:S(2)}) collective-permute-start(bf16[96,512]{1,0:T(8,128)(2,1)} %get-tuple-element.79.pair), channel_id=1, source_target_pairs={{0,8},{8,0},{16,24},{24,16},{32,40},{40,32},{48,56},{56,48},{64,72... | collective-permute-start | bytes 294920 | tf_op jit(solution)/shard_map/ppermute | solution.py:649
  93.9 4.4 %taps.1 = (f32[256,512]{1,0:T(8,128)}, f32[8,512]{1,0:T(8,128)}) custom-call(bf16[256,512]{1,0:T(8,128)(2,1)} %get-tuple-element.81.gco, bf16[128,512]{1,0:T(8,128)(2,1)} %filt.7, bf16[256,512]{1,0:T(8,128)(2,1)} %get-tuple-element.75.k_one, bf16[256,512]{1,0:T(8,128)(2,1)} %get-tuple-element.76.v_one, bf16[3,256,512]{2,1,0:T(8,128)(2,1)} %bitcast.24, ...), custom_call_target="tpu_custom_call" | custom-call | flops 1000000 | bytes 2048000 | tf_op jit(solution)/shard_map/taps/pallas_call | solution.py:627
  98.3 6.9 %collective-permute-done.2.got.other = bf16[96,512]{1,0:T(8,128)(2,1)S(1)} collective-permute-done((bf16[96,512]{1,0:T(8,128)(2,1)}, bf16[96,512]{1,0:T(8,128)(2,1)S(1)}, u32[]{:S(2)}, u32[]{:S(2)}) %collective-permute-start.2) | collective-permute-done | bytes 98336 | tf_op jit(solution)/shard_map/ppermute | solution.py:649
  105.2 0.6 copy-done.8
  105.8 1.8 %share.1 = bf16[16,24,512]{2,1,0:T(8,128)(2,1)} custom-call(s32[1]{0:T(128)} %bitcast.me, bf16[96,512]{1,0:T(8,128)(2,1)} %get-tuple-element.79.pair, bf16[96,512]{1,0:T(8,128)(2,1)} %copy-done.8, f32[80,512]{1,0:T(8,128)} %get-tuple-element.84.keep, f32[16,512]{1,0:T(8,128)} %get-tuple-element.63.rate), custom_call_target="tpu_custom_call" | custom-call | flops 1000000 | bytes 393220 | tf_op jit(solution)/shard_map/share/pallas_call | solution.py:627
  107.7 3.6 %all-to-all-start.3 = ((bf16[16,24,512]{2,1,0:T(8,128)(2,1)}), bf16[16,24,512]{2,1,0:T(8,128)(2,1)S(1)}, u32[]{:S(2)}, u32[]{:S(2)}) async-start(bf16[16,24,512]{2,1,0:T(8,128)(2,1)} %share.1), calls=%async_computation.3 | async-start | bytes 786432 | tf_op jit(solution)/shard_map/all_to_all | solution.py:654
  111.3 7.8 %modes.1 = (f32[256,512]{1,0:T(8,128)}, f32[80,512]{1,0:T(8,128)}, f32[16,8,512]{2,1,0:T(8,128)}) custom-call(bf16[256,512]{1,0:T(8,128)(2,1)} %get-tuple-element.85.x, bf16[256,512]{1,0:T(8,128)(2,1)} %get-tuple-element.71.gconv.g, f32[16,512]{1,0:T(8,128)} %get-tuple-element.63.rate, f32[16,512]{1,0:T(8,128)} %get-tuple-element.64.weight, ...), custom_call_target="tpu_custom_call" | custom-call | flops 1000000 | bytes 1114112 | tf_op jit(solution)/shard_map/modes/pallas_call | solution.py:627
  119.1 1.7 %all-to-all-done.3.sg = bf16[16,24,512]{2,1,0:T(8,128)(2,1)S(1)} async-done(((bf16[16,24,512]{2,1,0:T(8,128)(2,1)}), bf16[16,24,512]{2,1,0:T(8,128)(2,1)S(1)}, u32[]{:S(2)}, u32[]{:S(2)}) %all-to-all-start.3) | async-done | bytes 393248 | tf_op jit(solution)/shard_map/all_to_all | solution.py:654
  120.8 0.7 copy-done.3
  121.5 5.6 %answer.1 = (bf16[256,512]{1,0:T(8,128)(2,1)}, f32[256,512]{1,0:T(8,128)}, bf16[32,512]{1,0:T(8,128)(2,1)}, bf16[16,512]{1,0:T(8,128)(2,1)}, f32[16,512]{1,0:T(8,128)}, /*index=5*/f32[128,512]{1,0:T(8,128)}) custom-call(s32[1]{0:T(128)} %bitcast.me, bf16[16,24,512]{2,1,0:T(8,128)(2,1)} %copy-done.3, bf16[96,512]{1,0:T(8,128)(2,1)} %get-tuple-element.79.pair, ...), custom_call_target="tpu_custom_call" | custom-call | flops 1000000 | bytes 4636676 | tf_op jit(solution)/shard_map/answer/pallas_call | solution.py:627
  127.1 0.9 copy.31
  128.0 0.2 copy.32
  128.2 0.1 copy.33
  128.4 0.6 copy-done.12
  129.0 0.9 pad_maximum_fusion
  129.9 8.1 %all-to-all-start.4 = ((bf16[32,15,512]{2,1,0:T(8,128)(2,1)}), bf16[32,15,512]{2,1,0:T(8,128)(2,1)S(1)}, u32[]{:S(2)}, u32[]{:S(2)}) async-start(bf16[32,15,512]{2,1,0:T(8,128)(2,1)} %pad_maximum_fusion), calls=%async_computation.4 | async-start | bytes 1048576 | tf_op jit(solution)/shard_map/all_to_all | solution.py:658
  138.1 4.3 %inputs.1 = (bf16[3,256,512]{2,1,0:T(8,128)(2,1)}, bf16[2,256,512]{2,1,0:T(8,128)(2,1)}) custom-call(f32[256,512]{1,0:T(8,128)} %get-tuple-element.95.gq1, f32[256,512]{1,0:T(8,128)} %get-tuple-element.96.gpo, f32[128,512]{1,0:T(8,128)} %get-tuple-element.97.late, f32[256,512]{1,0:T(8,128)} %get-tuple-element.98.gq2, f32[256,512]{1,0:T(8,128)} %get-tuple-element.99.gk2, ...), custom_call_target="tpu_custom_call" | custom-call | flops 1000000 | bytes 3160064 | tf_op jit(solution)/shard_map/inputs/pallas_call | solution.py:627
  142.4 2.4 %copy.34 = bf16[256,2,512]{2,1,0:T(2,128)(2,1)} copy(bf16[256,2,512]{2,0,1:T(8,128)(2,1)} %bitcast.34) | data formatting | bytes 1048576
  144.7 11.5 %all-to-all-done.4.last = bf16[32,15,512]{2,1,0:T(8,128)(2,1)S(1)} async-done(((bf16[32,15,512]{2,1,0:T(8,128)(2,1)}), bf16[32,15,512]{2,1,0:T(8,128)(2,1)S(1)}, u32[]{:S(2)}, u32[]{:S(2)}) %all-to-all-start.4) | async-done | bytes 491552 | tf_op jit(solution)/shard_map/all_to_all | solution.py:658
  156.2 1.9 %finish.1 = (f32[3,3,512]{2,1,0:T(4,128)}, f32[3,2,512]{2,1,0:T(2,128)}, f32[128,512]{1,0:T(8,128)}, f32[1,512]{1,0:T(1,128)}, f32[16,16]{1,0:T(8,128)}, /*index=5*/f32[16,16]{1,0:T(8,128)}) custom-call(bf16[32,15,512]{2,1,0:T(8,128)(2,1)S(1)} %all-to-all-done.4.last), custom_call_target="tpu_custom_call" | custom-call | flops 1000000 | bytes 491520 | tf_op jit(solution)/shard_map/finish/pallas_call | solution.py:627
  (26 shorter events, 0.1 us)
Async XLA Ops:
  0.6 14.5 %copy-start = (bf16[256,3,512]{2,0,1:T(8,128)(2,1)S(1)}, bf16[256,3,512]{2,0,1:T(8,128)(2,1)}, u32[]{:S(2)}) copy-start(bf16[256,3,512]{2,0,1:T(8,128)(2,1)} %param.12) | copy-start | bytes 2359300
  2.2 32.4 %all-to-all-start = ((f32[32,16,128]{2,1,0:T(8,128)}), f32[32,16,128]{2,1,0:T(8,128)S(1)}, u32[]{:S(2)}, u32[]{:S(2)}) async-start(f32[32,16,128]{2,1,0:T(8,128)} %broadcast_in_dim.4), calls=%async_computation | async-start | bytes 524288 | tf_op jit(solution)/shard_map/all_to_all | solution.py:658
  14.4 0.7 copy-start.11
  15.1 8.4 %copy-start.7 = (bf16[256,2,512]{2,1,0:T(2,128)(2,1)S(1)}, bf16[256,2,512]{2,1,0:T(2,128)(2,1)}, u32[]{:S(2)}) copy-start(bf16[256,2,512]{2,1,0:T(2,128)(2,1)} %param.13) | copy-start | bytes 1572868
  15.2 0.6 copy-start.1
  15.8 8.6 %copy-start.13 = (f32[3,2,512]{2,1,0:T(2,128)S(1)}, f32[3,2,512]{2,1,0:T(2,128)}, u32[]{:S(2)}) copy-start(f32[3,2,512]{2,1,0:T(2,128)} %param.15) | copy-start | bytes 36868
  15.8 13.3 %collective-permute-start = (bf16[144,512]{1,0:T(8,128)(2,1)S(1)}, bf16[144,512]{1,0:T(8,128)(2,1)S(1)}, u32[]{:S(2)}, u32[]{:S(2)}) collective-permute-start(bf16[144,512]{1,0:T(8,128)(2,1)S(1)} %tail.1), channel_id=1, source_target_pairs={{0,8},{8,16},{16,24},{24,32},{32,40},{40,48},{48,56},{56,64},{64,7... | collective-permute-start | bytes 442376 | tf_op jit(solution)/shard_map/ppermute | solution.py:645
  29.1 5.5 %copy-start.2 = (bf16[144,512]{1,0:T(8,128)(2,1)}, bf16[144,512]{1,0:T(8,128)(2,1)S(1)}, u32[]{:S(2)}) copy-start(bf16[144,512]{1,0:T(8,128)(2,1)S(1)} %collective-permute-done.before) | copy-start | bytes 442372
  34.6 0.7 copy-start.4
  39.5 7.9 %collective-permute-start.1 = (bf16[16,512]{1,0:T(8,128)(2,1)}, bf16[16,512]{1,0:T(8,128)(2,1)S(1)}, u32[]{:S(2)}, u32[]{:S(2)}) collective-permute-start(bf16[16,512]{1,0:T(8,128)(2,1)} %get-tuple-element.60.own), channel_id=1, source_target_pairs={{0,8},{8,0},{16,24},{24,16},{32,40},{40,32},{48,56},{56,48},{64,72... | collective-permute-start | bytes 49160 | tf_op jit(solution)/shard_map/ppermute | solution.py:649
  47.4 0.6 copy-start.9
  49.6 13.8 %all-to-all-start.1 = ((bf16[16,16,512]{2,1,0:T(8,128)(2,1)}), bf16[16,16,512]{2,1,0:T(8,128)(2,1)S(1)}, u32[]{:S(2)}, u32[]{:S(2)}) async-start(bf16[16,16,512]{2,1,0:T(8,128)(2,1)} %join.1), calls=%async_computation.1 | async-start | bytes 524288 | tf_op jit(solution)/shard_map/all_to_all | solution.py:654
  63.4 0.7 copy-start.5
  68.8 9.1 %all-to-all-start.2 = ((f32[8,1,512]{2,1,0:T(1,128)}), f32[8,1,512]{2,1,0:T(1,128)S(1)}, u32[]{:S(2)}, u32[]{:S(2)}) async-start(f32[8,1,512]{2,1,0:T(1,128)} %get-tuple-element.70), calls=%async_computation.2 | async-start | bytes 32768 | tf_op jit(solution)/shard_map/all_to_all | solution.py:658
  77.9 0.6 copy-start.10
  85.9 19.3 %collective-permute-start.3 = (bf16[144,512]{1,0:T(8,128)(2,1)}, bf16[144,512]{1,0:T(8,128)(2,1)S(1)}, u32[]{:S(2)}, u32[]{:S(2)}) collective-permute-start(bf16[144,512]{1,0:T(8,128)(2,1)} %get-tuple-element.80), channel_id=1, source_target_pairs={{8,0},{16,8},{24,16},{32,24},{40,32},{48,40},{56,48},{64,56},{72,6... | collective-permute-start | bytes 442376 | tf_op jit(solution)/shard_map/ppermute | solution.py:645
  87.2 18.0 %collective-permute-start.2 = (bf16[96,512]{1,0:T(8,128)(2,1)}, bf16[96,512]{1,0:T(8,128)(2,1)S(1)}, u32[]{:S(2)}, u32[]{:S(2)}) collective-permute-start(bf16[96,512]{1,0:T(8,128)(2,1)} %get-tuple-element.79.pair), channel_id=1, source_target_pairs={{0,8},{8,0},{16,24},{24,16},{32,40},{40,32},{48,56},{56,48},{64,72... | collective-permute-start | bytes 294920 | tf_op jit(solution)/shard_map/ppermute | solution.py:649
  105.2 0.6 copy-start.8
  105.2 2.5 %copy-start.6 = (bf16[144,512]{1,0:T(8,128)(2,1)}, bf16[144,512]{1,0:T(8,128)(2,1)S(1)}, u32[]{:S(2)}) copy-start(bf16[144,512]{1,0:T(8,128)(2,1)S(1)} %collective-permute-done.3.after) | copy-start | bytes 442372
  107.7 13.1 %all-to-all-start.3 = ((bf16[16,24,512]{2,1,0:T(8,128)(2,1)}), bf16[16,24,512]{2,1,0:T(8,128)(2,1)S(1)}, u32[]{:S(2)}, u32[]{:S(2)}) async-start(bf16[16,24,512]{2,1,0:T(8,128)(2,1)} %share.1), calls=%async_computation.3 | async-start | bytes 786432 | tf_op jit(solution)/shard_map/all_to_all | solution.py:654
  120.8 0.7 copy-start.3
  128.2 0.7 copy-start.12
  129.9 26.3 %all-to-all-start.4 = ((bf16[32,15,512]{2,1,0:T(8,128)(2,1)}), bf16[32,15,512]{2,1,0:T(8,128)(2,1)S(1)}, u32[]{:S(2)}, u32[]{:S(2)}) async-start(bf16[32,15,512]{2,1,0:T(8,128)(2,1)} %pad_maximum_fusion), calls=%async_computation.4 | async-start | bytes 1048576 | tf_op jit(solution)/shard_map/all_to_all | solution.py:658

commit v3 on v2

--- a/solution.py
+++ b/solution.py
@@ -1,4 +1,3 @@
-import functools
 import math
 
 import jax
@@ -569,25 +568,40 @@
     lng_out[1] = back(gk2[...], tail[6:8, :], ltaps[1])
 
 
+def last_kernel(me, every, mine, partner, slot_out, slot):
+    first = me[0] % 2 == 0
+    ours, others = f32_of(every[...]), f32_of(partner[...])
+    slot[...] = jnp.zeros(slot.shape, F32)
+    slot[0:SHARE, :] = jnp.where(first, ours[0:SHARE], others[0:SHARE])
+    slot[SHARE : 2 * SHARE, :] = jnp.where(first, others[0:SHARE], ours[0:SHARE])
+    slot[2 * SHARE : 2 * SHARE + 9, :] = ours[SHARE : SHARE + 9] + others[SHARE : SHARE + 9]
+    own = f32_of(mine[...]) + others[MODES:]
+    for pair in range(PAIRS):
+        slot[2 * SHARE + 9 : 2 * SHARE + 10, :] = own[pair : pair + 1]
+        slot_out[pair] = slot[...].astype(BF16)
+
+
 def finish_kernel(last, mtap_out, ltap_out, filt_out, gain_out, res_out, log_out, f_all):
     added = jnp.zeros((last.shape[1], LANES), F32)
-    for place in range(last.shape[0]):
-        second, pair = place // PAIRS, place % PAIRS
-        piece = f32_of(last[2 * pair + second])
-        f_all[SHARE * place : SHARE * place + 8, :] = piece[0:8]
+    for pair in range(PAIRS):
+        piece = f32_of(last[pair])
+        f_all[SHARE * pair : SHARE * pair + 8, :] = piece[0:8]
         added = added + piece
+    for pair in range(PAIRS):
+        start = HALF + SHARE * pair
+        f_all[start : start + 8, :] = f32_of(last[pair])[SHARE : SHARE + 8]
     filt_out[...] = f_all[0:TAPS, :]
     gain_out[...] = f_all[TAPS : TAPS + 1, :]
     for shift in range(3):
         mtap_out[shift, 0:1, :] = f_all[TAPS + 1 + shift : TAPS + 2 + shift, :]
         ltap_out[shift, 1:2, :] = f_all[TAPS + 4 + shift : TAPS + 5 + shift, :]
-        mtap_out[shift, 1:2, :] = added[SHARE + shift : SHARE + 1 + shift]
-        mtap_out[shift, 2:3, :] = added[SHARE + 3 + shift : SHARE + 4 + shift]
-        ltap_out[shift, 0:1, :] = added[SHARE + 6 + shift : SHARE + 7 + shift]
+        mtap_out[shift, 1:2, :] = added[2 * SHARE + shift : 2 * SHARE + 1 + shift]
+        mtap_out[shift, 2:3, :] = added[2 * SHARE + 3 + shift : 2 * SHARE + 4 + shift]
+        ltap_out[shift, 0:1, :] = added[2 * SHARE + 6 + shift : 2 * SHARE + 7 + shift]
     block = pl.program_id(0)
     lane = lax.broadcasted_iota(jnp.int32, (MODES, LANES), 1)
     row = lax.broadcasted_iota(jnp.int32, (MODES, LANES), 0)
-    picked = jnp.where(lane % MODES == row, added[SHARE + 9 : SHARE + 10], 0.0)
+    picked = jnp.where(lane % MODES == row, added[2 * SHARE + 9 : 2 * SHARE + 10], 0.0)
     goal = (row == lane // MODES + 8 * (block % 2)).astype(F32)
     part = lax.dot_general(
         picked, goal, (((1,), (1,)), ((), ())), precision=precise, preferred_element_type=F32
@@ -731,14 +745,15 @@
         [(plane, BF16, "lane"), (plane, BF16, "lane"), (plane, F32, "lane"), (plane, F32, "lane"), ((HALO, width), BF16, "lane"), ((MODES + HALF, width), BF16, "lane"), ((HALF, width), F32, "lane")],
         [full, rows, ext, halo, (2 * HALF, LANES)],
     )
-    after = passed_along(edge, "ctx", -1)
     other = exchanged(pair)
     gpo, tap_rows = run(
         local_taps, "taps", width,
         [(gco, "lane"), (filt, "lane"), (k_one, "lane"), (v_one, "lane"), (med, "lane"), (before, "lane"), (forward, "whole"), (low, "whole")],
         [(plane, F32, "lane"), ((8, width), F32, "lane")], [ext, halo],
     )
-    other, after, tap_rows = lax.optimization_barrier((other, after, tap_rows))
+    edge, tap_rows = lax.optimization_barrier((edge, tap_rows))
+    after = passed_along(edge, "ctx", -1)
+    other, tap_rows = lax.optimization_barrier((other, tap_rows))
     (sent,) = run(
         share_kernel, "share", width,
         [(me, "scalar"), (pair, "lane"), (other, "lane"), (keep, "lane"), (rate, "lane")],
@@ -757,9 +772,17 @@
         [(plane, BF16, "lane"), (plane, F32, "lane"), ((2 * MODES, width), BF16, "lane"), ((MODES, width), BF16, "lane"), (modes, F32, "lane"), ((TAPS, width), F32, "lane")],
         [ext, rows, full, rows],
     )
-    every = jnp.broadcast_to(every[None, : SHARE + 9], (count, SHARE + 9, width))
-    own = res.reshape(2 * MODES, count, MODES).transpose(1, 0, 2).reshape(count, 1, width)
-    last = swap(jnp.concatenate([every, own], 1), "ctx")
+    own = res.reshape(2 * MODES, PAIRS, 2, MODES).transpose(2, 1, 0, 3).reshape(2, PAIRS, width)
+    second = me[0] % 2
+    mine = lax.dynamic_index_in_dim(own, second, 0, keepdims=False)
+    theirs = lax.dynamic_index_in_dim(own, 1 - second, 0, keepdims=False)
+    partner = exchanged(jnp.concatenate([every, theirs], 0))
+    (slots,) = run(
+        last_kernel, "last", width,
+        [(me, "scalar"), (every, "lane"), (mine, "lane"), (partner, "lane")],
+        [((PAIRS, 24, width), BF16, "lane")], [(24, width)], lanes=width,
+    )
+    last = in_plane(slots)
 
     grad_med, grad_lng = run(
         input_kernel, "inputs", width,

time: 160 us -> 155 us (0.969)
  waiting for transfers between devices: 35.3 us -> 31 us
  starting transfers between devices: 51 us -> 48.6 us
  Pallas kernels: 58 us -> 59.7 us
    all_to_all x3 -> x2, waiting for transfers between devices: 17 us -> 5.65 us  [swap(): return lax.all_to_all(array, axis, split_axis=0, concat_axis=0, tiled=True)]
    all_to_all x3 -> x2, starting transfers between devices: 25.4 us -> 17.9 us  [swap(): return lax.all_to_all(array, axis, split_axis=0, concat_axis=0, tiled=True)]
    all_to_all x2 -> x3, starting transfers between devices: 8.93 us -> 15.9 us  [in_plane(): lax.all_to_all(array, 'ctx', split_axis=0, concat_axis=0, tiled=True, axi...]
    ppermute x2, waiting for transfers between devices: 4.14 us -> 7.8 us  [passed_along(): return lax.ppermute(array, axis, pairs)]
    ppermute x2 -> x3, waiting for transfers between devices: 8.26 us -> 10.9 us  [exchanged(): lax.ppermute(array, 'ctx', [(i, i ^ 1) for i in range(lax.axis_size('ctx'...]
    ppermute x2 -> x3, starting transfers between devices: 7.65 us -> 5.93 us  [exchanged(): lax.ppermute(array, 'ctx', [(i, i ^ 1) for i in range(lax.axis_size('ctx'...]
    pallas_call x14 -> x15, Pallas kernels: 58 us -> 59.7 us  [run(): pl.pallas_call(kernel, grid=(width // lanes,), in_specs=[block_of(a.shape...]
    all_to_all x2 -> x3, waiting for transfers between devices: 5.87 us -> 6.63 us  [in_plane(): lax.all_to_all(array, 'ctx', split_axis=0, concat_axis=0, tiled=True, axi...]
  transfers between devices with their start and end apart: 9 -> 10, of which waited for: 7 -> 8; matrix products, arithmetic and copies ran while one was open for 3% -> 3% of each run, Pallas kernels for 20% -> 20%
where the time goes in v3:
time: 155 us; the launch traced here: 153 us
  Pallas kernels  59.7 us (39%)
  starting transfers between devices  48.6 us (31%)
  waiting for transfers between devices  31 us (20%)
  local copies, waits for them, and re-layouts  11.3 us (7%)
  other arithmetic  1.61 us (1%)
    pallas_call x15, Pallas kernels, run(): pl.pallas_call(kernel, grid=(width // lanes,), in_specs=[block_of(a.shape...  59.7 us
    all_to_all x2, starting transfers between devices, swap(): return lax.all_to_all(array, axis, split_axis=0, concat_axis=0, tiled=True)  17.9 us
    all_to_all x3, starting transfers between devices, in_plane(): lax.all_to_all(array, 'ctx', split_axis=0, concat_axis=0, tiled=True, axi...  15.9 us
    ppermute x3, waiting for transfers between devices, exchanged(): lax.ppermute(array, 'ctx', [(i, i ^ 1) for i in range(lax.axis_size('ctx'...  10.9 us
    ppermute x2, starting transfers between devices, passed_along(): return lax.ppermute(array, axis, pairs)  8.9 us
    unnamed x36, local copies, waits for them, and re-layouts  8.62 us
    ppermute x2, waiting for transfers between devices, passed_along(): return lax.ppermute(array, axis, pairs)  7.8 us
    all_to_all x3, waiting for transfers between devices, in_plane(): lax.all_to_all(array, 'ctx', split_axis=0, concat_axis=0, tiled=True, axi...  6.63 us
  transfers between devices with their start and end apart: 10, of which 8 were waited for; matrix products, arithmetic and copies ran while one was open for 3% of the time, Pallas kernels for 20%

profile of v3, /device:TPU:64, one launch (start us, length us, event | category | flops | bytes accessed | tf_op | source)
XLA Modules:
  0.0 153.1 jit_solution(1936503987683559235)
XLA Ops:
  0.7 0.9 select_maximum_fusion
  1.5 0.7 broadcast_in_dim.2
  2.2 12.3 %all-to-all-start = ((f32[32,16,128]{2,1,0:T(8,128)}), f32[32,16,128]{2,1,0:T(8,128)S(1)}, u32[]{:S(2)}, u32[]{:S(2)}) async-start(f32[32,16,128]{2,1,0:T(8,128)} %broadcast_in_dim.2), calls=%async_computation | async-start | bytes 524288 | tf_op jit(solution)/shard_map/all_to_all | solution.py:672
  14.6 0.7 convert_bitcast_fusion
  15.4 0.5 tail.1
  15.9 7.6 %collective-permute-start = (bf16[144,512]{1,0:T(8,128)(2,1)S(1)}, bf16[144,512]{1,0:T(8,128)(2,1)S(1)}, u32[]{:S(2)}, u32[]{:S(2)}) collective-permute-start(bf16[144,512]{1,0:T(8,128)(2,1)S(1)} %tail.1), channel_id=1, source_target_pairs={{0,8},{8,16},{16,24},{24,32},{32,40},{40,48},{48,56},{56,64},{64,7... | collective-permute-start | bytes 442376 | tf_op jit(solution)/shard_map/ppermute | solution.py:659
  23.5 0.8 copy.37
  24.4 0.6 copy.39
  25.0 4.0 %collective-permute-done.before = bf16[144,512]{1,0:T(8,128)(2,1)S(1)} collective-permute-done((bf16[144,512]{1,0:T(8,128)(2,1)S(1)}, bf16[144,512]{1,0:T(8,128)(2,1)S(1)}, u32[]{:S(2)}, u32[]{:S(2)}) %collective-permute-start) | collective-permute-done | bytes 147488 | tf_op jit(solution)/shard_map/ppermute | solution.py:659
  29.0 5.6 %all-to-all-done.packed = f32[32,16,128]{2,1,0:T(8,128)S(1)} async-done(((f32[32,16,128]{2,1,0:T(8,128)}), f32[32,16,128]{2,1,0:T(8,128)S(1)}, u32[]{:S(2)}, u32[]{:S(2)}) %all-to-all-start) | async-done | bytes 262176 | tf_op jit(solution)/shard_map/all_to_all | solution.py:672
  34.6 0.7 copy-done.4
  35.3 4.2 %long.1 = (f32[16,512]{1,0:T(8,128)}, f32[16,512]{1,0:T(8,128)}, bf16[256,512]{1,0:T(8,128)(2,1)}, bf16[256,512]{1,0:T(8,128)(2,1)}, bf16[256,512]{1,0:T(8,128)(...) custom-call(f32[32,16,128]{2,1,0:T(8,128)} %copy-done.4, bf16[144,512]{1,0:T(8,128)(2,1)} %copy-done.2, ...), custom_call_target="tpu_custom_call" | custom-call | flops 1000000 | bytes 1208320 | tf_op jit(solution)/shard_map/long/pallas_call | solution.py:641
  39.5 0.9 collective-permute-start.1
  40.3 5.6 %medium.1 = (bf16[384,512]{1,0:T(8,128)(2,1)}, bf16[256,512]{1,0:T(8,128)(2,1)}, bf16[256,512]{1,0:T(8,128)(2,1)}, bf16[256,512]{1,0:T(8,128)(2,1)}, f32[256,512...) custom-call(bf16[3,256,512]{2,1,0:T(8,128)(2,1)} %bitcast.26, bf16[144,512]{1,0:T(8,128)(2,1)} %copy-done.2, ...), custom_call_target="tpu_custom_call" | custom-call | flops 1000000 | bytes 1280000 | tf_op jit(solution)/shard_map/medium/pallas_call | solution.py:641
  45.9 1.5 collective-permute-done.1.other.z_other
  47.4 0.6 copy-done.9
  48.0 1.5 join.1
  49.5 5.2 %all-to-all-start.1 = ((bf16[16,16,512]{2,1,0:T(8,128)(2,1)}), bf16[16,16,512]{2,1,0:T(8,128)(2,1)S(1)}, u32[]{:S(2)}, u32[]{:S(2)}) async-start(bf16[16,16,512]{2,1,0:T(8,128)(2,1)} %join.1), calls=%async_computation.1 | async-start | bytes 524288 | tf_op jit(solution)/shard_map/all_to_all | solution.py:668
  54.8 4.3 %back.1.y_loc = f32[256,512]{1,0:T(8,128)} custom-call(bf16[256,512]{1,0:T(8,128)(2,1)} %get-tuple-element.72.gconv.g, f32[16,512]{1,0:T(8,128)} %get-tuple-element.64.rate, f32[16,512]{1,0:T(8,128)} %get-tuple-element.65.weight, f32[16,8,512]{2,1,0:T(8,128)} %get-tuple-element.67.ends), custom_call_target="tpu_custom_call" | custom-call | flops 1000000 | bytes 589824 | tf_op jit(solution)/shard_map/back/pallas_call | solution.py:641
  59.1 4.1 %all-to-all-done.1.zg = bf16[16,16,512]{2,1,0:T(8,128)(2,1)S(1)} async-done(((bf16[16,16,512]{2,1,0:T(8,128)(2,1)}), bf16[16,16,512]{2,1,0:T(8,128)(2,1)S(1)}, u32[]{:S(2)}, u32[]{:S(2)}) %all-to-all-start.1) | async-done | bytes 262176 | tf_op jit(solution)/shard_map/all_to_all | solution.py:668
  63.2 0.7 copy-done.5
  63.9 4.7 %inner.1 = (bf16[256,512]{1,0:T(8,128)(2,1)}, f32[16,512]{1,0:T(8,128)}, f32[8,1,512]{2,1,0:T(1,128)}) custom-call(s32[1]{0:T(128)} %bitcast.me, bf16[16,16,512]{2,1,0:T(8,128)(2,1)} %copy-done.5, bf16[16,512]{1,0:T(8,128)(2,1)} %copy-done.9, f32[16,512]{1,0:T(8,128)} %get-tuple-element.64.rate, f32[16,512]{1,0:T(8,128)} %get-tuple-element.65.weight, ...), custom_call_target="tpu_custom_call" | custom-call | flops 1000000 | bytes 1665028 | tf_op jit(solution)/shard_map/inner/pallas_call | solution.py:641
  68.6 5.6 %all-to-all-start.2 = ((f32[8,1,512]{2,1,0:T(1,128)}), f32[8,1,512]{2,1,0:T(1,128)S(1)}, u32[]{:S(2)}, u32[]{:S(2)}) async-start(f32[8,1,512]{2,1,0:T(1,128)} %get-tuple-element.71), calls=%async_computation.2 | async-start | bytes 32768 | tf_op jit(solution)/shard_map/all_to_all | solution.py:672
  74.2 4.0 %behind.1.ends = f32[32,8,512]{2,1,0:T(8,128)} custom-call(bf16[256,512]{1,0:T(8,128)(2,1)} %get-tuple-element.72.gconv.g, f32[16,512]{1,0:T(8,128)} %get-tuple-element.64.rate), custom_call_target="tpu_custom_call" | custom-call | flops 1000000 | bytes 294912 | tf_op jit(solution)/shard_map/behind/pallas_call | solution.py:641
  78.2 0.6 copy-done.10
  78.8 7.4 %norm.1 = (bf16[256,512]{1,0:T(8,128)(2,1)}, bf16[256,512]{1,0:T(8,128)(2,1)}, f32[256,512]{1,0:T(8,128)}, f32[256,512]{1,0:T(8,128)}, bf16[144,512]{1,0:T(8,128...) custom-call(s32[1]{0:T(128)} %bitcast.me, f32[8,1,512]{2,1,0:T(1,128)} %copy-done.10, ...), custom_call_target="tpu_custom_call" | custom-call | flops 1000000 | bytes 4851716 | tf_op jit(solution)/shard_map/norm/pallas_call | solution.py:641
  86.2 2.3 %collective-permute-start.2 = (bf16[96,512]{1,0:T(8,128)(2,1)}, bf16[96,512]{1,0:T(8,128)(2,1)S(1)}, u32[]{:S(2)}, u32[]{:S(2)}) collective-permute-start(bf16[96,512]{1,0:T(8,128)(2,1)} %get-tuple-element.80.pair), channel_id=1, source_target_pairs={{0,8},{8,0},{16,24},{24,16},{32,40},{40,32},{48,56},{56,48},{64,72... | collective-permute-start | bytes 294920 | tf_op jit(solution)/shard_map/ppermute | solution.py:663
  88.5 4.5 %taps.1 = (f32[256,512]{1,0:T(8,128)}, f32[8,512]{1,0:T(8,128)}) custom-call(bf16[256,512]{1,0:T(8,128)(2,1)} %get-tuple-element.82.gco, bf16[128,512]{1,0:T(8,128)(2,1)} %filt.7, bf16[256,512]{1,0:T(8,128)(2,1)} %get-tuple-element.76.k_one, bf16[256,512]{1,0:T(8,128)(2,1)} %get-tuple-element.77.v_one, bf16[3,256,512]{2,1,0:T(8,128)(2,1)} %bitcast.28, ...), custom_call_target="tpu_custom_call" | custom-call | flops 1000000 | bytes 2048000 | tf_op jit(solution)/shard_map/taps/pallas_call | solution.py:641
  93.0 4.4 %collective-permute-done.2.got.other = bf16[96,512]{1,0:T(8,128)(2,1)S(1)} collective-permute-done((bf16[96,512]{1,0:T(8,128)(2,1)}, bf16[96,512]{1,0:T(8,128)(2,1)S(1)}, u32[]{:S(2)}, u32[]{:S(2)}) %collective-permute-start.2) | collective-permute-done | bytes 98336 | tf_op jit(solution)/shard_map/ppermute | solution.py:663
  97.4 0.6 copy-done.8
  98.0 1.8 %share.1 = bf16[16,24,512]{2,1,0:T(8,128)(2,1)} custom-call(s32[1]{0:T(128)} %bitcast.me, bf16[96,512]{1,0:T(8,128)(2,1)} %get-tuple-element.80.pair, bf16[96,512]{1,0:T(8,128)(2,1)} %copy-done.8, f32[80,512]{1,0:T(8,128)} %get-tuple-element.86.keep, f32[16,512]{1,0:T(8,128)} %get-tuple-element.64.rate), custom_call_target="tpu_custom_call" | custom-call | flops 1000000 | bytes 393220 | tf_op jit(solution)/shard_map/share/pallas_call | solution.py:641
  99.9 3.7 %all-to-all-start.3 = ((bf16[16,24,512]{2,1,0:T(8,128)(2,1)}), bf16[16,24,512]{2,1,0:T(8,128)(2,1)S(1)}, u32[]{:S(2)}, u32[]{:S(2)}) async-start(bf16[16,24,512]{2,1,0:T(8,128)(2,1)} %share.1), calls=%async_computation.3 | async-start | bytes 786432 | tf_op jit(solution)/shard_map/all_to_all | solution.py:668
  103.6 1.3 collective-permute-start.3
  104.9 7.8 %modes.1 = (f32[256,512]{1,0:T(8,128)}, f32[80,512]{1,0:T(8,128)}, f32[16,8,512]{2,1,0:T(8,128)}) custom-call(bf16[256,512]{1,0:T(8,128)(2,1)} %get-tuple-element.87.x, bf16[256,512]{1,0:T(8,128)(2,1)} %get-tuple-element.72.gconv.g, f32[16,512]{1,0:T(8,128)} %get-tuple-element.64.rate, f32[16,512]{1,0:T(8,128)} %get-tuple-element.65.weight, ...), custom_call_target="tpu_custom_call" | custom-call | flops 1000000 | bytes 1114112 | tf_op jit(solution)/shard_map/modes/pallas_call | solution.py:641
  112.7 3.8 %collective-permute-done.3.after = bf16[144,512]{1,0:T(8,128)(2,1)S(1)} collective-permute-done((bf16[144,512]{1,0:T(8,128)(2,1)S(1)}, bf16[144,512]{1,0:T(8,128)(2,1)S(1)}, u32[]{:S(2)}, u32[]{:S(2)}) %collective-permute-start.3) | collective-permute-done | bytes 147488 | tf_op jit(solution)/shard_map/ppermute | solution.py:659
  116.5 0.7 copy-done.6
  117.3 5.6 %answer.1 = (bf16[256,512]{1,0:T(8,128)(2,1)}, f32[256,512]{1,0:T(8,128)}, bf16[32,512]{1,0:T(8,128)(2,1)}, bf16[16,512]{1,0:T(8,128)(2,1)}, f32[16,512]{1,0:T(8,128)}, /*index=5*/f32[128,512]{1,0:T(8,128)}) custom-call(s32[1]{0:T(128)} %bitcast.me, bf16[16,24,512]{2,1,0:T(8,128)(2,1)} %copy-done.3, bf16[96,512]{1,0:T(8,128)(2,1)} %get-tuple-element.80.pair, ...), custom_call_target="tpu_custom_call" | custom-call | flops 1000000 | bytes 4636676 | tf_op jit(solution)/shard_map/answer/pallas_call | solution.py:641
  122.9 0.9 copy.31
  124.3 0.6 dynamic-slice_bitcast_fusion
  125.0 2.8 %collective-permute-start.4 = (bf16[32,512]{1,0:T(8,128)(2,1)S(1)}, bf16[32,512]{1,0:T(8,128)(2,1)S(1)}, u32[]{:S(2)}, u32[]{:S(2)}) collective-permute-start(bf16[32,512]{1,0:T(8,128)(2,1)S(1)} %pad_maximum_fusion), channel_id=1, source_target_pairs={{0,8},{8,0},{16,24},{24,16},{32,40},{40,32},{48,56},{56,48},{64,72... | collective-permute-start | bytes 98312 | tf_op jit(solution)/shard_map/ppermute | solution.py:663
  127.8 5.1 %collective-permute-done.4.partner = bf16[32,512]{1,0:T(8,128)(2,1)S(1)} collective-permute-done((bf16[32,512]{1,0:T(8,128)(2,1)S(1)}, bf16[32,512]{1,0:T(8,128)(2,1)S(1)}, u32[]{:S(2)}, u32[]{:S(2)}) %collective-permute-start.4) | collective-permute-done | bytes 32800 | tf_op jit(solution)/shard_map/ppermute | solution.py:663
  132.8 0.6 copy-done.12
  133.4 1.7 %last.1 = bf16[16,24,512]{2,1,0:T(8,128)(2,1)} custom-call(s32[1]{0:T(128)} %bitcast.me, bf16[16,512]{1,0:T(8,128)(2,1)} %get-tuple-element.105.every, bf16[16,512]{1,0:T(8,128)(2,1)} %get-tuple-element.132.mine, bf16[32,512]{1,0:T(8,128)(2,1)} %copy-done.12), custom_call_target="tpu_custom_call" | custom-call | flops 1000000 | bytes 65540 | tf_op jit(solution)/shard_map/last/pallas_call | solution.py:641
  135.1 7.0 %all-to-all-start.4 = ((bf16[16,24,512]{2,1,0:T(8,128)(2,1)}), bf16[16,24,512]{2,1,0:T(8,128)(2,1)S(1)}, u32[]{:S(2)}, u32[]{:S(2)}) async-start(bf16[16,24,512]{2,1,0:T(8,128)(2,1)} %last.1), calls=%async_computation.4 | async-start | bytes 786432 | tf_op jit(solution)/shard_map/all_to_all | solution.py:668
  142.2 4.3 %inputs.1 = (bf16[3,256,512]{2,1,0:T(8,128)(2,1)}, bf16[2,256,512]{2,1,0:T(8,128)(2,1)}) custom-call(f32[256,512]{1,0:T(8,128)} %get-tuple-element.97.gq1, f32[256,512]{1,0:T(8,128)} %get-tuple-element.98.gpo, f32[128,512]{1,0:T(8,128)} %get-tuple-element.99.late, f32[256,512]{1,0:T(8,128)} %get-tuple-element.100.gq2, f32[256,512]{1,0:T(8,128)} %get-tuple-element.101.gk2, ...), custom_call_target="tpu_custom_call" | custom-call | flops 1000000 | bytes 3160064 | tf_op jit(solution)/shard_map/inputs/pallas_call | solution.py:641
  146.4 2.4 %copy.33 = bf16[256,2,512]{2,1,0:T(2,128)(2,1)} copy(bf16[256,2,512]{2,0,1:T(8,128)(2,1)} %bitcast.38) | data formatting | bytes 1048576
  148.8 2.5 %all-to-all-done.4.last = bf16[16,24,512]{2,1,0:T(8,128)(2,1)S(1)} async-done(((bf16[16,24,512]{2,1,0:T(8,128)(2,1)}), bf16[16,24,512]{2,1,0:T(8,128)(2,1)S(1)}, u32[]{:S(2)}, u32[]{:S(2)}) %all-to-all-start.4) | async-done | bytes 393248 | tf_op jit(solution)/shard_map/all_to_all | solution.py:668
  151.3 1.9 %finish.1 = (f32[3,3,512]{2,1,0:T(4,128)}, f32[3,2,512]{2,1,0:T(2,128)}, f32[128,512]{1,0:T(8,128)}, f32[1,512]{1,0:T(1,128)}, f32[16,16]{1,0:T(8,128)}, /*index=5*/f32[16,16]{1,0:T(8,128)}) custom-call(bf16[16,24,512]{2,1,0:T(8,128)(2,1)S(1)} %all-to-all-done.4.last), custom_call_target="tpu_custom_call" | custom-call | flops 1000000 | bytes 393216 | tf_op jit(solution)/shard_map/finish/pallas_call | solution.py:641
  (33 shorter events, 0.8 us)
Async XLA Ops:
  0.6 14.7 %copy-start = (bf16[256,3,512]{2,0,1:T(8,128)(2,1)S(1)}, bf16[256,3,512]{2,0,1:T(8,128)(2,1)}, u32[]{:S(2)}) copy-start(bf16[256,3,512]{2,0,1:T(8,128)(2,1)} %param.12) | copy-start | bytes 2359300
  2.2 12.3 %copy-start.13 = (f32[3,3,512]{2,1,0:T(4,128)S(1)}, f32[3,3,512]{2,1,0:T(4,128)}, u32[]{:S(2)}) copy-start(f32[3,3,512]{2,1,0:T(4,128)} %param.14) | copy-start | bytes 55300
  2.2 32.4 %all-to-all-start = ((f32[32,16,128]{2,1,0:T(8,128)}), f32[32,16,128]{2,1,0:T(8,128)S(1)}, u32[]{:S(2)}, u32[]{:S(2)}) async-start(f32[32,16,128]{2,1,0:T(8,128)} %broadcast_in_dim.2), calls=%async_computation | async-start | bytes 524288 | tf_op jit(solution)/shard_map/all_to_all | solution.py:672
  14.5 9.0 %copy-start.7 = (bf16[256,2,512]{2,1,0:T(2,128)(2,1)S(1)}, bf16[256,2,512]{2,1,0:T(2,128)(2,1)}, u32[]{:S(2)}) copy-start(bf16[256,2,512]{2,1,0:T(2,128)(2,1)} %param.13) | copy-start | bytes 1572868
  14.6 1.3 copy-start.1
  15.9 8.5 %copy-start.14 = (f32[3,2,512]{2,1,0:T(2,128)S(1)}, f32[3,2,512]{2,1,0:T(2,128)}, u32[]{:S(2)}) copy-start(f32[3,2,512]{2,1,0:T(2,128)} %param.15) | copy-start | bytes 36868
  15.9 13.1 %collective-permute-start = (bf16[144,512]{1,0:T(8,128)(2,1)S(1)}, bf16[144,512]{1,0:T(8,128)(2,1)S(1)}, u32[]{:S(2)}, u32[]{:S(2)}) collective-permute-start(bf16[144,512]{1,0:T(8,128)(2,1)S(1)} %tail.1), channel_id=1, source_target_pairs={{0,8},{8,16},{16,24},{24,32},{32,40},{40,48},{48,56},{56,64},{64,7... | collective-permute-start | bytes 442376 | tf_op jit(solution)/shard_map/ppermute | solution.py:659
  29.0 5.6 %copy-start.2 = (bf16[144,512]{1,0:T(8,128)(2,1)}, bf16[144,512]{1,0:T(8,128)(2,1)S(1)}, u32[]{:S(2)}) copy-start(bf16[144,512]{1,0:T(8,128)(2,1)S(1)} %collective-permute-done.before) | copy-start | bytes 442372
  34.6 0.7 copy-start.4
  39.5 7.9 %collective-permute-start.1 = (bf16[16,512]{1,0:T(8,128)(2,1)}, bf16[16,512]{1,0:T(8,128)(2,1)S(1)}, u32[]{:S(2)}, u32[]{:S(2)}) collective-permute-start(bf16[16,512]{1,0:T(8,128)(2,1)} %get-tuple-element.61.own), channel_id=1, source_target_pairs={{0,8},{8,0},{16,24},{24,16},{32,40},{40,32},{48,56},{56,48},{64,72... | collective-permute-start | bytes 49160 | tf_op jit(solution)/shard_map/ppermute | solution.py:663
  47.4 0.6 copy-start.9
  49.5 13.7 %all-to-all-start.1 = ((bf16[16,16,512]{2,1,0:T(8,128)(2,1)}), bf16[16,16,512]{2,1,0:T(8,128)(2,1)S(1)}, u32[]{:S(2)}, u32[]{:S(2)}) async-start(bf16[16,16,512]{2,1,0:T(8,128)(2,1)} %join.1), calls=%async_computation.1 | async-start | bytes 524288 | tf_op jit(solution)/shard_map/all_to_all | solution.py:668
  63.2 0.7 copy-start.5
  68.6 9.5 %all-to-all-start.2 = ((f32[8,1,512]{2,1,0:T(1,128)}), f32[8,1,512]{2,1,0:T(1,128)S(1)}, u32[]{:S(2)}, u32[]{:S(2)}) async-start(f32[8,1,512]{2,1,0:T(1,128)} %get-tuple-element.71), calls=%async_computation.2 | async-start | bytes 32768 | tf_op jit(solution)/shard_map/all_to_all | solution.py:672
  78.2 0.6 copy-start.10
  86.2 11.2 %collective-permute-start.2 = (bf16[96,512]{1,0:T(8,128)(2,1)}, bf16[96,512]{1,0:T(8,128)(2,1)S(1)}, u32[]{:S(2)}, u32[]{:S(2)}) collective-permute-start(bf16[96,512]{1,0:T(8,128)(2,1)} %get-tuple-element.80.pair), channel_id=1, source_target_pairs={{0,8},{8,0},{16,24},{24,16},{32,40},{40,32},{48,56},{56,48},{64,72... | collective-permute-start | bytes 294920 | tf_op jit(solution)/shard_map/ppermute | solution.py:663
  97.4 0.6 copy-start.8
  99.9 3.7 %copy-start.15 = (bf16[144,512]{1,0:T(8,128)(2,1)S(1)}, bf16[144,512]{1,0:T(8,128)(2,1)}, u32[]{:S(2)}) copy-start(bf16[144,512]{1,0:T(8,128)(2,1)} %get-tuple-element.95) | copy-start | bytes 442372
  99.9 16.7 %all-to-all-start.3 = ((bf16[16,24,512]{2,1,0:T(8,128)(2,1)}), bf16[16,24,512]{2,1,0:T(8,128)(2,1)S(1)}, u32[]{:S(2)}, u32[]{:S(2)}) async-start(bf16[16,24,512]{2,1,0:T(8,128)(2,1)} %share.1), calls=%async_computation.3 | async-start | bytes 786432 | tf_op jit(solution)/shard_map/all_to_all | solution.py:668
  103.6 12.9 %collective-permute-start.3 = (bf16[144,512]{1,0:T(8,128)(2,1)S(1)}, bf16[144,512]{1,0:T(8,128)(2,1)S(1)}, u32[]{:S(2)}, u32[]{:S(2)}) collective-permute-start(bf16[144,512]{1,0:T(8,128)(2,1)S(1)} %copy-done.15), channel_id=1, source_target_pairs={{8,0},{16,8},{24,16},{32,24},{40,32},{48,40},{56,48},{64,56},{72,6... | collective-permute-start | bytes 442376 | tf_op jit(solution)/shard_map/ppermute | solution.py:659
  116.5 0.7 copy-start.6
  116.5 0.8 copy-start.3
  124.3 0.7 copy-start.11
  125.0 7.8 %collective-permute-start.4 = (bf16[32,512]{1,0:T(8,128)(2,1)S(1)}, bf16[32,512]{1,0:T(8,128)(2,1)S(1)}, u32[]{:S(2)}, u32[]{:S(2)}) collective-permute-start(bf16[32,512]{1,0:T(8,128)(2,1)S(1)} %pad_maximum_fusion), channel_id=1, source_target_pairs={{0,8},{8,0},{16,24},{24,16},{32,40},{40,32},{48,56},{56,48},{64,72... | collective-permute-start | bytes 98312 | tf_op jit(solution)/shard_map/ppermute | solution.py:663
  132.8 0.6 copy-start.12
  135.1 16.2 %all-to-all-start.4 = ((bf16[16,24,512]{2,1,0:T(8,128)(2,1)}), bf16[16,24,512]{2,1,0:T(8,128)(2,1)S(1)}, u32[]{:S(2)}, u32[]{:S(2)}) async-start(bf16[16,24,512]{2,1,0:T(8,128)(2,1)} %last.1), calls=%async_computation.4 | async-start | bytes 786432 | tf_op jit(solution)/shard_map/all_to_all | solution.py:668

commit v4 on v3

--- a/solution.py
+++ b/solution.py
@@ -139,7 +139,7 @@
     lax.fori_loop(0, STEPS, body, tuple(entries), unroll=2)
 
 
-def add_entry(local, target, rate, weight, entry, backward, inside=None):
+def add_entry(target, rate, weight, entry, backward, inside=None):
     decay = jnp.exp(-rate)
     decays = [spread(decay, r) for r in range(MODES)]
     start = weight * entry
@@ -154,7 +154,7 @@
         terms = list(parts)
         while len(terms) > 1:
             terms = [terms[k] + terms[k + 1] for k in range(0, len(terms), 2)]
-        target[pl.ds(step, CHUNKS, stride=STEPS), :] = at_step(local, step) + terms[0]
+        target[pl.ds(step, CHUNKS, stride=STEPS), :] = at_step(target, step) + terms[0]
         return parts
 
     lax.fori_loop(0, STEPS, body, tuple(parts), unroll=4)
@@ -247,7 +247,7 @@
 
 
 def medium_kernel(med, before, taps, filt, forward, top,
-                  prod_out, q_out, k_out, v_out, conv_out, gated_out, sq_out, ext, halo):
+                  prod_out, q_out, k_out, v_out, conv_out, gated_out, sq_out, ext, halo, block):
     halo[...] = f32_of(before[...])
     feats = []
     for j in range(3):
@@ -276,23 +276,24 @@
         precision=precise, preferred_element_type=F32,
     )
 
-    @pl.when(pl.program_id(0) == 0)
-    def _():
-        sq_out[...] = jnp.zeros(sq_out.shape, F32)
-
-    sq_out[...] += part
-
-
-def back_kernel(gconv, rate, weight, ends, y_out, grad):
+    if block == 0:
+        sq_out[...] = part
+    else:
+        sq_out[...] += part
+
+
+def back_kernel(gconv, rate, weight, ends, y_out, grad, full):
     grad[...] = f32_of(gconv[...])
     entries = chunk_entries([ends[r] for r in range(MODES)], powers(rate[...]), True)
-    local_answer(grad, y_out, rate[...], weight[...], entries, True)
+    local_answer(grad, full, rate[...], weight[...], entries, True)
+    y_out[...] = full[...]
 
 
 def inner_kernel(me, zg, z_other, rate, weight, y_loc, k_two, gated, gain, square, gp_out, zin_out, in_out, full, total):
     entry = entry_state(zg, f32_of(z_other[...]), rate[...], me[0], True)
     zin_out[...] = entry
-    add_entry(y_loc, full, rate[...], weight[...], entry, True)
+    full[...] = y_loc[...]
+    add_entry(full, rate[...], weight[...], entry, True)
     sent = full[...].astype(BF16)
     gp_out[...] = sent
     product = f32_of(sent) * f32_of(k_two[...]) * gain[...] * gated[...]
@@ -301,15 +302,17 @@
         precision=precise, preferred_element_type=F32,
     )
 
-    @pl.when(pl.program_id(0) == 0)
+    block = pl.program_id(0)
+
+    @pl.when(block == 0)
     def _():
         total[...] = part
 
-    @pl.when(pl.program_id(0) > 0)
+    @pl.when(block > 0)
     def _():
         total[...] += part
 
-    @pl.when(pl.program_id(0) == pl.num_programs(0) - 1)
+    @pl.when(block == pl.num_programs(0) - 1)
     def _():
         for device in range(in_out.shape[0]):
             in_out[device, 0:1, 0:ROWS] = square[0:1, :]
@@ -413,7 +416,7 @@
             ends_out[MODES + base + r] = q[r]
 
 
-def modes_kernel(x, g, rate, weight, ends, y_out, sums_out, entry_out, xs, gs):
+def modes_kernel(x, g, rate, weight, ends, y_out, sums_out, entry_out, xs, gs, full):
     xs[...] = f32_of(x[...])
     gs[...] = f32_of(g[...])
     rates = rate[...]
@@ -439,8 +442,8 @@
             terms = [weights[r] * s[r] for r in range(half)]
             while len(terms) > 1:
                 terms = [terms[k] + terms[k + 1] for k in range(0, len(terms), 2)]
-            answer = terms[0] if base == 0 else at_step(y_out, n) + terms[0]
-            y_out[pl.ds(n, CHUNKS, stride=STEPS), :] = answer
+            answer = terms[0] if base == 0 else at_step(full, n) + terms[0]
+            full[pl.ds(n, CHUNKS, stride=STEPS), :] = answer
             return s, q, p, l
 
         s, q, p, l = lax.fori_loop(0, STEPS, ahead, ((zero,) * half,) * 4, unroll=4)
@@ -472,6 +475,7 @@
         for kind, value in enumerate(rows):
             place = kind * MODES + r
             sums_out[place : place + 1, :] = jnp.sum(value, 0, keepdims=True)
+    y_out[...] = full[...]
     for r in range(MODES):
         entry_out[r] = entries[r]
 
@@ -504,7 +508,8 @@
                   mixed_out, gq2_out, res_out, row_out, exit_out, late_out, ext, halo, full, rows):
     rates = rate[...]
     entry = entry_state(sg, f32_of(other[0:MODES, :]), rates, me[0], False)
-    add_entry(y_loc, full, rates, weight[...], entry, False, inside)
+    full[...] = y_loc[...]
+    add_entry(full, rates, weight[...], entry, False, inside)
     conv = rounded(full[...])
     grad_out = f32_of(cot[...])
     mixed_out[...] = (f32_of(q_two[...]) * conv).astype(BF16)
@@ -581,7 +586,7 @@
         slot_out[pair] = slot[...].astype(BF16)
 
 
-def finish_kernel(last, mtap_out, ltap_out, filt_out, gain_out, res_out, log_out, f_all):
+def finish_kernel(last, mtap_out, ltap_out, filt_out, gain_out, res_out, log_out, f_all, block):
     added = jnp.zeros((last.shape[1], LANES), F32)
     for pair in range(PAIRS):
         piece = f32_of(last[pair])
@@ -598,7 +603,6 @@
         mtap_out[shift, 1:2, :] = added[2 * SHARE + shift : 2 * SHARE + 1 + shift]
         mtap_out[shift, 2:3, :] = added[2 * SHARE + 3 + shift : 2 * SHARE + 4 + shift]
         ltap_out[shift, 0:1, :] = added[2 * SHARE + 6 + shift : 2 * SHARE + 7 + shift]
-    block = pl.program_id(0)
     lane = lax.broadcasted_iota(jnp.int32, (MODES, LANES), 1)
     row = lax.broadcasted_iota(jnp.int32, (MODES, LANES), 0)
     picked = jnp.where(lane % MODES == row, added[2 * SHARE + 9 : 2 * SHARE + 10], 0.0)
@@ -607,48 +611,64 @@
         picked, goal, (((1,), (1,)), ((), ())), precision=precise, preferred_element_type=F32
     )
 
-    @pl.when(block == 0)
-    def _():
-        res_out[...] = part
-
-    @pl.when(block == 1)
-    def _():
-        res_out[...] += part
-
-    @pl.when(block == 2)
-    def _():
-        log_out[...] = part
-
-    @pl.when(block == 3)
-    def _():
-        log_out[...] += part
-
-
-def block_of(shape, kind, lanes):
+    target = res_out if block < 2 else log_out
+    if block % 2 == 0:
+        target[...] = part
+    else:
+        target[...] += part
+
+
+def view_of(ref, kind, block):
     if kind == "lane":
-        lead = shape[:-1]
-        return pl.BlockSpec(lead + (lanes,), lambda l: (0,) * len(lead) + (l,))
+        return ref.at[(slice(None),) * (len(ref.shape) - 1) + (pl.ds(LANES * block, LANES),)]
+    if kind == "source":
+        return ref.at[pl.ds(8 * block, 8)]
+    return ref
+
+
+def spec_of(shape, kind):
+    lead = shape[:-1]
+    if kind == "lane":
+        return pl.BlockSpec(lead + (LANES,), lambda l: (0,) * len(lead) + (l,))
     if kind == "whole":
         return pl.BlockSpec(shape, lambda l: (0,) * len(shape))
-    if kind == "source":
-        return pl.BlockSpec((8,) + shape[1:], lambda l: (l,) + (0,) * (len(shape) - 1))
     return pl.BlockSpec(memory_space=pltpu.SMEM)
 
 
-def run(kernel, name, width, inputs, outputs, scratch, limit=63, flops=1000000, lanes=LANES):
+def run(kernel, name, width, inputs, outputs, scratch, limit=63, whole=False, blocks=False, grid=False):
     arrays = [array for array, _ in inputs]
+    kinds = [kind for _, kind in inputs] + [kind for _, _, kind in outputs]
+
+    def body(*refs):
+        if whole or grid:
+            return kernel(*refs)
+        for block in range(width // LANES):
+            views = [view_of(ref, kind, block) for ref, kind in zip(refs, kinds)]
+            extra = {"block": block} if blocks else {}
+            kernel(*views, *refs[len(kinds) :], **extra)
+
     moved = sum(a.size * a.dtype.itemsize for a in arrays)
+    vmem = pl.BlockSpec(memory_space=pltpu.VMEM)
+    if grid:
+        places = {
+            "grid": (width // LANES,),
+            "in_specs": [spec_of(a.shape, kind) for a, kind in inputs],
+            "out_specs": [spec_of(shape, kind) for shape, _, kind in outputs],
+        }
+    else:
+        places = {
+            "in_specs": [
+                pl.BlockSpec(memory_space=pltpu.SMEM) if kind == "scalar" else vmem for _, kind in inputs
+            ],
+            "out_specs": [vmem for _ in outputs],
+        }
     return pl.pallas_call(
-        kernel,
-        grid=(width // lanes,),
-        in_specs=[block_of(a.shape, kind, lanes) for a, kind in inputs],
-        out_specs=[block_of(shape, kind, lanes) for shape, _, kind in outputs],
-        out_shape=[
-            jax.ShapeDtypeStruct(shape, dtype) for shape, dtype, _ in outputs
-        ],
+        body,
+        **places,
+        out_shape=[jax.ShapeDtypeStruct(shape, dtype) for shape, dtype, _ in outputs],
         scratch_shapes=[pltpu.VMEM(shape, F32) for shape in scratch],
         compiler_params=pltpu.CompilerParams(vmem_limit_bytes=limit * 1024 * 1024),
-        cost_estimate=pl.CostEstimate(flops=flops, bytes_accessed=moved, transcendentals=0),
+        cost_estimate=pl.CostEstimate(flops=1000000, bytes_accessed=moved, transcendentals=0),
         name=name,
     )(*arrays)
 
@@ -712,24 +732,24 @@
         medium_kernel, "medium", width,
         [(med, "lane"), (before, "lane"), (mtaps, "lane"), (filt, "lane"), (forward, "whole"), (top, "whole")],
         [(wide, BF16, "lane"), (plane, BF16, "lane"), (plane, BF16, "lane"), (plane, BF16, "lane"), (plane, F32, "lane"), (plane, F32, "lane"), ((8, ROWS), F32, "whole")],
-        [ext, halo],
+        [ext, halo], blocks=True,
     )
     z_other, square = lax.optimization_barrier((z_other, square))
     (z_pairs,) = run(
         join_kernel, "join", width, [(me, "scalar"), (z_all, "lane"), (z_other, "lane"), (rate, "lane")],
-        [((PAIRS,) + modes, BF16, "lane")], [], lanes=width,
+        [((PAIRS,) + modes, BF16, "lane")], [], whole=True,
     )
     zg = in_plane(z_pairs)
     (y_back,) = run(
         back_kernel, "back", width,
         [(gconv, "lane"), (rate, "lane"), (weight, "lane"), (z_ends, "lane")],
-        [(plane, F32, "lane")], [full],
+        [(plane, F32, "lane")], [full, full],
     )
     grad_prod, zin, inner = run(
         inner_kernel, "inner", width,
         [(me, "scalar"), (zg, "lane"), (z_other, "lane"), (rate, "lane"), (weight, "lane"), (y_back, "lane"), (k_two, "lane"), (gated, "lane"), (gain, "lane"), (square, "whole")],
         [(plane, BF16, "lane"), (modes, F32, "lane"), ((8, 1, 2 * ROWS), F32, "whole")],
-        [full, (8, ROWS)],
+        [full, (8, ROWS)], grid=True,
     )
     sums = swap(inner, "tp")
     later, _ = lax.optimization_barrier((gconv, inner))
@@ -743,7 +763,7 @@
         norm_kernel, "norm", width,
         [(me, "scalar"), (sums, "whole"), (gated, "lane"), (conv, "lane"), (q_one, "lane"), (k_one, "lane"), (v_one, "lane"), (k_two, "lane"), (grad_prod, "lane"), (gain, "lane"), (filt, "lane"), (cotangent, "lane"), (prod, "lane"), (med, "lane"), (lng, "lane"), (before, "lane"), (rate, "lane"), (forward, "whole"), (low, "whole")],
         [(plane, BF16, "lane"), (plane, BF16, "lane"), (plane, F32, "lane"), (plane, F32, "lane"), ((HALO, width), BF16, "lane"), ((MODES + HALF, width), BF16, "lane"), ((HALF, width), F32, "lane")],
-        [full, rows, ext, halo, (2 * HALF, LANES)],
+        [full, rows, ext, halo, (2 * HALF, LANES)], grid=True,
     )
     other = exchanged(pair)
     gpo, tap_rows = run(
@@ -757,20 +777,20 @@
     (sent,) = run(
         share_kernel, "share", width,
         [(me, "scalar"), (pair, "lane"), (other, "lane"), (keep, "lane"), (rate, "lane")],
-        [((PAIRS, MODES + 8, width), BF16, "lane")], [(HALF + 8, width), (MODES + 8, width)], lanes=width,
+        [((PAIRS, MODES + 8, width), BF16, "lane")], [(HALF + 8, width), (MODES + 8, width)], whole=True,
     )
     got = in_plane(sent)
 
     y_front, mode_sums, inside = run(
         modes_kernel, "modes", width,
         [(x, "lane"), (gconv, "lane"), (rate, "lane"), (weight, "lane"), (ends_back, "lane")],
-        [(plane, F32, "lane"), ((5 * MODES, width), F32, "lane"), ((MODES, CHUNKS, width), F32, "lane")], [full, full],
+        [(plane, F32, "lane"), ((5 * MODES, width), F32, "lane"), ((MODES, CHUNKS, width), F32, "lane")], [full, full, full], grid=True,
     )
     mixed, gq2, res, every, leave, late = run(
         answer_kernel, "answer", width,
         [(me, "scalar"), (got, "lane"), (pair, "lane"), (other, "lane"), (rate, "lane"), (weight, "lane"), (y_front, "lane"), (inside, "lane"), (q_two, "lane"), (cotangent, "lane"), (mode_sums, "lane"), (zin, "lane"), (lng, "lane"), (before, "lane"), (tap_rows, "lane"), (after, "lane"), (filt, "lane"), (k_one, "lane"), (v_one, "lane"), (med, "lane"), (forward, "whole"), (low, "whole")],
         [(plane, BF16, "lane"), (plane, F32, "lane"), ((2 * MODES, width), BF16, "lane"), ((MODES, width), BF16, "lane"), (modes, F32, "lane"), ((TAPS, width), F32, "lane")],
-        [ext, rows, full, rows],
+        [ext, rows, full, rows], grid=True,
     )
     own = res.reshape(2 * MODES, PAIRS, 2, MODES).transpose(2, 1, 0, 3).reshape(2, PAIRS, width)
     second = me[0] % 2
@@ -780,7 +800,7 @@
     (slots,) = run(
         last_kernel, "last", width,
         [(me, "scalar"), (every, "lane"), (mine, "lane"), (partner, "lane")],
-        [((PAIRS, 24, width), BF16, "lane")], [(24, width)], lanes=width,
+        [((PAIRS, 24, width), BF16, "lane")], [(24, width)], whole=True,
     )
     last = in_plane(slots)
 
@@ -793,7 +813,7 @@
     taps_medium, taps_long, grad_filter, gain_total, grad_residue, grad_log = run(
         finish_kernel, "finish", width, [(last, "lane")],
         [((3, 3, width), F32, "lane"), ((3, 2, width), F32, "lane"), ((TAPS, width), F32, "lane"), ((1, width), F32, "lane"), ((MODES, MODES), F32, "whole"), ((MODES, MODES), F32, "whole")],
-        [(SHARE * count + 8, LANES)], limit=16,
+        [(SHARE * count + 8, LANES)], limit=16, blocks=True,
     )
     return (
         mixed,

time: 155 us -> 153 us (0.987)
  Pallas kernels: 59.7 us -> 55.8 us
    pallas_call x15, Pallas kernels: 59.7 us -> 55.8 us  [run(): pl.pallas_call(body, **places, out_shape=[jax.ShapeDtypeStruct(shape, dty...]
    ppermute x3, starting transfers between devices: 5.93 us -> 7.7 us  [exchanged(): lax.ppermute(array, 'ctx', [(i, i ^ 1) for i in range(lax.axis_size('ctx'...]
  transfers between devices with their start and end apart: 10 -> 10, of which waited for: 8 -> 8; matrix products, arithmetic and copies ran while one was open for 3% -> 3% of each run, Pallas kernels for 20% -> 18%
where the time goes in v4:
time: 153 us; the launch traced here: 151 us
  Pallas kernels  55.8 us (36%)
  starting transfers between devices  49.5 us (32%)
  waiting for transfers between devices  31.8 us (21%)
  local copies, waits for them, and re-layouts  11.3 us (7%)
  other arithmetic  1.61 us (1%)
    pallas_call x15, Pallas kernels, run(): pl.pallas_call(body, **places, out_shape=[jax.ShapeDtypeStruct(shape, dty...  55.8 us
    all_to_all x2, starting transfers between devices, swap(): return lax.all_to_all(array, axis, split_axis=0, concat_axis=0, tiled=True)  17.2 us
    all_to_all x3, starting transfers between devices, in_plane(): lax.all_to_all(array, 'ctx', split_axis=0, concat_axis=0, tiled=True, axi...  15.5 us
    ppermute x3, waiting for transfers between devices, exchanged(): lax.ppermute(array, 'ctx', [(i, i ^ 1) for i in range(lax.axis_size('ctx'...  11.6 us
    ppermute x2, starting transfers between devices, passed_along(): return lax.ppermute(array, axis, pairs)  9.03 us
    unnamed x36, local copies, waits for them, and re-layouts  8.61 us
    ppermute x3, starting transfers between devices, exchanged(): lax.ppermute(array, 'ctx', [(i, i ^ 1) for i in range(lax.axis_size('ctx'...  7.7 us
    ppermute x2, waiting for transfers between devices, passed_along(): return lax.ppermute(array, axis, pairs)  7.26 us
  transfers between devices with their start and end apart: 10, of which 8 were waited for; matrix products, arithmetic and copies ran while one was open for 3% of the time, Pallas kernels for 18%

profile of v4, /device:TPU:64, one launch (start us, length us, event | category | flops | bytes accessed | tf_op | source)
XLA Modules:
  0.0 150.9 jit_solution(1663490576912478648)
XLA Ops:
  0.7 0.9 select_maximum_fusion
  1.5 0.7 broadcast_in_dim.2
  2.2 12.3 %all-to-all-start = ((f32[32,16,128]{2,1,0:T(8,128)}), f32[32,16,128]{2,1,0:T(8,128)S(1)}, u32[]{:S(2)}, u32[]{:S(2)}) async-start(f32[32,16,128]{2,1,0:T(8,128)} %broadcast_in_dim.2), calls=%async_computation | async-start | bytes 524288 | tf_op jit(solution)/shard_map/all_to_all | solution.py:692
  14.6 0.7 convert_bitcast_fusion
  15.6 7.7 %collective-permute-start = (bf16[144,512]{1,0:T(8,128)(2,1)S(1)}, bf16[144,512]{1,0:T(8,128)(2,1)S(1)}, u32[]{:S(2)}, u32[]{:S(2)}) collective-permute-start(bf16[144,512]{1,0:T(8,128)(2,1)S(1)} %tail.1), channel_id=1, source_target_pairs={{0,8},{8,16},{16,24},{24,32},{32,40},{40,48},{48,56},{56,64},{64,7... | collective-permute-start | bytes 442376 | tf_op jit(solution)/shard_map/ppermute | solution.py:679
  23.4 0.8 copy.37
  24.2 0.6 copy.39
  24.8 3.8 %collective-permute-done.refs_1_.refs_15_.refs_5_.refs_13_ = bf16[144,512]{1,0:T(8,128)(2,1)S(1)} collective-permute-done((bf16[144,512]{1,0:T(8,128)(2,1)S(1)}, bf16[144,512]{1,0:T(8,128)(2,1)S(1)}, u32[]{:S(2)}, u32[]{:S(2)}) %collective-permute-start) | collective-permute-done | bytes 147488 | tf_op jit(solution)/shard_map/ppermute | solution.py:679
  28.7 5.8 %all-to-all-done.refs_0_ = f32[32,16,128]{2,1,0:T(8,128)S(1)} async-done(((f32[32,16,128]{2,1,0:T(8,128)}), f32[32,16,128]{2,1,0:T(8,128)S(1)}, u32[]{:S(2)}, u32[]{:S(2)}) %all-to-all-start) | async-done | bytes 262176 | tf_op jit(solution)/shard_map/all_to_all | solution.py:692
  34.5 0.7 copy-done.4
  35.2 3.9 %long.1 = (f32[16,512]{1,0:T(8,128)}, f32[16,512]{1,0:T(8,128)}, bf16[256,512]{1,0:T(8,128)(2,1)}, bf16[256,512]{1,0:T(8,128)(2,1)}, bf16[256,512]{1,0:T(8,128)(...) custom-call(f32[32,16,128]{2,1,0:T(8,128)} %copy-done.4, bf16[144,512]{1,0:T(8,128)(2,1)} %copy-done.2, ...), custom_call_target="tpu_custom_call" | custom-call | flops 1000000 | bytes 1208320 | tf_op jit(solution)/shard_map/long/pallas_call | solution.py:665
  39.1 0.6 collective-permute-start.1
  39.7 4.2 %medium.1 = (bf16[384,512]{1,0:T(8,128)(2,1)}, bf16[256,512]{1,0:T(8,128)(2,1)}, bf16[256,512]{1,0:T(8,128)(2,1)}, bf16[256,512]{1,0:T(8,128)(2,1)}, f32[256,512...) custom-call(bf16[3,256,512]{2,1,0:T(8,128)(2,1)} %bitcast.26, bf16[144,512]{1,0:T(8,128)(2,1)} %copy-done.2, ...), custom_call_target="tpu_custom_call" | custom-call | flops 1000000 | bytes 1280000 | tf_op jit(solution)/shard_map/medium/pallas_call | solution.py:665
  43.9 3.0 %collective-permute-done.1.refs_2_ = bf16[16,512]{1,0:T(8,128)(2,1)S(1)} collective-permute-done((bf16[16,512]{1,0:T(8,128)(2,1)}, bf16[16,512]{1,0:T(8,128)(2,1)S(1)}, u32[]{:S(2)}, u32[]{:S(2)}) %collective-permute-start.1) | collective-permute-done | bytes 16416 | tf_op jit(solution)/shard_map/ppermute | solution.py:683
  47.0 0.6 copy-done.9
  47.5 1.5 %join.1 = bf16[16,16,512]{2,1,0:T(8,128)(2,1)} custom-call(s32[1]{0:T(128)} %bitcast.refs_0_, bf16[16,512]{1,0:T(8,128)(2,1)} %get-tuple-element.61.refs_1_, bf16[16,512]{1,0:T(8,128)(2,1)} %copy-done.9, f32[16,512]{1,0:T(8,128)} %get-tuple-element.64.refs_3_.refs_1_.refs_16_.refs_4_.refs_2_.refs_9_), custom_call_target="tpu_custom_call" | custom-call | flops 1000000 | bytes 65540 | tf_op jit(solution)/shard_map/join/pallas_call | solution.py:665
  49.1 4.8 %all-to-all-start.1 = ((bf16[16,16,512]{2,1,0:T(8,128)(2,1)}), bf16[16,16,512]{2,1,0:T(8,128)(2,1)S(1)}, u32[]{:S(2)}, u32[]{:S(2)}) async-start(bf16[16,16,512]{2,1,0:T(8,128)(2,1)} %join.1), calls=%async_computation.1 | async-start | bytes 524288 | tf_op jit(solution)/shard_map/all_to_all | solution.py:688
  53.9 4.2 %back.1.refs_5_ = f32[256,512]{1,0:T(8,128)} custom-call(bf16[256,512]{1,0:T(8,128)(2,1)} %get-tuple-element.72.refs_0_.refs_1_, f32[16,512]{1,0:T(8,128)} %get-tuple-element.64.refs_3_.refs_1_.refs_16_.refs_4_.refs_2_.refs_9_, f32[16,512]{1,0:T(8,128)} %get-tuple-element.65.refs_2_.refs_4_.refs_3_.refs_5_.refs_10_, f32[16,8,512]{2,1,0:T(8,128)} %get-tuple-element.67.refs_3_), custom_call_target="tpu_custom_call" | custom-call | flops 1000000 | bytes 589824 | tf_op jit(solution)/shard_map/back/pallas_call | solution.py:665
  58.1 4.3 %all-to-all-done.1.refs_1_ = bf16[16,16,512]{2,1,0:T(8,128)(2,1)S(1)} async-done(((bf16[16,16,512]{2,1,0:T(8,128)(2,1)}), bf16[16,16,512]{2,1,0:T(8,128)(2,1)S(1)}, u32[]{:S(2)}, u32[]{:S(2)}) %all-to-all-start.1) | async-done | bytes 262176 | tf_op jit(solution)/shard_map/all_to_all | solution.py:688
  62.4 0.7 copy-done.5
  63.1 5.2 %inner.1 = (bf16[256,512]{1,0:T(8,128)(2,1)}, f32[16,512]{1,0:T(8,128)}, f32[8,1,512]{2,1,0:T(1,128)}) custom-call(s32[1]{0:T(128)} %bitcast.refs_0_, bf16[16,16,512]{2,1,0:T(8,128)(2,1)} %copy-done.5, bf16[16,512]{1,0:T(8,128)(2,1)} %copy-done.9, f32[16,512]{1,0:T(8,128)} %get-tuple-element.64.refs_3_.refs_1_.refs_16_.refs_4_.refs_2_.refs_9_, ...), custom_call_target="tpu_custom_call" | custom-call | flops 1000000 | bytes 1665028 | tf_op jit(solution)/shard_map/inner/pallas_call | solution.py:665
  68.3 4.9 %all-to-all-start.2 = ((f32[8,1,512]{2,1,0:T(1,128)}), f32[8,1,512]{2,1,0:T(1,128)S(1)}, u32[]{:S(2)}, u32[]{:S(2)}) async-start(f32[8,1,512]{2,1,0:T(1,128)} %get-tuple-element.71), calls=%async_computation.2 | async-start | bytes 32768 | tf_op jit(solution)/shard_map/all_to_all | solution.py:692
  73.2 3.7 %behind.1.refs_4_ = f32[32,8,512]{2,1,0:T(8,128)} custom-call(bf16[256,512]{1,0:T(8,128)(2,1)} %get-tuple-element.72.refs_0_.refs_1_, f32[16,512]{1,0:T(8,128)} %get-tuple-element.64.refs_3_.refs_1_.refs_16_.refs_4_.refs_2_.refs_9_), custom_call_target="tpu_custom_call" | custom-call | flops 1000000 | bytes 294912 | tf_op jit(solution)/shard_map/behind/pallas_call | solution.py:665
  76.9 0.6 copy-done.10
  77.5 7.4 %norm.1 = (bf16[256,512]{1,0:T(8,128)(2,1)}, bf16[256,512]{1,0:T(8,128)(2,1)}, f32[256,512]{1,0:T(8,128)}, f32[256,512]{1,0:T(8,128)}, bf16[144,512]{1,0:T(8,128...) custom-call(s32[1]{0:T(128)} %bitcast.refs_0_, f32[8,1,512]{2,1,0:T(1,128)} %copy-done.10, ...), custom_call_target="tpu_custom_call" | custom-call | flops 1000000 | bytes 4851716 | tf_op jit(solution)/shard_map/norm/pallas_call | solution.py:665
  84.9 3.7 %collective-permute-start.2 = (bf16[96,512]{1,0:T(8,128)(2,1)}, bf16[96,512]{1,0:T(8,128)(2,1)S(1)}, u32[]{:S(2)}, u32[]{:S(2)}) collective-permute-start(bf16[96,512]{1,0:T(8,128)(2,1)} %get-tuple-element.80.refs_1_.refs_2_), channel_id=1, source_target_pairs={{0,8},{8,0},{16,24},{24,16},{32,40},{40,32},{48,56},{56,48},{64,72... | collective-permute-start | bytes 294920 | tf_op jit(solution)/shard_map/ppermute | solution.py:683
  88.6 3.5 %taps.1 = (f32[256,512]{1,0:T(8,128)}, f32[8,512]{1,0:T(8,128)}) custom-call(bf16[256,512]{1,0:T(8,128)(2,1)} %get-tuple-element.82.refs_0_, bf16[128,512]{1,0:T(8,128)(2,1)} %refs_16_.1, bf16[256,512]{1,0:T(8,128)(2,1)} %get-tuple-element.76.refs_5_.refs_2_.refs_17_, bf16[256,512]{1,0:T(8,128)(2,1)} %get-tuple-element.77.refs_6_.refs_3_.refs_18_, ...), custom_call_target="tpu_custom_call" | custom-call | flops 1000000 | bytes 2048000 | tf_op jit(solution)/shard_map/taps/pallas_call | solution.py:665
  92.2 3.8 %collective-permute-done.2.refs_2_.refs_3_ = bf16[96,512]{1,0:T(8,128)(2,1)S(1)} collective-permute-done((bf16[96,512]{1,0:T(8,128)(2,1)}, bf16[96,512]{1,0:T(8,128)(2,1)S(1)}, u32[]{:S(2)}, u32[]{:S(2)}) %collective-permute-start.2) | collective-permute-done | bytes 98336 | tf_op jit(solution)/shard_map/ppermute | solution.py:683
  95.9 0.6 copy-done.8
  96.6 1.8 %share.1 = bf16[16,24,512]{2,1,0:T(8,128)(2,1)} custom-call(s32[1]{0:T(128)} %bitcast.refs_0_, bf16[96,512]{1,0:T(8,128)(2,1)} %get-tuple-element.80.refs_1_.refs_2_, bf16[96,512]{1,0:T(8,128)(2,1)} %copy-done.8, f32[80,512]{1,0:T(8,128)} %get-tuple-element.86.refs_3_, f32[16,512]{1,0:T(8,128)} %get-tuple-element.64.refs_3_.refs_1_.refs_16_.refs_4_.refs_2_.refs_9_), custom_call_target="tpu_custom_call" | custom-call | flops 1000000 | bytes 393220 | tf_op jit(solution)/shard_map/share/pallas_call | solution.py:665
  98.4 3.7 %all-to-all-start.3 = ((bf16[16,24,512]{2,1,0:T(8,128)(2,1)}), bf16[16,24,512]{2,1,0:T(8,128)(2,1)S(1)}, u32[]{:S(2)}, u32[]{:S(2)}) async-start(bf16[16,24,512]{2,1,0:T(8,128)(2,1)} %share.1), calls=%async_computation.3 | async-start | bytes 786432 | tf_op jit(solution)/shard_map/all_to_all | solution.py:688
  102.1 1.3 collective-permute-start.3
  103.5 7.9 %modes.1 = (f32[256,512]{1,0:T(8,128)}, f32[80,512]{1,0:T(8,128)}, f32[16,8,512]{2,1,0:T(8,128)}) custom-call(bf16[256,512]{1,0:T(8,128)(2,1)} %get-tuple-element.87.refs_0_, bf16[256,512]{1,0:T(8,128)(2,1)} %get-tuple-element.72.refs_0_.refs_1_, f32[16,512]{1,0:T(8,128)} %get-tuple-element.64.refs_3_.refs_1_.refs_16_.refs_4_.refs_2_.refs_9_, ...), custom_call_target="tpu_custom_call" | custom-call | flops 1000000 | bytes 1114112 | tf_op jit(solution)/shard_map/modes/pallas_call | solution.py:665
  111.4 3.4 %collective-permute-done.3.refs_15_.refs_7_ = bf16[144,512]{1,0:T(8,128)(2,1)S(1)} collective-permute-done((bf16[144,512]{1,0:T(8,128)(2,1)S(1)}, bf16[144,512]{1,0:T(8,128)(2,1)S(1)}, u32[]{:S(2)}, u32[]{:S(2)}) %collective-permute-start.3) | collective-permute-done | bytes 147488 | tf_op jit(solution)/shard_map/ppermute | solution.py:679
  114.8 0.7 copy-done.6
  115.6 5.6 %answer.1 = (bf16[256,512]{1,0:T(8,128)(2,1)}, f32[256,512]{1,0:T(8,128)}, bf16[32,512]{1,0:T(8,128)(2,1)}, bf16[16,512]{1,0:T(8,128)(2,1)}, f32[16,512]{1,0:T(8,128)}, /*index=5*/f32[128,512]{1,0:T(8,128)}) custom-call(s32[1]{0:T(128)} %bitcast.refs_0_, bf16[16,24,512]{2,1,0:T(8,128)(2,1)} %copy-done.3, bf16[96,512]{1,0:T(8,128)(2,1)} %get-tuple-element.80.refs_1_.refs_2_, ...), custom_call_target="tpu_custom_call" | custom-call | flops 1000000 | bytes 4636676 | tf_op jit(solution)/shard_map/answer/pallas_call | solution.py:665
  121.2 0.9 copy.31
  122.3 0.3 reshape.44
  122.6 0.6 dynamic-slice_bitcast_fusion
  123.3 3.4 %collective-permute-start.4 = (bf16[32,512]{1,0:T(8,128)(2,1)S(1)}, bf16[32,512]{1,0:T(8,128)(2,1)S(1)}, u32[]{:S(2)}, u32[]{:S(2)}) collective-permute-start(bf16[32,512]{1,0:T(8,128)(2,1)S(1)} %pad_maximum_fusion), channel_id=1, source_target_pairs={{0,8},{8,0},{16,24},{24,16},{32,40},{40,32},{48,56},{56,48},{64,72... | collective-permute-start | bytes 98312 | tf_op jit(solution)/shard_map/ppermute | solution.py:683
  126.6 4.8 %collective-permute-done.4.refs_3_ = bf16[32,512]{1,0:T(8,128)(2,1)S(1)} collective-permute-done((bf16[32,512]{1,0:T(8,128)(2,1)S(1)}, bf16[32,512]{1,0:T(8,128)(2,1)S(1)}, u32[]{:S(2)}, u32[]{:S(2)}) %collective-permute-start.4) | collective-permute-done | bytes 32800 | tf_op jit(solution)/shard_map/ppermute | solution.py:683
  131.5 0.6 copy-done.12
  132.1 1.7 %last.1 = bf16[16,24,512]{2,1,0:T(8,128)(2,1)} custom-call(s32[1]{0:T(128)} %bitcast.refs_0_, bf16[16,512]{1,0:T(8,128)(2,1)} %get-tuple-element.105.refs_1_, bf16[16,512]{1,0:T(8,128)(2,1)} %get-tuple-element.132.refs_2_, bf16[32,512]{1,0:T(8,128)(2,1)} %copy-done.12), custom_call_target="tpu_custom_call" | custom-call | flops 1000000 | bytes 65540 | tf_op jit(solution)/shard_map/last/pallas_call | solution.py:665
  133.8 7.1 %all-to-all-start.4 = ((bf16[16,24,512]{2,1,0:T(8,128)(2,1)}), bf16[16,24,512]{2,1,0:T(8,128)(2,1)S(1)}, u32[]{:S(2)}, u32[]{:S(2)}) async-start(bf16[16,24,512]{2,1,0:T(8,128)(2,1)} %last.1), calls=%async_computation.4 | async-start | bytes 786432 | tf_op jit(solution)/shard_map/all_to_all | solution.py:688
  140.8 3.9 %inputs.1 = (bf16[3,256,512]{2,1,0:T(8,128)(2,1)}, bf16[2,256,512]{2,1,0:T(8,128)(2,1)}) custom-call(f32[256,512]{1,0:T(8,128)} %get-tuple-element.97.refs_0_, f32[256,512]{1,0:T(8,128)} %get-tuple-element.98.refs_1_, f32[128,512]{1,0:T(8,128)} %get-tuple-element.99.refs_2_, f32[256,512]{1,0:T(8,128)} %get-tuple-element.100.refs_3_, ...), custom_call_target="tpu_custom_call" | custom-call | flops 1000000 | bytes 3160064 | tf_op jit(solution)/shard_map/inputs/pallas_call | solution.py:665
  144.7 2.4 %copy.33 = bf16[256,2,512]{2,1,0:T(2,128)(2,1)} copy(bf16[256,2,512]{2,0,1:T(8,128)(2,1)} %bitcast.38) | data formatting | bytes 1048576
  147.1 2.8 %all-to-all-done.4.refs_0_ = bf16[16,24,512]{2,1,0:T(8,128)(2,1)S(1)} async-done(((bf16[16,24,512]{2,1,0:T(8,128)(2,1)}), bf16[16,24,512]{2,1,0:T(8,128)(2,1)S(1)}, u32[]{:S(2)}, u32[]{:S(2)}) %all-to-all-start.4) | async-done | bytes 393248 | tf_op jit(solution)/shard_map/all_to_all | solution.py:688
  150.0 0.9 finish.1
  (33 shorter events, 0.7 us)
Async XLA Ops:
  0.6 14.7 %copy-start = (bf16[256,3,512]{2,0,1:T(8,128)(2,1)S(1)}, bf16[256,3,512]{2,0,1:T(8,128)(2,1)}, u32[]{:S(2)}) copy-start(bf16[256,3,512]{2,0,1:T(8,128)(2,1)} %param.12) | copy-start | bytes 2359300
  2.2 12.3 %copy-start.13 = (f32[3,3,512]{2,1,0:T(4,128)S(1)}, f32[3,3,512]{2,1,0:T(4,128)}, u32[]{:S(2)}) copy-start(f32[3,3,512]{2,1,0:T(4,128)} %param.14) | copy-start | bytes 55300
  2.2 32.2 %all-to-all-start = ((f32[32,16,128]{2,1,0:T(8,128)}), f32[32,16,128]{2,1,0:T(8,128)S(1)}, u32[]{:S(2)}, u32[]{:S(2)}) async-start(f32[32,16,128]{2,1,0:T(8,128)} %broadcast_in_dim.2), calls=%async_computation | async-start | bytes 524288 | tf_op jit(solution)/shard_map/all_to_all | solution.py:692
  14.5 8.8 %copy-start.7 = (bf16[256,2,512]{2,1,0:T(2,128)(2,1)S(1)}, bf16[256,2,512]{2,1,0:T(2,128)(2,1)}, u32[]{:S(2)}) copy-start(bf16[256,2,512]{2,1,0:T(2,128)(2,1)} %param.13) | copy-start | bytes 1572868
  14.6 1.0 copy-start.1
  15.6 8.6 %copy-start.14 = (f32[3,2,512]{2,1,0:T(2,128)S(1)}, f32[3,2,512]{2,1,0:T(2,128)}, u32[]{:S(2)}) copy-start(f32[3,2,512]{2,1,0:T(2,128)} %param.15) | copy-start | bytes 36868
  15.6 13.1 %collective-permute-start = (bf16[144,512]{1,0:T(8,128)(2,1)S(1)}, bf16[144,512]{1,0:T(8,128)(2,1)S(1)}, u32[]{:S(2)}, u32[]{:S(2)}) collective-permute-start(bf16[144,512]{1,0:T(8,128)(2,1)S(1)} %tail.1), channel_id=1, source_target_pairs={{0,8},{8,16},{16,24},{24,32},{32,40},{40,48},{48,56},{56,64},{64,7... | collective-permute-start | bytes 442376 | tf_op jit(solution)/shard_map/ppermute | solution.py:679
  28.6 5.8 %copy-start.2 = (bf16[144,512]{1,0:T(8,128)(2,1)}, bf16[144,512]{1,0:T(8,128)(2,1)S(1)}, u32[]{:S(2)}) copy-start(bf16[144,512]{1,0:T(8,128)(2,1)S(1)} %collective-permute-done.refs_1_.refs_15_.refs_5_.refs_13_) | copy-start | bytes 442372
  34.5 0.7 copy-start.4
  39.1 7.9 %collective-permute-start.1 = (bf16[16,512]{1,0:T(8,128)(2,1)}, bf16[16,512]{1,0:T(8,128)(2,1)S(1)}, u32[]{:S(2)}, u32[]{:S(2)}) collective-permute-start(bf16[16,512]{1,0:T(8,128)(2,1)} %get-tuple-element.61.refs_1_), channel_id=1, source_target_pairs={{0,8},{8,0},{16,24},{24,16},{32,40},{40,32},{48,56},{56,48},{64,72... | collective-permute-start | bytes 49160 | tf_op jit(solution)/shard_map/ppermute | solution.py:683
  47.0 0.6 copy-start.9
  49.1 13.3 %all-to-all-start.1 = ((bf16[16,16,512]{2,1,0:T(8,128)(2,1)}), bf16[16,16,512]{2,1,0:T(8,128)(2,1)S(1)}, u32[]{:S(2)}, u32[]{:S(2)}) async-start(bf16[16,16,512]{2,1,0:T(8,128)(2,1)} %join.1), calls=%async_computation.1 | async-start | bytes 524288 | tf_op jit(solution)/shard_map/all_to_all | solution.py:688
  62.4 0.7 copy-start.5
  68.3 8.6 %all-to-all-start.2 = ((f32[8,1,512]{2,1,0:T(1,128)}), f32[8,1,512]{2,1,0:T(1,128)S(1)}, u32[]{:S(2)}, u32[]{:S(2)}) async-start(f32[8,1,512]{2,1,0:T(1,128)} %get-tuple-element.71), calls=%async_computation.2 | async-start | bytes 32768 | tf_op jit(solution)/shard_map/all_to_all | solution.py:692
  76.9 0.6 copy-start.10
  84.9 11.0 %collective-permute-start.2 = (bf16[96,512]{1,0:T(8,128)(2,1)}, bf16[96,512]{1,0:T(8,128)(2,1)S(1)}, u32[]{:S(2)}, u32[]{:S(2)}) collective-permute-start(bf16[96,512]{1,0:T(8,128)(2,1)} %get-tuple-element.80.refs_1_.refs_2_), channel_id=1, source_target_pairs={{0,8},{8,0},{16,24},{24,16},{32,40},{40,32},{48,56},{56,48},{64,72... | collective-permute-start | bytes 294920 | tf_op jit(solution)/shard_map/ppermute | solution.py:683
  95.9 0.6 copy-start.8
  98.4 3.7 %copy-start.15 = (bf16[144,512]{1,0:T(8,128)(2,1)S(1)}, bf16[144,512]{1,0:T(8,128)(2,1)}, u32[]{:S(2)}) copy-start(bf16[144,512]{1,0:T(8,128)(2,1)} %get-tuple-element.95) | copy-start | bytes 442372
  98.4 16.4 %all-to-all-start.3 = ((bf16[16,24,512]{2,1,0:T(8,128)(2,1)}), bf16[16,24,512]{2,1,0:T(8,128)(2,1)S(1)}, u32[]{:S(2)}, u32[]{:S(2)}) async-start(bf16[16,24,512]{2,1,0:T(8,128)(2,1)} %share.1), calls=%async_computation.3 | async-start | bytes 786432 | tf_op jit(solution)/shard_map/all_to_all | solution.py:688
  102.1 12.7 %collective-permute-start.3 = (bf16[144,512]{1,0:T(8,128)(2,1)S(1)}, bf16[144,512]{1,0:T(8,128)(2,1)S(1)}, u32[]{:S(2)}, u32[]{:S(2)}) collective-permute-start(bf16[144,512]{1,0:T(8,128)(2,1)S(1)} %copy-done.15), channel_id=1, source_target_pairs={{8,0},{16,8},{24,16},{32,24},{40,32},{48,40},{56,48},{64,56},{72,6... | collective-permute-start | bytes 442376 | tf_op jit(solution)/shard_map/ppermute | solution.py:679
  114.8 0.7 copy-start.6
  114.8 0.8 copy-start.3
  122.6 0.7 copy-start.11
  123.3 8.2 %collective-permute-start.4 = (bf16[32,512]{1,0:T(8,128)(2,1)S(1)}, bf16[32,512]{1,0:T(8,128)(2,1)S(1)}, u32[]{:S(2)}, u32[]{:S(2)}) collective-permute-start(bf16[32,512]{1,0:T(8,128)(2,1)S(1)} %pad_maximum_fusion), channel_id=1, source_target_pairs={{0,8},{8,0},{16,24},{24,16},{32,40},{40,32},{48,56},{56,48},{64,72... | collective-permute-start | bytes 98312 | tf_op jit(solution)/shard_map/ppermute | solution.py:683
  131.5 0.6 copy-start.12
  133.8 16.2 %all-to-all-start.4 = ((bf16[16,24,512]{2,1,0:T(8,128)(2,1)}), bf16[16,24,512]{2,1,0:T(8,128)(2,1)S(1)}, u32[]{:S(2)}, u32[]{:S(2)}) async-start(bf16[16,24,512]{2,1,0:T(8,128)(2,1)} %last.1), calls=%async_computation.4 | async-start | bytes 786432 | tf_op jit(solution)/shard_map/all_to_all | solution.py:688
